TPU v7x, 256 devices: a whole 4x4x8 slice. The times are simulated.
256 devices in a mesh: dp: 16 (over y_lo, z), tensor: 16 (over y_hi, x, core).
Axes of the slice: x: 4, y: 4 (y_hi: 2, y_lo: 2; y = y_hi * 2 + y_lo), z: 8, core: 2. Of those that a mesh axis runs over, the one named last changes fastest.
Arguments:
- out_grad: bfloat16 [32768, 4096], P(('dp', 'tensor')), may hold values from -24 to 24
- attn_out: bfloat16 [32768, 4096], P('dp', 'tensor'), may hold values from -0.078125 to 0.078125
- o_weight: bfloat16 [4096, 4096], P('dp', 'tensor'), may hold values from -0.09375 to 0.09375
Outputs:
- attn_grad: bfloat16 [32768, 4096], P('dp', 'tensor')
- weight_grad: float32 [4096, 4096], P('dp', 'tensor')
All inputs are finite; a program needn't handle non-finite values.
Results may differ from a plain program's by a relative error of at most 0.001.
Values may be sent and summed in bfloat16 or wider, within the bound.
No kernel may reach another device: no remote copies, remote signals or barrier semaphores. Data moves between devices by JAX's collectives and lax.ppermute only.
A program may use at most 64 MiB of HBM per device.

v0:
```python
import jax
import jax.numpy as jnp
from jax import lax
from jax.sharding import PartitionSpec as P


def body(out_grad, attn_out, o_weight):
    full_weight = lax.all_gather(o_weight, "dp", axis=0, tiled=True)
    gathered = lax.all_gather(out_grad, "tensor", axis=0, tiled=True)
    attn_grad = jnp.dot(gathered, full_weight, preferred_element_type=jnp.float32).astype(
        jnp.bfloat16
    )
    weight_grad = lax.psum_scatter(
        lax.dot_general(
            gathered, attn_out, (((0,), (0,)), ((), ())), preferred_element_type=jnp.float32
        ),
        "dp",
        scatter_dimension=0,
        tiled=True,
    )
    return (attn_grad, weight_grad)


def solution(mesh):
    return jax.shard_map(
        body,
        mesh=mesh,
        in_specs=(P(("dp", "tensor"), None), P("dp", "tensor"), P("dp", "tensor")),
        out_specs=(P("dp", "tensor"), P("dp", "tensor")),
        check_vma=False,
    )
```

profile of v0, /device:TPU:2, one launch (start us, length us, event | category | flops | bytes accessed | tf_op | source)
XLA Modules:
  0.0 287.6 jit_solution(3332159857697970733)
XLA Ops:
  7.2 0.0 copy-start
  7.2 0.0 all-gather.3.cloned.1.call-start
  7.2 0.7 all-gather.3.cloned.1.call-update
  7.9 0.0 all-gather.5.cloned.1.call-start
  8.0 0.7 all-gather.5.cloned.1.call-update
  8.7 0.0 reduce-scatter.2.cloned.1.call-start
  8.7 119.1 %all-gather.3.cloned.1.call-done = bf16[2048,4096]{1,0:T(8,128)(2,1)} async-done(((bf16[128,4096]{1,0:T(8,128)(2,1)}), bf16[2048,4096]{1,0:T(8,128)(2,1)}) %all-gather.3.cloned.1.call-update) | async-done | bytes 16777232 | tf_op jit(solution)/shard_map/all_gather | solution.py:9
  127.8 0.0 copy-done
  127.8 10.2 %fusion = f32[4096,256]{1,0:T(8,128)} fusion(bf16[2048,4096]{1,0:T(8,128)(2,1)} %all-gather.3.cloned.1.call-done, bf16[2048,256]{1,0:T(8,128)(2,1)S(1)} %copy-done), kind=kOutput, calls=%fused_computation.1 | convolution fusion | flops 4294967296 | bytes 22020096 | tf_op jit(solution)/shard_map/dot_general | solution.py:14
  138.0 0.0 reduce-scatter.2.cloned.1.call-update
  138.0 62.3 %all-gather.5.cloned.1.call-done = bf16[4096,256]{1,0:T(8,128)(2,1)} async-done(((bf16[256,256]{1,0:T(8,128)(2,1)}), bf16[4096,256]{1,0:T(8,128)(2,1)}) %all-gather.5.cloned.1.call-update) | async-done | bytes 2097168 | tf_op jit(solution)/shard_map/all_gather | solution.py:8
  200.3 12.0 %convolution_convert_fusion = bf16[2048,256]{1,0:T(8,128)(2,1)} fusion(bf16[2048,4096]{1,0:T(8,128)(2,1)} %all-gather.3.cloned.1.call-done, bf16[4096,256]{1,0:T(8,128)(2,1)} %all-gather.5.cloned.1.call-done), kind=kOutput, calls=%fused_computation | convolution fusion | flops 4295491584 | bytes 19922944 | tf_op jit(solution)/shard_map/dot_general | solution.py:10
  212.3 68.8 %reduce-scatter.2.cloned.1.call-done = f32[256,256]{1,0:T(8,128)} async-done(((f32[4096,256]{1,0:T(8,128)}), f32[256,256]{1,0:T(8,128)}) %reduce-scatter.2.cloned.1.call-update) | async-done | bytes 262160 | tf_op jit(solution)/shard_map/reduce_scatter | solution.py:13
Async XLA Ops:
  7.2 120.6 %copy-start = (bf16[2048,256]{1,0:T(8,128)(2,1)S(1)}, bf16[2048,256]{1,0:T(8,128)(2,1)}, u32[]{:S(2)}) copy-start(bf16[2048,256]{1,0:T(8,128)(2,1)} %param.4) | copy-start | bytes 3145732
  7.2 120.6 %all-gather.3.cloned.1.call-start = ((), (), s32[]{:S(2)}) async-start(), calls=%async_computation.1 | async-start | bytes 17825792 | tf_op jit(solution)/shard_map/all_gather | solution.py:9
  7.9 192.4 %all-gather.5.cloned.1.call-start = ((), (), s32[]{:S(2)}) async-start(), calls=%async_computation.2 | async-start | bytes 2228224 | tf_op jit(solution)/shard_map/all_gather | solution.py:8
  8.7 272.4 %reduce-scatter.2.cloned.1.call-start = ((), (), s32[]{:S(2)}) async-start(), calls=%async_computation.3 | async-start | bytes 4456448 | tf_op jit(solution)/shard_map/reduce_scatter | solution.py:13
Sparse Core Ops, SparseCore 0:
  10.7 116.9 all-gather.2
  129.5 70.6 all-gather.4
  203.4 77.6 reduce-scatter.1
where the time goes:
time: 288 us
  waiting for transfers between devices  251 us (87%)
  matrix products  22.3 us (8%)
  between operations  13.8 us (5%)
    all_gather x1, waiting for transfers between devices, body(): gathered = lax.all_gather(out_grad, 'tensor', axis=0, tiled=True)  119 us
    reduce_scatter x1, waiting for transfers between devices, body(): lax.psum_scatter(lax.dot_general(gathered, attn_out, (((0,), (0,)), ((),...  68.8 us
    all_gather x1, waiting for transfers between devices, body(): full_weight = lax.all_gather(o_weight, 'dp', axis=0, tiled=True)  62.3 us
    dot_general x1, matrix products, body(): jnp.dot(gathered, full_weight, preferred_element_type=jnp.float32)  12 us
    dot_general x1, matrix products, body(): lax.dot_general(gathered, attn_out, (((0,), (0,)), ((), ())), preferred_e...  10.2 us
  transfers between devices with their start and end apart: 3, of which 3 were waited for; matrix products, arithmetic and copies ran while one was open for 8% of the time, Pallas kernels for 0%

commit v1 on v0

v1 whole, which is shorter than its diff:
```python
import jax
import jax.numpy as jnp
import numpy as np
from jax import lax
from jax.experimental import pallas as pl
from jax.experimental.pallas import tpu as pltpu
from jax.sharding import Mesh
from jax.sharding import PartitionSpec as P

AXES = ("yl", "z", "yh", "x", "c")
SIZES = dict(yl=2, z=8, yh=2, x=4, c=2)
BF16, F32 = jnp.bfloat16, jnp.float32
HALF = 128
BLK = 256
N_Z = 8
CHUNKS = ((4, 3, 5, 2), (6, 1, 7, 0))
VMEM_LIMIT = 48 * 1024 * 1024


def permute(value, axes, target):
    shape = [SIZES[a] for a in axes]
    pairs = []
    for at in np.ndindex(*shape):
        to = target(*at)
        if to is None:
            continue
        to = tuple(v % s for v, s in zip(to, shape))
        pairs.append((int(np.ravel_multi_index(at, shape)), int(np.ravel_multi_index(to, shape))))
    return lax.ppermute(value, axes if len(axes) > 1 else axes[0], pairs)


def right(v):
    return permute(v, ("x",), lambda i: (i + 1,))


def left(v):
    return permute(v, ("x",), lambda i: (i - 1,))


def across(v):
    return permute(v, ("yh",), lambda i: (i + 1,))


def core(v):
    return permute(v, ("c",), lambda i: (i + 1,))


def z_up(v):
    return permute(v, ("z",), lambda i: (i + 1,))


def z_down(v):
    return permute(v, ("z",), lambda i: (i - 1,))


def kernel_call(kernel, out_shape, flops, nbytes, n_in, scratch=()):
    return pl.pallas_call(
        kernel,
        out_shape=out_shape,
        in_specs=[pl.BlockSpec(memory_space=pltpu.SMEM)]
        + [pl.BlockSpec(memory_space=pltpu.VMEM)] * n_in,
        out_specs=jax.tree.map(lambda _: pl.BlockSpec(memory_space=pltpu.VMEM), out_shape),
        scratch_shapes=list(scratch),
        compiler_params=pltpu.CompilerParams(vmem_limit_bytes=VMEM_LIMIT),
        cost_estimate=pl.CostEstimate(flops=flops, bytes_accessed=nbytes, transcendentals=0),
    )


def split_kernel(pos, og, *outs):
    z, c = pos[0], pos[1]
    for k, chunk in enumerate(CHUNKS):
        for who, half in ((0, 1 - c), (1, c)):
            out = outs[2 * k + who]
            for j, r in enumerate(chunk):
                col = pl.multiple_of(half * (N_Z * BLK) + lax.rem(z + r, N_Z) * BLK, BLK)
                out[:, j * BLK : (j + 1) * BLK] = og[:, pl.ds(col, BLK)]


def turn_kernel(rows, own, other, out):
    for i in range(16):
        row = pl.multiple_of(rows[i] * HALF, HALF)
        for h, src in enumerate((own, other)):
            block = src[pl.ds(row, HALF), :].astype(F32)
            out[h * BLK : (h + 1) * BLK, i * HALF : (i + 1) * HALF] = block.T.astype(BF16)


def weight_kernel(_, turned, *refs):
    pieces, outs = refs[:9], refs[9:]
    for j, out in enumerate(outs):
        rhs = jnp.concatenate([p[:, j * BLK : (j + 1) * BLK] for p in pieces], axis=0)
        out[...] = jnp.dot(turned[...], rhs, preferred_element_type=F32)


def attn_kernel(info, own_w, other_w, *refs):
    pieces = (refs[:9], refs[9:18])
    keep, send, w = refs[18:]
    z = info[16]
    for k, chunk in enumerate(CHUNKS):
        for j, r in enumerate(chunk):
            row = pl.multiple_of(lax.rem(z + r, N_Z) * BLK, BLK)
            at = (k * len(chunk) + j) * BLK
            w[at : at + BLK, :BLK] = own_w[pl.ds(row, BLK), :]
            w[at : at + BLK, BLK:] = other_w[pl.ds(row, BLK), :]
    i = 0
    for a, b in zip(*pieces):
        res = jnp.dot(
            jnp.concatenate([a[...], b[...]], axis=1), w[...], preferred_element_type=F32
        )
        for h in range(a.shape[0] // HALF):
            row = pl.multiple_of(info[i] * HALF, HALF)
            part = res[h * HALF : (h + 1) * HALF]
            keep[pl.ds(row, HALF), :] = part[:, :BLK]
            send[pl.ds(row, HALF), :] = part[:, BLK:]
            i += 1


def gather(own):
    p, l, r = across(own), right(own), left(own)
    xa = right(jnp.concatenate([l[:HALF], p[:HALF]], axis=0))
    xb = left(jnp.concatenate([r[HALF:], p[HALF:]], axis=0))
    yb = across(jnp.concatenate([l[HALF:], r[:HALF]], axis=0))
    za = right(xa[HALF:])
    zb = left(xb[HALF:])
    return [own, p, l, r, xa, xb, yb, za, zb]


def piece_rows(yh, x, c):
    def at(dy, dx, half):
        return ((yh + dy) % 2) * 8 + ((x + dx) % 4) * 2 + (c + half) % 2

    halves = [(0, 0, 0), (0, 0, 1), (1, 0, 0), (1, 0, 1), (0, -1, 0), (0, -1, 1), (0, 1, 0), (0, 1, 1)]
    halves += [(0, 2, 0), (1, -1, 0), (0, 2, 1), (1, 1, 1), (1, -1, 1), (1, 1, 0), (1, 2, 0), (1, 2, 1)]
    return [at(*h) for h in halves]


def body(out_grad, attn_out, o_weight):
    yl, z, yh, x, c = (lax.axis_index(a) for a in AXES)
    rows = piece_rows(yh, x, c)
    info = jnp.stack(rows + [z]).astype(jnp.int32)

    part = jax.ShapeDtypeStruct((HALF, 4 * BLK), BF16)
    send_a, keep_a, send_b, keep_b = kernel_call(split_kernel, (part,) * 4, 0, 2 << 20, 1)(
        jnp.stack([z, c]).astype(jnp.int32), out_grad
    )
    own_a = jnp.concatenate([keep_a, core(send_a)], axis=0)
    own_b = jnp.concatenate([keep_b, core(send_b)], axis=0)

    full_weight = lax.all_gather(o_weight, ("yl", "z"), axis=0, tiled=True)

    pieces_a = gather(own_a)
    pieces_b = gather(own_b)

    turned = kernel_call(
        turn_kernel, jax.ShapeDtypeStruct((2 * BLK, 16 * HALF), BF16), 0, 4 << 20, 2
    )(info, attn_out, core(attn_out))

    block = jax.ShapeDtypeStruct((2 * BLK, BLK), F32)
    grads = {}
    for chunk, pieces in zip(CHUNKS, (pieces_a, pieces_b)):
        made = kernel_call(
            weight_kernel, (block,) * 4, 2 * 512 * 2048 * 1024, 8 << 20, 10
        )(info, turned, *pieces)
        grads.update(zip(chunk, made))

    down = z_down(grads[4])
    up = z_up(grads[3])
    down = z_down(down + grads[5])
    up = z_up(up + grads[2])
    down = z_down(down + grads[6])
    up = z_up(up + grads[1])
    down = z_down(down + grads[7])
    total = up + grads[0] + down

    same = yl == c
    first, second = total[:BLK], total[BLK:]
    alpha = permute(
        jnp.where(same, second, first),
        ("yl", "c"),
        lambda i, j: (i, 1 - j) if i == j else (1 - i, j),
    )
    beta = permute(second, ("yl", "c"), lambda i, j: None if i == j else (1 - i, 1 - j))
    weight_grad = (alpha + jnp.where(same, first, beta)).T

    half = N_Z * BLK
    own_w = lax.dynamic_slice(full_weight, (c * half, 0), (half, BLK))
    other_w = core(lax.dynamic_slice(full_weight, ((1 - c) * half, 0), (half, BLK)))
    acc = jax.ShapeDtypeStruct((16 * HALF, BLK), F32)
    keep, send = kernel_call(
        attn_kernel,
        (acc, acc),
        2 * 2048 * 2048 * 512,
        14 << 20,
        20,
        [pltpu.VMEM((half, 2 * BLK), BF16)],
    )(info, own_w, other_w, *pieces_a, *pieces_b)
    attn_grad = (keep + core(send)).astype(BF16)
    return attn_grad, weight_grad


def solution(mesh):
    fine = Mesh(mesh.devices.reshape([SIZES[a] for a in AXES]), AXES)
    dp, tensor = ("yl", "z"), ("yh", "x", "c")
    return jax.shard_map(
        body,
        mesh=fine,
        in_specs=(P(dp + tensor, None), P(dp, tensor), P(dp, tensor)),
        out_specs=(P(dp, tensor), P(dp, tensor)),
        check_vma=False,
    )
```

time: 288 us -> 187 us (0.65)
  the two profiles are of different devices: /device:TPU:2 before, /device:TPU:1 now
where the time goes in v1:
time: 187 us; the launch traced here: 186 us
  waiting for transfers between devices  78.5 us (42%)
  starting transfers between devices  49 us (26%)
  Pallas kernels  20.2 us (11%)
  local copies, waits for them, and re-layouts  18.5 us (10%)
  between operations  14.4 us (8%)
  other arithmetic  5.74 us (3%)
    ppermute x30, waiting for transfers between devices, permute(): return lax.ppermute(value, axes if len(axes) > 1 else axes[0], pairs)  64.8 us
    ppermute x30, starting transfers between devices, permute(): return lax.ppermute(value, axes if len(axes) > 1 else axes[0], pairs)  49 us
    all_gather x1, waiting for transfers between devices, body(): full_weight = lax.all_gather(o_weight, ('yl', 'z'), axis=0, tiled=True)  13 us
    unnamed x67, local copies, waits for them, and re-layouts  9.79 us
    pallas_call x1, Pallas kernels, body(): kernel_call(attn_kernel, (acc, acc), 2 * 2048 * 2048 * 512, 14 << 20, 20,...  9.3 us
    pallas_call x2, Pallas kernels, body(): kernel_call(weight_kernel, (block,) * 4, 2 * 512 * 2048 * 1024, 8 << 20, 10)  8.24 us
  transfers between devices with their start and end apart: 31, of which 13 were waited for; matrix products, arithmetic and copies ran while one was open for 7% of the time, Pallas kernels for 11%

profile of v1, /device:TPU:1, one launch (start us, length us, event | category | flops | bytes accessed | tf_op | source)
XLA Modules:
  0.0 186.4 jit_solution(16679383352848964607)
XLA Ops:
  7.2 0.7 all-gather.2.cloned.1.call-update
  8.0 1.2 copy-done.2
  9.2 1.4 shard_map.50
  10.6 3.2 %collective-permute-start.1 = (bf16[128,1024]{1,0:T(8,128)(2,1)S(1)}, bf16[128,1024]{1,0:T(8,128)(2,1)S(1)}, u32[]{:S(2)}, u32[]{:S(2)}) collective-permute-start(bf16[128,1024]{1,0:T(8,128)(2,1)S(1)} %get-tuple-element.17), channel_id=1, source_target_pairs={{0,1},{1,0},{2,3},{3,2},{4,5},{5,4},{6,7},{7,6},{8,9},{9,8},{10,11... | collective-permute-start | bytes 786440 | tf_op jit(solution)/shard_map/ppermute | solution.py:29
  13.8 0.7 constant_dynamic-update-slice_fusion.1
  14.6 0.4 collective-permute-done.1
  15.0 0.7 constant_dynamic-update-slice_fusion.refs_0_
  15.7 1.2 collective-permute-start.2
  16.9 0.7 collective-permute-start.10
  17.6 1.2 collective-permute-start.3
  19.2 1.5 collective-permute-start.4
  20.7 1.0 constant_dynamic-update-slice_fusion.2.refs_9_.refs_0_
  21.7 1.9 %collective-permute-start.11 = (bf16[256,1024]{1,0:T(8,128)(2,1)S(1)}, bf16[256,1024]{1,0:T(8,128)(2,1)S(1)}, u32[]{:S(2)}, u32[]{:S(2)}) collective-permute-start(bf16[256,1024]{1,0:T(8,128)(2,1)S(1)} %constant_dynamic-update-slice_fusion.2.refs_9_.refs_0_), channel_id=1, source_target_pairs={{0,8},{8,0},{1,9},{9,1},{2,10},{10,2},{3,11},{11,3},{4,12},{12,4},... | collective-permute-start | bytes 1572872 | tf_op jit(solution)/shard_map/ppermute | solution.py:29
  23.6 7.1 %collective-permute-done.2.refs_1_ = bf16[256,1024]{1,0:T(8,128)(2,1)S(1)} collective-permute-done((bf16[256,1024]{1,0:T(8,128)(2,1)}, bf16[256,1024]{1,0:T(8,128)(2,1)S(1)}, u32[]{:S(2)}, u32[]{:S(2)}) %collective-permute-start.2) | collective-permute-done | bytes 524320 | tf_op jit(solution)/shard_map/ppermute | solution.py:29
  30.7 1.8 collective-permute-done.3.refs_2_
  32.5 1.4 collective-permute-start.13
  34.3 15.8 %collective-permute-done.11.refs_10_.refs_1_ = bf16[256,1024]{1,0:T(8,128)(2,1)S(1)} collective-permute-done((bf16[256,1024]{1,0:T(8,128)(2,1)S(1)}, bf16[256,1024]{1,0:T(8,128)(2,1)S(1)}, u32[]{:S(2)}, u32[]{:S(2)}) %collective-permute-start.11) | collective-permute-done | bytes 524320 | tf_op jit(solution)/shard_map/ppermute | solution.py:29
  50.1 0.9 fusion.3
  51.0 0.8 pad_maximum_fusion.2
  51.8 4.0 %collective-permute-start.7 = (bf16[256,1024]{1,0:T(8,128)(2,1)}, bf16[256,1024]{1,0:T(8,128)(2,1)}, u32[]{:S(2)}, u32[]{:S(2)}) collective-permute-start(bf16[256,1024]{1,0:T(8,128)(2,1)} %pad_maximum_fusion.2), channel_id=1, source_target_pairs={{0,8},{8,0},{1,9},{9,1},{2,10},{10,2},{3,11},{11,3},{4,12},{12,4},... | collective-permute-start | bytes 1572872 | tf_op jit(solution)/shard_map/ppermute | solution.py:29
  55.8 0.8 fusion.1
  56.7 0.9 fusion.2
  57.6 0.8 slice.78
  58.4 3.6 %collective-permute-done.6.refs_5_ = bf16[256,1024]{1,0:T(8,128)(2,1)S(1)} collective-permute-done((bf16[256,1024]{1,0:T(8,128)(2,1)S(1)}, bf16[256,1024]{1,0:T(8,128)(2,1)S(1)}, u32[]{:S(2)}, u32[]{:S(2)}) %collective-permute-start.6) | collective-permute-done | bytes 524320 | tf_op jit(solution)/shard_map/ppermute | solution.py:29
  62.0 0.7 slice.79
  62.8 0.8 copy-done.13
  63.8 13.0 %all-gather.2.cloned.1.call-done = bf16[4096,256]{1,0:T(8,128)(2,1)} async-done(((bf16[256,256]{1,0:T(8,128)(2,1)}), bf16[4096,256]{1,0:T(8,128)(2,1)}) %all-gather.2.cloned.1.call-update) | async-done | bytes 2097168 | tf_op jit(solution)/shard_map/all_gather | solution.py:148
  76.8 2.7 %constant_dynamic-slice_fusion = (bf16[2048,256]{1,0:T(8,128)(2,1)S(1)}, bf16[2048,256]{1,0:T(8,128)(2,1)}) fusion(bf16[4096,256]{1,0:T(8,128)(2,1)} %all-gather.2.cloned.1.call-done, s32[]{:T(128)S(6)} %select_n.142, s32[]{:T(128)S(6)} %select_n.141), kind=kLoop, calls=%fused_computation.15 | loop fusion | bytes 4194312 | tf_op jit(solution)/shard_map/dynamic_slice | solution.py:186
  79.6 9.1 %collective-permute-start = (bf16[2048,256]{1,0:T(8,128)(2,1)S(1)}, bf16[2048,256]{1,0:T(8,128)(2,1)S(1)}, u32[]{:S(2)}, u32[]{:S(2)}) collective-permute-start(bf16[2048,256]{1,0:T(8,128)(2,1)S(1)} %get-tuple-element.32), channel_id=1, source_target_pairs={{0,1},{1,0},{2,3},{3,2},{4,5},{5,4},{6,7},{7,6},{8,9},{9,8},{10,11... | collective-permute-start | bytes 3145736 | tf_op jit(solution)/shard_map/ppermute | solution.py:29
  88.9 1.8 collective-permute-start.14
  90.6 1.2 shard_map.52.turned
  91.9 1.3 copy-done
  93.2 1.2 collective-permute-start.15
  94.4 4.2 %shard_map.53 = (f32[512,256]{1,0:T(8,128)S(1)}, f32[512,256]{1,0:T(8,128)S(1)}, f32[512,256]{1,0:T(8,128)S(1)}, f32[512,256]{1,0:T(8,128)S(1)}) custom-call(s32[17]{0:T(128)S(1)} %stack.78.info.rows._, bf16[512,2048]{1,0:T(8,128)(2,1)} %copy-done, bf16[256,1024]{1,0:T(8,128)(2,1)} %constant_dynamic-update-slice_fusion.refs_0_, ...), custom_call_target="tpu_custom_call" | custom-call | flops 2147483648 | bytes 8388608 | tf_op jit(solution)/shard_map/pallas_call | solution.py:160
  98.7 2.1 %collective-permute-start.24 = (f32[512,256]{1,0:T(8,128)S(1)}, f32[512,256]{1,0:T(8,128)S(1)}, u32[]{:S(2)}, u32[]{:S(2)}) collective-permute-start(f32[512,256]{1,0:T(8,128)S(1)} %get-tuple-element.26), channel_id=1, source_target_pairs={{0,112},{16,0},{32,16},{48,32},{64,48},{80,64},{96,80},{112,96},{1... | collective-permute-start | bytes 1572872 | tf_op jit(solution)/shard_map/ppermute | solution.py:29
  100.8 2.6 %collective-permute-start.16 = (bf16[256,1024]{1,0:T(8,128)(2,1)S(1)}, bf16[256,1024]{1,0:T(8,128)(2,1)S(1)}, u32[]{:S(2)}, u32[]{:S(2)}) collective-permute-start(bf16[256,1024]{1,0:T(8,128)(2,1)S(1)} %pad_maximum_fusion.5), channel_id=1, source_target_pairs={{0,8},{8,0},{1,9},{9,1},{2,10},{10,2},{3,11},{11,3},{4,12},{12,4},... | collective-permute-start | bytes 1572872 | tf_op jit(solution)/shard_map/ppermute | solution.py:29
  103.4 0.5 collective-permute-done.14.refs_13_.refs_4_
  103.9 0.4 collective-permute-start.17
  104.3 2.1 %collective-permute-done.15.refs_14_.refs_5_ = bf16[256,1024]{1,0:T(8,128)(2,1)S(1)} collective-permute-done((bf16[256,1024]{1,0:T(8,128)(2,1)S(1)}, bf16[256,1024]{1,0:T(8,128)(2,1)S(1)}, u32[]{:S(2)}, u32[]{:S(2)}) %collective-permute-start.15) | collective-permute-done | bytes 524320 | tf_op jit(solution)/shard_map/ppermute | solution.py:29
  106.4 2.5 %collective-permute-start.18 = (bf16[128,1024]{1,0:T(8,128)(2,1)S(1)}, bf16[128,1024]{1,0:T(8,128)(2,1)S(1)}, u32[]{:S(2)}, u32[]{:S(2)}) collective-permute-start(bf16[128,1024]{1,0:T(8,128)(2,1)S(1)} %slice.87), channel_id=1, source_target_pairs={{0,6},{2,0},{4,2},{6,4},{1,7},{3,1},{5,3},{7,5},{8,14},{10,8},{12,... | collective-permute-start | bytes 786440 | tf_op jit(solution)/shard_map/ppermute | solution.py:29
  108.9 2.7 %collective-permute-done.24 = f32[512,256]{1,0:T(8,128)S(1)} collective-permute-done((f32[512,256]{1,0:T(8,128)S(1)}, f32[512,256]{1,0:T(8,128)S(1)}, u32[]{:S(2)}, u32[]{:S(2)}) %collective-permute-start.24) | collective-permute-done | bytes 524320 | tf_op jit(solution)/shard_map/ppermute | solution.py:29
  111.6 0.6 collective-permute-start.21
  112.3 2.7 %collective-permute-done.16.refs_15_.refs_6_ = bf16[256,1024]{1,0:T(8,128)(2,1)S(1)} collective-permute-done((bf16[256,1024]{1,0:T(8,128)(2,1)S(1)}, bf16[256,1024]{1,0:T(8,128)(2,1)S(1)}, u32[]{:S(2)}, u32[]{:S(2)}) %collective-permute-start.16) | collective-permute-done | bytes 524320 | tf_op jit(solution)/shard_map/ppermute | solution.py:29
  115.0 0.4 collective-permute-start.25
  115.4 0.4 copy-done.31
  115.8 0.6 copy-done.30
  116.4 9.3 %shard_map.51 = (f32[2048,256]{1,0:T(8,128)}, f32[2048,256]{1,0:T(8,128)}) custom-call(s32[17]{0:T(128)S(1)} %stack.78.info.rows._, bf16[2048,256]{1,0:T(8,128)(2,1)} %get-tuple-element.33.own_w, bf16[2048,256]{1,0:T(8,128)(2,1)} %copy-done.30, bf16[256,1024]{1,0:T(8,128)(2,1)} %constant_dynamic-update-slice_fusion.refs_0_, ...), custom_call_target="tpu_custom_call" | custom-call | flops 4294967296 | bytes 14680064 | tf_op jit(solution)/shard_map/pallas_call | solution.py:188
  125.7 1.7 collective-permute-start.19
  127.4 1.0 copy-done.16
  128.5 1.0 copy-done.18
  129.5 4.0 %shard_map.54 = (f32[512,256]{1,0:T(8,128)S(1)}, f32[512,256]{1,0:T(8,128)S(1)}, f32[512,256]{1,0:T(8,128)S(1)}, f32[512,256]{1,0:T(8,128)S(1)}) custom-call(s32[17]{0:T(128)S(1)} %stack.78.info.rows._, bf16[512,2048]{1,0:T(8,128)(2,1)} %copy-done, bf16[256,1024]{1,0:T(8,128)(2,1)S(1)} %copy-done.20, bf16[256,1024]{1,0:T(8,128)(2,1)S(1)} %copy-done.4, ...), custom_call_target="tpu_custom_call" | custom-call | flops 2147483648 | bytes 8388608 | tf_op jit(solution)/shard_map/pallas_call | solution.py:160
  133.6 1.5 collective-permute-start.22
  135.2 1.3 collective-permute-start.26
  136.5 11.9 %collective-permute-done.22 = f32[512,256]{1,0:T(8,128)S(1)} collective-permute-done((f32[512,256]{1,0:T(8,128)S(1)}, f32[512,256]{1,0:T(8,128)S(1)}, u32[]{:S(2)}, u32[]{:S(2)}) %collective-permute-start.22) | collective-permute-done | bytes 524320 | tf_op jit(solution)/shard_map/ppermute | solution.py:29
  148.9 2.5 %collective-permute-start.27 = (f32[512,256]{1,0:T(8,128)S(1)}, f32[512,256]{1,0:T(8,128)S(1)}, u32[]{:S(2)}, u32[]{:S(2)}) collective-permute-start(f32[512,256]{1,0:T(8,128)S(1)} %add.261), channel_id=1, source_target_pairs={{0,112},{16,0},{32,16},{48,32},{64,48},{80,64},{96,80},{112,96},{1... | collective-permute-start | bytes 1572872 | tf_op jit(solution)/shard_map/ppermute | solution.py:29
  151.4 11.0 %collective-permute-done.23 = f32[512,256]{1,0:T(8,128)S(1)} collective-permute-done((f32[512,256]{1,0:T(8,128)S(1)}, f32[512,256]{1,0:T(8,128)S(1)}, u32[]{:S(2)}, u32[]{:S(2)}) %collective-permute-start.23) | collective-permute-done | bytes 524320 | tf_op jit(solution)/shard_map/ppermute | solution.py:29
  162.5 0.8 copy-done.28
  163.3 0.8 copy-done.29
  164.1 1.4 add_add_fusion
  165.6 1.0 collective-permute-start.28
  166.6 4.3 %collective-permute-start.29 = (f32[256,256]{1,0:T(8,128)S(1)}, f32[256,256]{1,0:T(8,128)S(1)}, u32[]{:S(2)}, u32[]{:S(2)}) collective-permute-start(f32[256,256]{1,0:T(8,128)S(1)} %get-tuple-element.34), channel_id=1, source_target_pairs={{1,128},{128,1},{3,130},{130,3},{5,132},{132,5},{7,134},{134,7},{9... | collective-permute-start | bytes 786440 | tf_op jit(solution)/shard_map/ppermute | solution.py:29
  170.9 4.9 %collective-permute-done.29 = f32[256,256]{1,0:T(8,128)S(1)} collective-permute-done((f32[256,256]{1,0:T(8,128)S(1)}, f32[256,256]{1,0:T(8,128)S(1)}, u32[]{:S(2)}, u32[]{:S(2)}) %collective-permute-start.29) | collective-permute-done | bytes 262176 | tf_op jit(solution)/shard_map/ppermute | solution.py:29
  175.9 0.8 copy.5
  176.7 2.8 %add_convert_fusion = bf16[2048,256]{1,0:T(8,128)(2,1)} fusion(f32[2048,256]{1,0:T(8,128)S(1)} %copy-done.21, f32[2048,256]{1,0:T(8,128)} %collective-permute-done.19), kind=kLoop, calls=%fused_computation | loop fusion | flops 1048576 | bytes 5242880 | tf_op jit(solution)/shard_map/convert_element_type | solution.py:196
  (101 shorter events, 2.1 us)
Async XLA Ops:
  7.2 11.6 %copy-start.1 = (bf16[2048,256]{1,0:T(8,128)(2,1)S(1)}, bf16[2048,256]{1,0:T(8,128)(2,1)}, u32[]{:S(2)}) copy-start(bf16[2048,256]{1,0:T(8,128)(2,1)} %own.1) | copy-start | bytes 3145732
  7.2 69.7 %all-gather.2.cloned.1.call-start = ((), (), s32[]{:S(2)}) async-start(), calls=%async_computation | async-start | bytes 2228224 | tf_op jit(solution)/shard_map/all_gather | solution.py:148
  8.0 1.2 copy-start.2
  10.6 4.4 %collective-permute-start.1 = (bf16[128,1024]{1,0:T(8,128)(2,1)S(1)}, bf16[128,1024]{1,0:T(8,128)(2,1)S(1)}, u32[]{:S(2)}, u32[]{:S(2)}) collective-permute-start(bf16[128,1024]{1,0:T(8,128)(2,1)S(1)} %get-tuple-element.17), channel_id=1, source_target_pairs={{0,1},{1,0},{2,3},{3,2},{4,5},{5,4},{6,7},{7,6},{8,9},{9,8},{10,11... | collective-permute-start | bytes 786440 | tf_op jit(solution)/shard_map/ppermute | solution.py:29
  15.7 15.0 %collective-permute-start.2 = (bf16[256,1024]{1,0:T(8,128)(2,1)}, bf16[256,1024]{1,0:T(8,128)(2,1)S(1)}, u32[]{:S(2)}, u32[]{:S(2)}) collective-permute-start(bf16[256,1024]{1,0:T(8,128)(2,1)} %constant_dynamic-update-slice_fusion.refs_0_), channel_id=1, source_target_pairs={{0,8},{8,0},{1,9},{9,1},{2,10},{10,2},{3,11},{11,3},{4,12},{12,4},... | collective-permute-start | bytes 1572872 | tf_op jit(solution)/shard_map/ppermute | solution.py:29
  16.9 3.8 %collective-permute-start.10 = (bf16[128,1024]{1,0:T(8,128)(2,1)}, bf16[128,1024]{1,0:T(8,128)(2,1)}, u32[]{:S(2)}, u32[]{:S(2)}) collective-permute-start(bf16[128,1024]{1,0:T(8,128)(2,1)} %get-tuple-element.19), channel_id=1, source_target_pairs={{0,1},{1,0},{2,3},{3,2},{4,5},{5,4},{6,7},{7,6},{8,9},{9,8},{10,11... | collective-permute-start | bytes 786440 | tf_op jit(solution)/shard_map/ppermute | solution.py:29
  17.6 15.0 %collective-permute-start.3 = (bf16[256,1024]{1,0:T(8,128)(2,1)}, bf16[256,1024]{1,0:T(8,128)(2,1)S(1)}, u32[]{:S(2)}, u32[]{:S(2)}) collective-permute-start(bf16[256,1024]{1,0:T(8,128)(2,1)} %constant_dynamic-update-slice_fusion.refs_0_), channel_id=1, source_target_pairs={{0,2},{2,4},{4,6},{6,0},{1,3},{3,5},{5,7},{7,1},{8,10},{10,12},{12... | collective-permute-start | bytes 1572872 | tf_op jit(solution)/shard_map/ppermute | solution.py:29
  18.8 70.1 %collective-permute-start.20 = (bf16[2048,256]{1,0:T(8,128)(2,1)S(1)}, bf16[2048,256]{1,0:T(8,128)(2,1)S(1)}, u32[]{:S(2)}, u32[]{:S(2)}) collective-permute-start(bf16[2048,256]{1,0:T(8,128)(2,1)S(1)} %copy-done.1), channel_id=1, source_target_pairs={{0,1},{1,0},{2,3},{3,2},{4,5},{5,4},{6,7},{7,6},{8,9},{9,8},{10,11... | collective-permute-start | bytes 3145736 | tf_op jit(solution)/shard_map/ppermute | solution.py:29
  19.2 14.8 %collective-permute-start.4 = (bf16[256,1024]{1,0:T(8,128)(2,1)}, bf16[256,1024]{1,0:T(8,128)(2,1)S(1)}, u32[]{:S(2)}, u32[]{:S(2)}) collective-permute-start(bf16[256,1024]{1,0:T(8,128)(2,1)} %constant_dynamic-update-slice_fusion.refs_0_), channel_id=1, source_target_pairs={{0,6},{2,0},{4,2},{6,4},{1,7},{3,1},{5,3},{7,5},{8,14},{10,8},{12,... | collective-permute-start | bytes 1572872 | tf_op jit(solution)/shard_map/ppermute | solution.py:29
  21.7 12.5 %copy-start.19 = (bf16[256,1024]{1,0:T(8,128)(2,1)}, bf16[256,1024]{1,0:T(8,128)(2,1)S(1)}, u32[]{:S(2)}) copy-start(bf16[256,1024]{1,0:T(8,128)(2,1)S(1)} %constant_dynamic-update-slice_fusion.2.refs_9_.refs_0_) | copy-start | bytes 1572868
  21.7 28.4 %collective-permute-start.11 = (bf16[256,1024]{1,0:T(8,128)(2,1)S(1)}, bf16[256,1024]{1,0:T(8,128)(2,1)S(1)}, u32[]{:S(2)}, u32[]{:S(2)}) collective-permute-start(bf16[256,1024]{1,0:T(8,128)(2,1)S(1)} %constant_dynamic-update-slice_fusion.2.refs_9_.refs_0_), channel_id=1, source_target_pairs={{0,8},{8,0},{1,9},{9,1},{2,10},{10,2},{3,11},{11,3},{4,12},{12,4},... | collective-permute-start | bytes 1572872 | tf_op jit(solution)/shard_map/ppermute | solution.py:29
  30.7 21.1 %collective-permute-start.12 = (bf16[256,1024]{1,0:T(8,128)(2,1)S(1)}, bf16[256,1024]{1,0:T(8,128)(2,1)S(1)}, u32[]{:S(2)}, u32[]{:S(2)}) collective-permute-start(bf16[256,1024]{1,0:T(8,128)(2,1)S(1)} %constant_dynamic-update-slice_fusion.2.refs_9_.refs_0_), channel_id=1, source_target_pairs={{0,2},{2,4},{4,6},{6,0},{1,3},{3,5},{5,7},{7,1},{8,10},{10,12},{12... | collective-permute-start | bytes 1572872 | tf_op jit(solution)/shard_map/ppermute | solution.py:29
  32.5 24.1 %collective-permute-start.13 = (bf16[256,1024]{1,0:T(8,128)(2,1)S(1)}, bf16[256,1024]{1,0:T(8,128)(2,1)S(1)}, u32[]{:S(2)}, u32[]{:S(2)}) collective-permute-start(bf16[256,1024]{1,0:T(8,128)(2,1)S(1)} %constant_dynamic-update-slice_fusion.2.refs_9_.refs_0_), channel_id=1, source_target_pairs={{0,6},{2,0},{4,2},{6,4},{1,7},{3,1},{5,3},{7,5},{8,14},{10,8},{12,... | collective-permute-start | bytes 1572872 | tf_op jit(solution)/shard_map/ppermute | solution.py:29
  34.0 17.8 %copy-start.7 = (bf16[256,1024]{1,0:T(8,128)(2,1)}, bf16[256,1024]{1,0:T(8,128)(2,1)S(1)}, u32[]{:S(2)}) copy-start(bf16[256,1024]{1,0:T(8,128)(2,1)S(1)} %collective-permute-done.4.refs_3_) | copy-start | bytes 1572868
  34.0 23.5 %collective-permute-start.5 = (bf16[256,1024]{1,0:T(8,128)(2,1)S(1)}, bf16[256,1024]{1,0:T(8,128)(2,1)S(1)}, u32[]{:S(2)}, u32[]{:S(2)}) collective-permute-start(bf16[256,1024]{1,0:T(8,128)(2,1)S(1)} %pad_maximum_fusion), channel_id=1, source_target_pairs={{0,2},{2,4},{4,6},{6,0},{1,3},{3,5},{5,7},{7,1},{8,10},{10,12},{12... | collective-permute-start | bytes 1572872 | tf_op jit(solution)/shard_map/ppermute | solution.py:29
  50.1 7.5 %copy-start.3 = (bf16[256,1024]{1,0:T(8,128)(2,1)}, bf16[256,1024]{1,0:T(8,128)(2,1)S(1)}, u32[]{:S(2)}) copy-start(bf16[256,1024]{1,0:T(8,128)(2,1)S(1)} %collective-permute-done.11.refs_10_.refs_1_) | copy-start | bytes 1572868
  50.1 12.0 %collective-permute-start.6 = (bf16[256,1024]{1,0:T(8,128)(2,1)S(1)}, bf16[256,1024]{1,0:T(8,128)(2,1)S(1)}, u32[]{:S(2)}, u32[]{:S(2)}) collective-permute-start(bf16[256,1024]{1,0:T(8,128)(2,1)S(1)} %pad_maximum_fusion.1), channel_id=1, source_target_pairs={{0,6},{2,0},{4,2},{6,4},{1,7},{3,1},{5,3},{7,5},{8,14},{10,8},{12,... | collective-permute-start | bytes 1572872 | tf_op jit(solution)/shard_map/ppermute | solution.py:29
  51.8 5.8 %copy-start.5 = (bf16[256,1024]{1,0:T(8,128)(2,1)}, bf16[256,1024]{1,0:T(8,128)(2,1)S(1)}, u32[]{:S(2)}) copy-start(bf16[256,1024]{1,0:T(8,128)(2,1)S(1)} %collective-permute-done.12.refs_11_.refs_2_) | copy-start | bytes 1572868
  51.8 41.4 %collective-permute-start.7 = (bf16[256,1024]{1,0:T(8,128)(2,1)}, bf16[256,1024]{1,0:T(8,128)(2,1)}, u32[]{:S(2)}, u32[]{:S(2)}) collective-permute-start(bf16[256,1024]{1,0:T(8,128)(2,1)} %pad_maximum_fusion.2), channel_id=1, source_target_pairs={{0,8},{8,0},{1,9},{9,1},{2,10},{10,2},{3,11},{11,3},{4,12},{12,4},... | collective-permute-start | bytes 1572872 | tf_op jit(solution)/shard_map/ppermute | solution.py:29
  56.7 1.7 copy-start.9
  57.6 0.9 copy-start.11
  58.3 36.0 %collective-permute-start.8 = (bf16[128,1024]{1,0:T(8,128)(2,1)}, bf16[128,1024]{1,0:T(8,128)(2,1)S(1)}, u32[]{:S(2)}, u32[]{:S(2)}) collective-permute-start(bf16[128,1024]{1,0:T(8,128)(2,1)} %slice.78), channel_id=1, source_target_pairs={{0,2},{2,4},{4,6},{6,0},{1,3},{3,5},{5,7},{7,1},{8,10},{10,12},{12... | collective-permute-start | bytes 786440 | tf_op jit(solution)/shard_map/ppermute | solution.py:29
  62.8 0.8 copy-start.13
  63.6 30.8 %collective-permute-start.9 = (bf16[128,1024]{1,0:T(8,128)(2,1)}, bf16[128,1024]{1,0:T(8,128)(2,1)}, u32[]{:S(2)}, u32[]{:S(2)}) collective-permute-start(bf16[128,1024]{1,0:T(8,128)(2,1)} %slice.79), channel_id=1, source_target_pairs={{0,6},{2,0},{4,2},{6,4},{1,7},{3,1},{5,3},{7,5},{8,14},{10,8},{12,... | collective-permute-start | bytes 786440 | tf_op jit(solution)/shard_map/ppermute | solution.py:29
  76.8 11.9 %copy-start.25 = (bf16[128,1024]{1,0:T(8,128)(2,1)S(1)}, bf16[128,1024]{1,0:T(8,128)(2,1)}, u32[]{:S(2)}) copy-start(bf16[128,1024]{1,0:T(8,128)(2,1)} %get-tuple-element.41) | copy-start | bytes 786436
  76.8 11.9 %copy-start.26 = (bf16[128,1024]{1,0:T(8,128)(2,1)S(1)}, bf16[128,1024]{1,0:T(8,128)(2,1)}, u32[]{:S(2)}) copy-start(bf16[128,1024]{1,0:T(8,128)(2,1)} %get-tuple-element.37) | copy-start | bytes 786436
  76.8 11.9 %copy-start.24 = (bf16[128,1024]{1,0:T(8,128)(2,1)S(1)}, bf16[128,1024]{1,0:T(8,128)(2,1)}, u32[]{:S(2)}) copy-start(bf16[128,1024]{1,0:T(8,128)(2,1)} %get-tuple-element.40) | copy-start | bytes 786436
  76.8 11.9 %copy-start.27 = (bf16[128,1024]{1,0:T(8,128)(2,1)S(1)}, bf16[128,1024]{1,0:T(8,128)(2,1)}, u32[]{:S(2)}) copy-start(bf16[128,1024]{1,0:T(8,128)(2,1)} %get-tuple-element.39) | copy-start | bytes 786436
  79.6 35.8 %collective-permute-start = (bf16[2048,256]{1,0:T(8,128)(2,1)S(1)}, bf16[2048,256]{1,0:T(8,128)(2,1)S(1)}, u32[]{:S(2)}, u32[]{:S(2)}) collective-permute-start(bf16[2048,256]{1,0:T(8,128)(2,1)S(1)} %get-tuple-element.32), channel_id=1, source_target_pairs={{0,1},{1,0},{2,3},{3,2},{4,5},{5,4},{6,7},{7,6},{8,9},{9,8},{10,11... | collective-permute-start | bytes 3145736 | tf_op jit(solution)/shard_map/ppermute | solution.py:29
  88.8 5.5 %copy-start.8 = (bf16[256,1024]{1,0:T(8,128)(2,1)S(1)}, bf16[256,1024]{1,0:T(8,128)(2,1)}, u32[]{:S(2)}) copy-start(bf16[256,1024]{1,0:T(8,128)(2,1)} %copy-done.7) | copy-start | bytes 1572868
  88.8 5.5 %copy-start.12 = (bf16[256,1024]{1,0:T(8,128)(2,1)S(1)}, bf16[256,1024]{1,0:T(8,128)(2,1)}, u32[]{:S(2)}) copy-start(bf16[256,1024]{1,0:T(8,128)(2,1)} %copy-done.11) | copy-start | bytes 1572868
  88.8 5.5 %copy-start.14 = (bf16[256,1024]{1,0:T(8,128)(2,1)S(1)}, bf16[256,1024]{1,0:T(8,128)(2,1)}, u32[]{:S(2)}) copy-start(bf16[256,1024]{1,0:T(8,128)(2,1)} %copy-done.13) | copy-start | bytes 1572868
  88.9 15.0 %collective-permute-start.14 = (bf16[256,1024]{1,0:T(8,128)(2,1)S(1)}, bf16[256,1024]{1,0:T(8,128)(2,1)S(1)}, u32[]{:S(2)}, u32[]{:S(2)}) collective-permute-start(bf16[256,1024]{1,0:T(8,128)(2,1)S(1)} %pad_maximum_fusion.3), channel_id=1, source_target_pairs={{0,2},{2,4},{4,6},{6,0},{1,3},{3,5},{5,7},{7,1},{8,10},{10,12},{12... | collective-permute-start | bytes 1572872 | tf_op jit(solution)/shard_map/ppermute | solution.py:29
  91.9 1.3 copy-start
  93.2 7.6 %copy-start.22 = (bf16[128,1024]{1,0:T(8,128)(2,1)S(1)}, bf16[128,1024]{1,0:T(8,128)(2,1)}, u32[]{:S(2)}) copy-start(bf16[128,1024]{1,0:T(8,128)(2,1)} %get-tuple-element.36) | copy-start | bytes 786436
  93.2 7.6 %copy-start.23 = (bf16[128,1024]{1,0:T(8,128)(2,1)S(1)}, bf16[128,1024]{1,0:T(8,128)(2,1)}, u32[]{:S(2)}) copy-start(bf16[128,1024]{1,0:T(8,128)(2,1)} %get-tuple-element.38) | copy-start | bytes 786436
  93.2 13.2 %collective-permute-start.15 = (bf16[256,1024]{1,0:T(8,128)(2,1)S(1)}, bf16[256,1024]{1,0:T(8,128)(2,1)S(1)}, u32[]{:S(2)}, u32[]{:S(2)}) collective-permute-start(bf16[256,1024]{1,0:T(8,128)(2,1)S(1)} %pad_maximum_fusion.4), channel_id=1, source_target_pairs={{0,6},{2,0},{4,2},{6,4},{1,7},{3,1},{5,3},{7,5},{8,14},{10,8},{12,... | collective-permute-start | bytes 1572872 | tf_op jit(solution)/shard_map/ppermute | solution.py:29
  98.6 17.8 %copy-start.4 = (bf16[256,1024]{1,0:T(8,128)(2,1)S(1)}, bf16[256,1024]{1,0:T(8,128)(2,1)}, u32[]{:S(2)}) copy-start(bf16[256,1024]{1,0:T(8,128)(2,1)} %copy-done.3) | copy-start | bytes 1572868
  98.6 17.8 %copy-start.20 = (bf16[256,1024]{1,0:T(8,128)(2,1)S(1)}, bf16[256,1024]{1,0:T(8,128)(2,1)}, u32[]{:S(2)}) copy-start(bf16[256,1024]{1,0:T(8,128)(2,1)} %copy-done.19) | copy-start | bytes 1572868
  98.7 13.0 %collective-permute-start.24 = (f32[512,256]{1,0:T(8,128)S(1)}, f32[512,256]{1,0:T(8,128)S(1)}, u32[]{:S(2)}, u32[]{:S(2)}) collective-permute-start(f32[512,256]{1,0:T(8,128)S(1)} %get-tuple-element.26), channel_id=1, source_target_pairs={{0,112},{16,0},{32,16},{48,32},{64,48},{80,64},{96,80},{112,96},{1... | collective-permute-start | bytes 1572872 | tf_op jit(solution)/shard_map/ppermute | solution.py:29
  100.8 14.2 %collective-permute-start.16 = (bf16[256,1024]{1,0:T(8,128)(2,1)S(1)}, bf16[256,1024]{1,0:T(8,128)(2,1)S(1)}, u32[]{:S(2)}, u32[]{:S(2)}) collective-permute-start(bf16[256,1024]{1,0:T(8,128)(2,1)S(1)} %pad_maximum_fusion.5), channel_id=1, source_target_pairs={{0,8},{8,0},{1,9},{9,1},{2,10},{10,2},{3,11},{11,3},{4,12},{12,4},... | collective-permute-start | bytes 1572872 | tf_op jit(solution)/shard_map/ppermute | solution.py:29
  103.9 11.5 %copy-start.15 = (bf16[256,1024]{1,0:T(8,128)(2,1)}, bf16[256,1024]{1,0:T(8,128)(2,1)S(1)}, u32[]{:S(2)}) copy-start(bf16[256,1024]{1,0:T(8,128)(2,1)S(1)} %collective-permute-done.14.refs_13_.refs_4_) | copy-start | bytes 1572868
  103.9 11.5 %collective-permute-start.17 = (bf16[128,1024]{1,0:T(8,128)(2,1)S(1)}, bf16[128,1024]{1,0:T(8,128)(2,1)S(1)}, u32[]{:S(2)}, u32[]{:S(2)}) collective-permute-start(bf16[128,1024]{1,0:T(8,128)(2,1)S(1)} %slice.86), channel_id=1, source_target_pairs={{0,2},{2,4},{4,6},{6,0},{1,3},{3,5},{5,7},{7,1},{8,10},{10,12},{12... | collective-permute-start | bytes 786440 | tf_op jit(solution)/shard_map/ppermute | solution.py:29
  106.4 9.0 %copy-start.17 = (bf16[256,1024]{1,0:T(8,128)(2,1)}, bf16[256,1024]{1,0:T(8,128)(2,1)S(1)}, u32[]{:S(2)}) copy-start(bf16[256,1024]{1,0:T(8,128)(2,1)S(1)} %collective-permute-done.15.refs_14_.refs_5_) | copy-start | bytes 1572868
  106.4 8.9 %collective-permute-start.18 = (bf16[128,1024]{1,0:T(8,128)(2,1)S(1)}, bf16[128,1024]{1,0:T(8,128)(2,1)S(1)}, u32[]{:S(2)}, u32[]{:S(2)}) collective-permute-start(bf16[128,1024]{1,0:T(8,128)(2,1)S(1)} %slice.87), channel_id=1, source_target_pairs={{0,6},{2,0},{4,2},{6,4},{1,7},{3,1},{5,3},{7,5},{8,14},{10,8},{12,... | collective-permute-start | bytes 786440 | tf_op jit(solution)/shard_map/ppermute | solution.py:29
  111.6 21.9 %collective-permute-start.21 = (f32[512,256]{1,0:T(8,128)S(1)}, f32[512,256]{1,0:T(8,128)S(1)}, u32[]{:S(2)}, u32[]{:S(2)}) collective-permute-start(f32[512,256]{1,0:T(8,128)S(1)} %get-tuple-element.22), channel_id=1, source_target_pairs={{0,16},{16,32},{32,48},{48,64},{64,80},{80,96},{96,112},{112,0},{1... | collective-permute-start | bytes 1572872 | tf_op jit(solution)/shard_map/ppermute | solution.py:29
  115.0 0.8 copy-start.31
  115.0 20.1 %collective-permute-start.25 = (f32[512,256]{1,0:T(8,128)S(1)}, f32[512,256]{1,0:T(8,128)S(1)}, u32[]{:S(2)}, u32[]{:S(2)}) collective-permute-start(f32[512,256]{1,0:T(8,128)S(1)} %add.259), channel_id=1, source_target_pairs={{0,112},{16,0},{32,16},{48,32},{64,48},{80,64},{96,80},{112,96},{1... | collective-permute-start | bytes 1572872 | tf_op jit(solution)/shard_map/ppermute | solution.py:29
  115.4 1.0 copy-start.30
  116.4 11.0 %copy-start.6 = (bf16[256,1024]{1,0:T(8,128)(2,1)S(1)}, bf16[256,1024]{1,0:T(8,128)(2,1)}, u32[]{:S(2)}) copy-start(bf16[256,1024]{1,0:T(8,128)(2,1)} %copy-done.5) | copy-start | bytes 1572868
  116.4 11.0 %copy-start.10 = (bf16[256,1024]{1,0:T(8,128)(2,1)S(1)}, bf16[256,1024]{1,0:T(8,128)(2,1)}, u32[]{:S(2)}) copy-start(bf16[256,1024]{1,0:T(8,128)(2,1)} %copy-done.9) | copy-start | bytes 1572868
  125.7 51.0 %collective-permute-start.19 = (f32[2048,256]{1,0:T(8,128)}, f32[2048,256]{1,0:T(8,128)}, u32[]{:S(2)}, u32[]{:S(2)}) collective-permute-start(f32[2048,256]{1,0:T(8,128)} %get-tuple-element.21), channel_id=1, source_target_pairs={{0,1},{1,0},{2,3},{3,2},{4,5},{5,4},{6,7},{7,6},{8,9},{9,8},{10,11... | collective-permute-start | bytes 6291464 | tf_op jit(solution)/shard_map/ppermute | solution.py:29
  127.4 1.0 copy-start.16
  128.5 1.0 copy-start.18
  133.6 14.8 %collective-permute-start.22 = (f32[512,256]{1,0:T(8,128)S(1)}, f32[512,256]{1,0:T(8,128)S(1)}, u32[]{:S(2)}, u32[]{:S(2)}) collective-permute-start(f32[512,256]{1,0:T(8,128)S(1)} %add.256), channel_id=1, source_target_pairs={{0,16},{16,32},{32,48},{48,64},{64,80},{80,96},{96,112},{112,0},{1... | collective-permute-start | bytes 1572872 | tf_op jit(solution)/shard_map/ppermute | solution.py:29
  135.2 13.6 %collective-permute-start.26 = (f32[512,256]{1,0:T(8,128)S(1)}, f32[512,256]{1,0:T(8,128)S(1)}, u32[]{:S(2)}, u32[]{:S(2)}) collective-permute-start(f32[512,256]{1,0:T(8,128)S(1)} %add.260), channel_id=1, source_target_pairs={{0,112},{16,0},{32,16},{48,32},{64,48},{80,64},{96,80},{112,96},{1... | collective-permute-start | bytes 1572872 | tf_op jit(solution)/shard_map/ppermute | solution.py:29
  148.5 13.9 %collective-permute-start.23 = (f32[512,256]{1,0:T(8,128)S(1)}, f32[512,256]{1,0:T(8,128)S(1)}, u32[]{:S(2)}, u32[]{:S(2)}) collective-permute-start(f32[512,256]{1,0:T(8,128)S(1)} %add.257), channel_id=1, source_target_pairs={{0,16},{16,32},{32,48},{48,64},{64,80},{80,96},{96,112},{112,0},{1... | collective-permute-start | bytes 1572872 | tf_op jit(solution)/shard_map/ppermute | solution.py:29
  148.9 13.6 %collective-permute-start.27 = (f32[512,256]{1,0:T(8,128)S(1)}, f32[512,256]{1,0:T(8,128)S(1)}, u32[]{:S(2)}, u32[]{:S(2)}) collective-permute-start(f32[512,256]{1,0:T(8,128)S(1)} %add.261), channel_id=1, source_target_pairs={{0,112},{16,0},{32,16},{48,32},{64,48},{80,64},{96,80},{112,96},{1... | collective-permute-start | bytes 1572872 | tf_op jit(solution)/shard_map/ppermute | solution.py:29
  162.5 0.8 copy-start.28
  163.3 0.8 copy-start.29
  164.1 12.7 %copy-start.21 = (f32[2048,256]{1,0:T(8,128)S(1)}, f32[2048,256]{1,0:T(8,128)}, u32[]{:S(2)}) copy-start(f32[2048,256]{1,0:T(8,128)} %get-tuple-element.20) | copy-start | bytes 6291460
  165.6 5.3 %collective-permute-start.28 = (f32[256,256]{1,0:T(8,128)S(1)}, f32[256,256]{1,0:T(8,128)S(1)}, u32[]{:S(2)}, u32[]{:S(2)}) collective-permute-start(f32[256,256]{1,0:T(8,128)S(1)} %get-tuple-element.35), channel_id=1, source_target_pairs={{0,1},{1,129},{128,0},{129,128},{2,3},{3,131},{130,2},{131,130},{4... | collective-permute-start | bytes 786440 | tf_op jit(solution)/shard_map/ppermute | solution.py:29
  166.6 9.3 %collective-permute-start.29 = (f32[256,256]{1,0:T(8,128)S(1)}, f32[256,256]{1,0:T(8,128)S(1)}, u32[]{:S(2)}, u32[]{:S(2)}) collective-permute-start(f32[256,256]{1,0:T(8,128)S(1)} %get-tuple-element.34), channel_id=1, source_target_pairs={{1,128},{128,1},{3,130},{130,3},{5,132},{132,5},{7,134},{134,7},{9... | collective-permute-start | bytes 786440 | tf_op jit(solution)/shard_map/ppermute | solution.py:29
Sparse Core Ops, SparseCore 0:
  9.8 66.9 all-gather.1

commit v2 on v0

v2 whole, which is shorter than its diff:
```python
import functools

import jax
import jax.numpy as jnp
import numpy as np
from jax import lax
from jax.experimental import pallas as pl
from jax.experimental.pallas import tpu as pltpu
from jax.sharding import Mesh
from jax.sharding import PartitionSpec as P

AXES = ("yl", "z", "yh", "x", "c")
SIZES = dict(yl=2, z=8, yh=2, x=4, c=2)
BF16, F32 = jnp.bfloat16, jnp.float32
HALF = 128
TOK = 256
BLK = 256
FEAT = 2 * BLK
N_Z = 8
STEPS = 4
MIB = 1 << 20


def permute(value, axes, target):
    shape = [SIZES[a] for a in axes]
    pairs = []
    for at in np.ndindex(*shape):
        to = target(*at)
        if to is None:
            continue
        to = tuple(v % s for v, s in zip(to, shape))
        pairs.append((int(np.ravel_multi_index(at, shape)), int(np.ravel_multi_index(to, shape))))
    return lax.ppermute(value, axes if len(axes) > 1 else axes[0], pairs)


def along_x(v):
    return permute(v, ("x", "c"), lambda i, c: (i + 1 - 2 * c, c))


def along_z(v):
    return permute(v, ("z", "yh", "x", "c"), lambda z, y, i, c: (z - 1 + 2 * c, y, i, c))


def along_z_last(v):
    return permute(
        v, ("z", "yh", "x", "c"), lambda z, y, i, c: (z - 1, y, i, c) if c == 0 else None
    )


def against_z(v):
    return permute(v, ("z", "yh", "x", "c"), lambda z, y, i, c: (z + 1 - 2 * c, y, i, c))


def against_z_last(v):
    return permute(
        v, ("z", "yh", "x", "c"), lambda z, y, i, c: (z + 1, y, i, c) if c == 0 else None
    )


def across(v):
    return permute(v, ("yh",), lambda i: (i + 1,))


def across_other(v):
    return permute(v, ("yh", "x", "c"), lambda i, x, c: (i + 1, x, 1 - c))


def across_lo(v):
    return permute(v, ("yl",), lambda i: (i + 1,))


def core(v):
    return permute(v, ("c",), lambda i: (i + 1,))


def call(kernel, out_shape, vmem, pos, *args, scratch=(), flops=0):
    return pl.pallas_call(
        kernel,
        out_shape=out_shape,
        in_specs=[pl.BlockSpec(memory_space=pltpu.SMEM)]
        + [pl.BlockSpec(memory_space=pltpu.VMEM)] * len(args),
        out_specs=jax.tree.map(lambda _: pl.BlockSpec(memory_space=pltpu.VMEM), out_shape),
        scratch_shapes=list(scratch),
        compiler_params=pltpu.CompilerParams(vmem_limit_bytes=vmem * MIB),
        cost_estimate=pl.CostEstimate(flops=flops, bytes_accessed=1 << 16, transcendentals=0),
    )(pos, *args)


def shape(rows, columns, dtype=BF16):
    return jax.ShapeDtypeStruct((rows, columns), dtype)


def owner_row(z, core_at, step, y_lo):
    distance = jnp.where(core_at == 0, 4 + step, 3 - step)
    return pl.multiple_of((y_lo * N_Z + lax.rem(z + distance, N_Z)) * BLK, BLK)


def token_blocks(pos):
    yh, x, c = pos[1], pos[2], pos[3]
    s = 2 * c - 1

    def at(dy, dx, half):
        return lax.rem(yh + dy, 2) * 8 + lax.rem(x + dx + 4, 4) * 2 + half

    whole = ((0, 0), (1, 0), (0, s))
    out = [at(dy, dx, h) for dy, dx in whole for h in (0, 1)]
    out += [at(0, 2, c)]
    out += [at(dy, dx, h) for dy, dx in ((1, s), (1, -s), (1, 2), (0, -s)) for h in (0, 1)]
    out += [at(0, 2, 1 - c)]
    return out


def parts_of(stage):
    return [p for p in (3, 2, 1) if 0 <= stage - p < STEPS]


def offset(kind, stage, part):
    rows = {"x": {1: 2 * TOK, 2: 2 * TOK, 3: TOK}, "y": {1: TOK, 2: TOK}, "d": {2: TOK, 3: HALF}}[kind]
    at = 0
    for p in parts_of(stage):
        if p == part:
            return at
        at += rows.get(p, 0)
    return at


def pack_kernel(stage, pos, *refs):
    parts = parts_of(stage)
    z, c, yl = pos[0], pos[3], pos[4]
    refs = list(refs)
    if 1 in parts:
        mine, other = refs.pop(0), refs.pop(0)
    if stage > 1:
        x_in, y_in = refs.pop(0), refs.pop(0)
    outs = refs[-1 - (2 in parts or 1 in parts) - (2 in parts or 3 in parts) - (1 in parts) :]
    outs = list(outs)
    x_out = outs.pop(0)
    y_out = outs.pop(0) if (2 in parts or 1 in parts) else None
    d_out = outs.pop(0) if (2 in parts or 3 in parts) else None
    before = stage - 1
    if 3 in parts:
        was = offset("x", before, 2)
        to = offset("x", stage, 3)
        x_out[to : to + TOK] = x_in[was + TOK : was + 2 * TOK]
        to = offset("d", stage, 3)
        d_out[to : to + HALF] = x_in[was + HALF : was + TOK]
    if 2 in parts:
        was = offset("x", before, 1)
        to = offset("x", stage, 2)
        half = pl.multiple_of(c * HALF, HALF)
        x_out[to : to + HALF] = x_in[pl.ds(was + half, HALF), :]
        x_out[to + HALF : to + TOK] = x_in[pl.ds(was + TOK + half, HALF), :]
        had = offset("y", before, 1)
        x_out[to + TOK : to + 2 * TOK] = y_in[had : had + TOK]
        far = x_in[was + TOK : was + 2 * TOK]
        to = offset("y", stage, 2)
        y_out[to : to + TOK] = far
        to = offset("d", stage, 2)
        d_out[to : to + TOK] = far
    if 1 in parts:
        own = outs.pop(0)
        x_to, y_to = offset("x", stage, 1), offset("y", stage, 1)
        for rel in range(2):
            y_lo = lax.rem(yl + 1 + rel, 2)
            to = slice(rel * BLK, (rel + 1) * BLK)
            for which, core_at in enumerate((c, 1 - c)):
                col = owner_row(z, core_at, stage - 1, y_lo)
                for src, at in ((mine, c), (other, 1 - c)):
                    block = src[:, pl.ds(col, BLK)]
                    row = pl.multiple_of(at * HALF, HALF)
                    x_out[pl.ds(x_to + which * TOK + row, HALF), to] = block
                    if which == 0:
                        own[pl.ds(row, HALF), to] = block
                    else:
                        y_out[pl.ds(y_to + row, HALF), to] = block


def pieces_of(step, own, xs, ys, ds):
    a, b, c = step + 1, step + 2, step + 3
    x1, x2 = offset("x", a, 1), offset("x", b, 2)
    return [
        (own[step], 0, TOK),
        (ys[a], offset("y", a, 1), TOK),
        (xs[a], x1, TOK),
        (xs[b], x2, HALF),
        (xs[b], x2 + TOK, TOK),
        (ys[b], offset("y", b, 2), TOK),
        (xs[c], offset("x", c, 3), TOK),
        (ds[b], offset("d", b, 2), TOK),
        (ds[c], offset("d", c, 3), HALF),
    ]


def turn_kernel(pos, own, other, out):
    for i, block in enumerate(token_blocks(pos)):
        row = pl.multiple_of(block * HALF, HALF)
        for h, src in enumerate((own, other)):
            part = src[pl.ds(row, HALF), :].astype(F32)
            out[h * BLK : (h + 1) * BLK, i * HALF : (i + 1) * HALF] = part.T.astype(BF16)


def weight_kernel(where, _, turned, *refs):
    out = refs[-1]
    rhs = jnp.concatenate([r[at : at + n] for r, (at, n) in zip(refs, where)], axis=0)
    out[...] = jnp.dot(turned[...], rhs, preferred_element_type=F32)


def stack_kernel(_, away, own, out):
    out[:BLK] = away[...]
    out[BLK:] = own[...]


def join_kernel(_, mine, other, out):
    out[:, :BLK] = mine[...]
    out[:, BLK:] = other[...]


def attn_kernel(where, again, n_near, pos, *refs):
    near, refs = refs[:n_near], refs[n_near:]
    sums = refs[:2] if again else ()
    arrays = refs[len(sums) : -3]
    keep, send, w = refs[-3:]
    for i in range(len(where)):
        a, b = near[2 * i : 2 * i + 2]
        w[i * FEAT : (i + 1) * FEAT] = jnp.where(pos[3] == 0, a[...], b[...])
    blocks = token_blocks(pos)
    i = 0
    for p in range(9):
        n = where[0][p][2]
        lhs = jnp.concatenate(
            [arrays[step[p][0]][step[p][1] : step[p][1] + n] for step in where], axis=1
        )
        res = jnp.dot(lhs, w[...], preferred_element_type=F32)
        for h in range(n // HALF):
            rows = pl.ds(pl.multiple_of(blocks[i + h] * HALF, HALF), HALF)
            part = res[h * HALF : (h + 1) * HALF]
            for j, out in enumerate((keep, send)):
                block = part[:, j * BLK : (j + 1) * BLK]
                out[rows, :] = block + sums[j][rows, :] if again else block
        i += n // HALF


def add_kernel(_, a, b, out):
    out[...] = a[...] + b[...]


def add_split_kernel(_, a, b, out, away, own):
    total = a[...] + b[...]
    out[...] = total
    away[...] = total[:, :BLK]
    own[...] = total[:, BLK:]


def round_kernel(_, a, b, out):
    out[...] = (a[...] + b[...]).astype(BF16)


def early_kernel(_, s4, to_core, to_y):
    to_core[...] = s4[BLK:]
    to_y[...] = s4[:BLK, :BLK]


def late_kernel(_, away, early, same, cross):
    same[...] = away[:BLK] + early[:, :BLK]
    cross[...] = away[BLK:]


def cut_kernel(_, own, near):
    near[...] = own[BLK:]


def final_kernel(pos, r4, s4, early, same, cross, near, from_y, out):
    mine = pos[3] == 0

    @pl.when(mine)
    def _():
        out[...] = (r4[:BLK] + early[:, BLK:] + same[...]).T

    @pl.when(jnp.logical_not(mine))
    def _():
        out[...] = (s4[:BLK, BLK:] + from_y[...] + near[...] + cross[...]).T


def body(out_grad, attn_out, o_weight):
    yl, z, yh, x, c = (lax.axis_index(a) for a in AXES)
    pos = jnp.stack([z, yh, x, c, yl]).astype(jnp.int32)
    last = []

    def run(kernel, out_shape, vmem, *args, **more):
        args = lax.optimization_barrier((*args, *last))[: len(args)]
        out = call(kernel, out_shape, vmem, pos, *args, **more)
        last[:] = [out[-1] if isinstance(out, (tuple, list)) else out]
        return out

    def wait(*moved):
        last.extend(moved)

    def send(move, value):
        return move(lax.optimization_barrier((value, *last))[0] if last else value)

    own, xs, ys, ds = {}, {}, {}, {}

    def stage(k):
        parts = parts_of(k)
        args, outs = [], []
        if 1 in parts:
            args += [out_grad, other_grad]
        if k > 1:
            args += [xs[k - 1], ys[k - 1]] + ([ds[k - 1]] if k - 1 in ds else [])
        outs.append(shape(sum({1: 512, 2: 512, 3: 256}[p] for p in parts), FEAT))
        has_y, has_d = 2 in parts or 1 in parts, 2 in parts or 3 in parts
        if has_y:
            outs.append(shape(sum({1: 256, 2: 256, 3: 0}[p] for p in parts), FEAT))
        if has_d:
            outs.append(shape(sum({1: 0, 2: 256, 3: 128}[p] for p in parts), FEAT))
        if 1 in parts:
            outs.append(shape(TOK, FEAT))
        made = list(run(functools.partial(pack_kernel, k), tuple(outs), 8, *args))
        if 1 in parts:
            own[k - 1] = made[-1]
        xs[k] = send(along_x, made.pop(0))
        if has_y:
            ys[k] = send(across_other, made.pop(0))
        if has_d:
            ds[k] = send(core, made.pop(0))

    def weight(step):
        pieces = pieces_of(step, own, xs, ys, ds)
        kernel = functools.partial(weight_kernel, [p[1:] for p in pieces])
        return run(kernel, shape(2 * BLK, FEAT, F32), 8, turned, *[p[0] for p in pieces])

    def add(a, b):
        return run(add_kernel, shape(2 * BLK, FEAT, F32), 4, a, b)

    def attn(which, near, sums=()):
        steps = [pieces_of(s, own, xs, ys, ds) for s in which]
        near = sum(([near[4 - s], near[3 - s]] for s in which), [])
        arrays = []
        for piece in sum(steps, []):
            if all(piece[0] is not a for a in arrays):
                arrays.append(piece[0])
        where = [
            [([a is p[0] for a in arrays].index(True), p[1], p[2]) for p in step] for step in steps
        ]
        return run(
            functools.partial(attn_kernel, where, bool(sums), len(near)),
            (shape(16 * HALF, BLK, F32),) * 2, 16, *near, *sums, *arrays,
            scratch=[pltpu.VMEM((len(steps) * FEAT, 2 * BLK), BF16)],
        )

    other_grad = send(core, out_grad)
    w_away = send(across_lo, o_weight)
    other_attn = send(core, attn_out)

    stage(1)
    w_mine = run(stack_kernel, shape(FEAT, BLK), 4, w_away, o_weight)
    w_other = send(core, w_mine)
    turned = run(turn_kernel, shape(2 * BLK, 16 * HALF), 8, attn_out, other_attn)
    w0 = run(join_kernel, shape(FEAT, 2 * BLK), 4, w_mine, w_other)
    w1 = send(against_z, w0)
    wait(w1)
    stage(2)
    w2 = send(against_z, w1)
    wait(w2)
    stage(3)
    w3 = send(against_z, w2)
    wait(w3)
    stage(4)
    w4 = send(against_z_last, w3)
    g1 = weight(0)
    r1 = send(along_z, g1)
    stage(5)
    g2 = weight(1)
    s2 = add(r1, g2)
    r2 = send(along_z, s2)
    stage(6)
    g3 = weight(2)
    s3 = add(r2, g3)
    r3 = send(along_z, s3)
    near = (w0, w1, w2, w3, w4)
    sums = attn((1, 2), near)
    g4 = weight(3)
    half = shape(2 * BLK, BLK, F32)
    s4, s4_away, s4_own = run(
        add_split_kernel, (shape(2 * BLK, FEAT, F32), half, half), 4, r3, g4
    )
    r4_away, r4_own = along_z_last(s4_away), along_z_last(s4_own)
    to_core, to_y = run(early_kernel, (shape(BLK, FEAT, F32), shape(BLK, BLK, F32)), 4, s4)
    early = permute(to_core, ("c",), lambda i: (0,) if i == 1 else None)
    from_y = permute(to_y, ("yl", "c"), lambda i, j: (i + 1, j) if j == 1 else None)

    keep, out = attn((0, 3), near, sums)
    other = send(core, out)
    wait(early, from_y)
    same, cross = run(late_kernel, (shape(BLK, BLK, F32),) * 2, 4, r4_away, early)
    same = permute(same, ("yl", "c"), lambda i, j: (i + 1, 0) if j == 0 else None)
    cross = permute(cross, ("yl", "c"), lambda i, j: (i + 1, 1) if j == 0 else None)
    near = run(cut_kernel, shape(BLK, BLK, F32), 4, r4_own)
    near = permute(near, ("c",), lambda i: (1,) if i == 0 else None)
    attn_grad = run(round_kernel, shape(16 * HALF, BLK), 8, keep, other)
    weight_grad = run(
        final_kernel, shape(BLK, BLK, F32), 4, r4_own, s4, early, same, cross, near, from_y
    )
    return attn_grad, weight_grad


def solution(mesh):
    fine = Mesh(mesh.devices.reshape([SIZES[a] for a in AXES]), AXES)
    dp, tensor = ("yl", "z"), ("yh", "x", "c")
    return jax.shard_map(
        body,
        mesh=fine,
        in_specs=(P(dp + tensor, None), P(dp, tensor), P(dp, tensor)),
        out_specs=(P(dp, tensor), P(dp, tensor)),
        check_vma=False,
    )
```

time: 288 us -> 159 us (0.55)
  the two profiles are of different devices: /device:TPU:2 before, /device:TPU:1 now
where the time goes in v2:
time: 159 us
  waiting for transfers between devices  77.3 us (49%)
  starting transfers between devices  52.7 us (33%)
  Pallas kernels  26.3 us (17%)
    ppermute x35, waiting for transfers between devices, permute(): return lax.ppermute(value, axes if len(axes) > 1 else axes[0], pairs)  77.3 us
    ppermute x35, starting transfers between devices, permute(): return lax.ppermute(value, axes if len(axes) > 1 else axes[0], pairs)  52.7 us
    pallas_call x23, Pallas kernels, call(): pl.pallas_call(kernel, out_shape=out_shape, in_specs=[pl.BlockSpec(memory...  26.3 us
  transfers between devices with their start and end apart: 35, of which 16 were waited for; matrix products, arithmetic and copies ran while one was open for 0% of the time, Pallas kernels for 12%

profile of v2, /device:TPU:1, one launch (start us, length us, event | category | flops | bytes accessed | tf_op | source)
XLA Modules:
  0.0 158.6 jit_solution(142962441622125714)
XLA Ops:
  0.6 3.3 %collective-permute-start.1 = (bf16[128,4096]{1,0:T(8,128)(2,1)}, bf16[128,4096]{1,0:T(8,128)(2,1)S(1)}, u32[]{:S(2)}, u32[]{:S(2)}) collective-permute-start(bf16[128,4096]{1,0:T(8,128)(2,1)} %refs_0_.3), channel_id=1, source_target_pairs={{0,1},{1,0},{2,3},{3,2},{4,5},{5,4},{6,7},{7,6},{8,9},{9,8},{10,11... | collective-permute-start | bytes 3145736 | tf_op jit(solution)/shard_map/ppermute | solution.py:33
  4.1 2.3 %collective-permute-done.1.refs_1_ = bf16[128,4096]{1,0:T(8,128)(2,1)S(1)} collective-permute-done((bf16[128,4096]{1,0:T(8,128)(2,1)}, bf16[128,4096]{1,0:T(8,128)(2,1)S(1)}, u32[]{:S(2)}, u32[]{:S(2)}) %collective-permute-start.1) | collective-permute-done | bytes 1048608 | tf_op jit(solution)/shard_map/ppermute | solution.py:33
  6.5 1.2 copy-done
  7.7 0.6 shard_map.50
  8.3 0.6 collective-permute-done.away
  8.9 0.6 shard_map.51.mine
  9.5 1.3 collective-permute-start.2
  10.8 0.7 collective-permute-start.5
  11.6 1.2 shard_map.52.turned
  12.9 0.6 shard_map.53.refs_3_
  13.4 5.7 %collective-permute-start.4 = (bf16[512,512]{1,0:T(8,128)(2,1)S(1)}, bf16[512,512]{1,0:T(8,128)(2,1)S(1)}, u32[]{:S(2)}, u32[]{:S(2)}) collective-permute-start(bf16[512,512]{1,0:T(8,128)(2,1)S(1)} %shard_map.53.refs_3_), channel_id=1, source_target_pairs={{0,16},{1,113},{2,18},{3,115},{4,20},{5,117},{6,22},{7,119},{8,24}... | collective-permute-start | bytes 1572872 | tf_op jit(solution)/shard_map/ppermute | solution.py:33
  19.1 9.5 %collective-permute-done.6.refs_3_.refs_1_.refs_7_ = bf16[256,512]{1,0:T(8,128)(2,1)S(1)} collective-permute-done((bf16[256,512]{1,0:T(8,128)(2,1)S(1)}, bf16[256,512]{1,0:T(8,128)(2,1)S(1)}, u32[]{:S(2)}, u32[]{:S(2)}) %collective-permute-start.6) | collective-permute-done | bytes 262176 | tf_op jit(solution)/shard_map/ppermute | solution.py:33
  28.6 0.7 shard_map.54
  29.3 0.6 collective-permute-start.8
  29.9 0.7 collective-permute-start.7
  30.7 2.6 %collective-permute-start.10 = (bf16[256,512]{1,0:T(8,128)(2,1)S(1)}, bf16[256,512]{1,0:T(8,128)(2,1)S(1)}, u32[]{:S(2)}, u32[]{:S(2)}) collective-permute-start(bf16[256,512]{1,0:T(8,128)(2,1)S(1)} %get-tuple-element.209), channel_id=1, source_target_pairs={{0,1},{1,0},{2,3},{3,2},{4,5},{5,4},{6,7},{7,6},{8,9},{9,8},{10,11... | collective-permute-start | bytes 786440 | tf_op jit(solution)/shard_map/ppermute | solution.py:33
  33.3 1.2 collective-permute-done.10.refs_4_.refs_7_.refs_12_
  34.5 3.8 %collective-permute-done.7.refs_1_.refs_2_ = bf16[512,512]{1,0:T(8,128)(2,1)S(1)} collective-permute-done((bf16[512,512]{1,0:T(8,128)(2,1)S(1)}, bf16[512,512]{1,0:T(8,128)(2,1)S(1)}, u32[]{:S(2)}, u32[]{:S(2)}) %collective-permute-start.7) | collective-permute-done | bytes 524320 | tf_op jit(solution)/shard_map/ppermute | solution.py:33
  38.3 6.8 %collective-permute-done.9.refs_3_.refs_5_.refs_1_.refs_10_ = bf16[512,512]{1,0:T(8,128)(2,1)S(1)} collective-permute-done((bf16[512,512]{1,0:T(8,128)(2,1)S(1)}, bf16[512,512]{1,0:T(8,128)(2,1)S(1)}, u32[]{:S(2)}, u32[]{:S(2)}) %collective-permute-start.9) | collective-permute-done | bytes 524320 | tf_op jit(solution)/shard_map/ppermute | solution.py:33
  45.1 0.7 shard_map.55
  45.9 1.9 %collective-permute-start.12 = (bf16[1280,512]{1,0:T(8,128)(2,1)S(1)}, bf16[1280,512]{1,0:T(8,128)(2,1)S(1)}, u32[]{:S(2)}, u32[]{:S(2)}) collective-permute-start(bf16[1280,512]{1,0:T(8,128)(2,1)S(1)} %get-tuple-element.218), channel_id=1, source_target_pairs={{0,2},{1,7},{2,4},{3,1},{4,6},{5,3},{6,0},{7,5},{8,10},{9,15},{10,... | collective-permute-start | bytes 3932168 | tf_op jit(solution)/shard_map/ppermute | solution.py:33
  47.7 0.7 collective-permute-start.11
  48.4 3.1 %collective-permute-start.14 = (bf16[384,512]{1,0:T(8,128)(2,1)S(1)}, bf16[384,512]{1,0:T(8,128)(2,1)S(1)}, u32[]{:S(2)}, u32[]{:S(2)}) collective-permute-start(bf16[384,512]{1,0:T(8,128)(2,1)S(1)} %get-tuple-element.222), channel_id=1, source_target_pairs={{0,1},{1,0},{2,3},{3,2},{4,5},{5,4},{6,7},{7,6},{8,9},{9,8},{10,11... | collective-permute-start | bytes 1179656 | tf_op jit(solution)/shard_map/ppermute | solution.py:33
  51.5 1.3 collective-permute-done.14.refs_4_.refs_8_.refs_7_.refs_10_.refs_13_
  52.9 3.2 %collective-permute-done.11.refs_0_.refs_1_ = bf16[512,512]{1,0:T(8,128)(2,1)S(1)} collective-permute-done((bf16[512,512]{1,0:T(8,128)(2,1)S(1)}, bf16[512,512]{1,0:T(8,128)(2,1)S(1)}, u32[]{:S(2)}, u32[]{:S(2)}) %collective-permute-start.11) | collective-permute-done | bytes 524320 | tf_op jit(solution)/shard_map/ppermute | solution.py:33
  56.1 7.3 %collective-permute-done.13.refs_3_.refs_5_.refs_1_.refs_8_ = bf16[512,512]{1,0:T(8,128)(2,1)S(1)} collective-permute-done((bf16[512,512]{1,0:T(8,128)(2,1)S(1)}, bf16[512,512]{1,0:T(8,128)(2,1)S(1)}, u32[]{:S(2)}, u32[]{:S(2)}) %collective-permute-start.13) | collective-permute-done | bytes 524320 | tf_op jit(solution)/shard_map/ppermute | solution.py:33
  63.3 0.7 shard_map.56
  64.1 2.3 %collective-permute-start.16 = (bf16[1280,512]{1,0:T(8,128)(2,1)S(1)}, bf16[1280,512]{1,0:T(8,128)(2,1)S(1)}, u32[]{:S(2)}, u32[]{:S(2)}) collective-permute-start(bf16[1280,512]{1,0:T(8,128)(2,1)S(1)} %get-tuple-element.231), channel_id=1, source_target_pairs={{0,2},{1,7},{2,4},{3,1},{4,6},{5,3},{6,0},{7,5},{8,10},{9,15},{10,... | collective-permute-start | bytes 3932168 | tf_op jit(solution)/shard_map/ppermute | solution.py:33
  66.4 1.8 %shard_map.57 = f32[512,512]{1,0:T(8,128)S(1)} custom-call(s32[5]{0:T(128)S(1)} %stack.23.pos._, bf16[512,2048]{1,0:T(8,128)(2,1)S(1)} %shard_map.52.turned, bf16[256,512]{1,0:T(8,128)(2,1)S(1)} %get-tuple-element.328.refs_0_.refs_6_, bf16[256,512]{1,0:T(8,128)(2,1)S(1)} %collective-permute-done.6.refs_3_.refs_1_.refs_7_, ...), custom_call_target="tpu_custom_call" | custom-call | bytes 65536 | tf_op jit(solution)/shard_map/pallas_call | solution.py:77
  68.5 3.2 %collective-permute-start.18 = (bf16[512,512]{1,0:T(8,128)(2,1)S(1)}, bf16[512,512]{1,0:T(8,128)(2,1)S(1)}, u32[]{:S(2)}, u32[]{:S(2)}) collective-permute-start(bf16[512,512]{1,0:T(8,128)(2,1)S(1)} %get-tuple-element.235), channel_id=1, source_target_pairs={{0,9},{1,8},{2,11},{3,10},{4,13},{5,12},{6,15},{7,14},{8,1},{9,0},... | collective-permute-start | bytes 1572872 | tf_op jit(solution)/shard_map/ppermute | solution.py:33
  71.7 1.7 %collective-permute-done.17.refs_2_.refs_8_.refs_7_.refs_11_ = bf16[384,512]{1,0:T(8,128)(2,1)S(1)} collective-permute-done((bf16[384,512]{1,0:T(8,128)(2,1)S(1)}, bf16[384,512]{1,0:T(8,128)(2,1)S(1)}, u32[]{:S(2)}, u32[]{:S(2)}) %collective-permute-start.17) | collective-permute-done | bytes 393248 | tf_op jit(solution)/shard_map/ppermute | solution.py:33
  73.5 9.4 %collective-permute-done.18.refs_1_.refs_5_.refs_13_.refs_15_ = bf16[512,512]{1,0:T(8,128)(2,1)S(1)} collective-permute-done((bf16[512,512]{1,0:T(8,128)(2,1)S(1)}, bf16[512,512]{1,0:T(8,128)(2,1)S(1)}, u32[]{:S(2)}, u32[]{:S(2)}) %collective-permute-start.18) | collective-permute-done | bytes 524320 | tf_op jit(solution)/shard_map/ppermute | solution.py:33
  82.8 0.6 shard_map.58
  83.5 1.8 %shard_map.59.b = f32[512,512]{1,0:T(8,128)S(1)} custom-call(s32[5]{0:T(128)S(1)} %stack.23.pos._, bf16[512,2048]{1,0:T(8,128)(2,1)S(1)} %shard_map.52.turned, bf16[256,512]{1,0:T(8,128)(2,1)S(1)} %get-tuple-element.289.refs_0_.refs_4_, bf16[512,512]{1,0:T(8,128)(2,1)S(1)} %collective-permute-done.9.refs_3_.refs_5_.refs_1_.refs_10_, ...), custom_call_target="tpu_custom_call" | custom-call | bytes 65536 | tf_op jit(solution)/shard_map/pallas_call | solution.py:77
  85.3 0.6 shard_map.60
  85.9 2.1 %collective-permute-start.22 = (f32[512,512]{1,0:T(8,128)S(1)}, f32[512,512]{1,0:T(8,128)S(1)}, u32[]{:S(2)}, u32[]{:S(2)}) collective-permute-start(f32[512,512]{1,0:T(8,128)S(1)} %shard_map.60), channel_id=1, source_target_pairs={{0,112},{1,17},{2,114},{3,19},{4,116},{5,21},{6,118},{7,23},{8,120... | collective-permute-start | bytes 3145736 | tf_op jit(solution)/shard_map/ppermute | solution.py:33
  88.4 2.7 %collective-permute-start.20 = (bf16[384,512]{1,0:T(8,128)(2,1)S(1)}, bf16[384,512]{1,0:T(8,128)(2,1)S(1)}, u32[]{:S(2)}, u32[]{:S(2)}) collective-permute-start(bf16[384,512]{1,0:T(8,128)(2,1)S(1)} %get-tuple-element.252), channel_id=1, source_target_pairs={{0,1},{1,0},{2,3},{3,2},{4,5},{5,4},{6,7},{7,6},{8,9},{9,8},{10,11... | collective-permute-start | bytes 1179656 | tf_op jit(solution)/shard_map/ppermute | solution.py:33
  91.0 1.4 collective-permute-start.23
  92.5 8.0 %collective-permute-done.23.refs_1_.refs_5_.refs_18_ = bf16[256,512]{1,0:T(8,128)(2,1)S(1)} collective-permute-done((bf16[256,512]{1,0:T(8,128)(2,1)S(1)}, bf16[256,512]{1,0:T(8,128)(2,1)S(1)}, u32[]{:S(2)}, u32[]{:S(2)}) %collective-permute-start.23) | collective-permute-done | bytes 262176 | tf_op jit(solution)/shard_map/ppermute | solution.py:33
  100.4 0.6 shard_map.61
  101.0 1.8 %shard_map.62.b = f32[512,512]{1,0:T(8,128)S(1)} custom-call(s32[5]{0:T(128)S(1)} %stack.23.pos._, bf16[512,2048]{1,0:T(8,128)(2,1)S(1)} %shard_map.52.turned, bf16[256,512]{1,0:T(8,128)(2,1)S(1)} %get-tuple-element.297.refs_0_.refs_12_, bf16[512,512]{1,0:T(8,128)(2,1)S(1)} %collective-permute-done.13.refs_3_.refs_5_.refs_1_.refs_8_, ...), custom_call_target="tpu_custom_call" | custom-call | bytes 65536 | tf_op jit(solution)/shard_map/pallas_call | solution.py:77
  102.8 0.6 shard_map.63
  103.9 0.7 collective-permute-start.15
  104.6 2.7 %collective-permute-start.24 = (bf16[256,512]{1,0:T(8,128)(2,1)S(1)}, bf16[256,512]{1,0:T(8,128)(2,1)S(1)}, u32[]{:S(2)}, u32[]{:S(2)}) collective-permute-start(bf16[256,512]{1,0:T(8,128)(2,1)S(1)} %get-tuple-element.303), channel_id=1, source_target_pairs={{0,2},{1,7},{2,4},{3,1},{4,6},{5,3},{6,0},{7,5},{8,10},{9,15},{10,... | collective-permute-start | bytes 786440 | tf_op jit(solution)/shard_map/ppermute | solution.py:33
  107.3 4.3 %collective-permute-start.25 = (bf16[128,512]{1,0:T(8,128)(2,1)S(1)}, bf16[128,512]{1,0:T(8,128)(2,1)S(1)}, u32[]{:S(2)}, u32[]{:S(2)}) collective-permute-start(bf16[128,512]{1,0:T(8,128)(2,1)S(1)} %get-tuple-element.304), channel_id=1, source_target_pairs={{0,1},{1,0},{2,3},{3,2},{4,5},{5,4},{6,7},{7,6},{8,9},{9,8},{10,11... | collective-permute-start | bytes 393224 | tf_op jit(solution)/shard_map/ppermute | solution.py:33
  111.6 2.9 %shard_map.64 = (f32[2048,256]{1,0:T(8,128)S(1)}, f32[2048,256]{1,0:T(8,128)S(1)}) custom-call(s32[5]{0:T(128)S(1)} %stack.23.pos._, bf16[512,512]{1,0:T(8,128)(2,1)S(1)} %collective-permute-done.11.refs_0_.refs_1_, bf16[512,512]{1,0:T(8,128)(2,1)S(1)} %collective-permute-done.7.refs_1_.refs_2_, bf16[512,512]{1,0:T(8,128)(2,1)S(1)} %collective-permute-done.7.refs_1_.refs_2_, ...), custom_call_target="tpu_custom_call" | custom-call | bytes 65536 | tf_op jit(solution)/shard_map/pallas_call | solution.py:77
  114.6 1.8 %shard_map.65.b = f32[512,512]{1,0:T(8,128)S(1)} custom-call(s32[5]{0:T(128)S(1)} %stack.23.pos._, bf16[512,2048]{1,0:T(8,128)(2,1)S(1)} %shard_map.52.turned, bf16[256,512]{1,0:T(8,128)(2,1)S(1)} %get-tuple-element.336.refs_0_.refs_14_, bf16[512,512]{1,0:T(8,128)(2,1)S(1)} %collective-permute-done.18.refs_1_.refs_5_.refs_13_.refs_15_, ...), custom_call_target="tpu_custom_call" | custom-call | bytes 65536 | tf_op jit(solution)/shard_map/pallas_call | solution.py:77
  116.4 6.9 %collective-permute-done.26.a = f32[512,512]{1,0:T(8,128)S(1)} collective-permute-done((f32[512,512]{1,0:T(8,128)S(1)}, f32[512,512]{1,0:T(8,128)S(1)}, u32[]{:S(2)}, u32[]{:S(2)}) %collective-permute-start.26) | collective-permute-done | bytes 1048608 | tf_op jit(solution)/shard_map/ppermute | solution.py:33
  123.3 0.7 shard_map.66
  124.0 0.6 shard_map.67
  124.6 3.0 %shard_map.68 = (f32[2048,256]{1,0:T(8,128)S(1)}, f32[2048,256]{1,0:T(8,128)S(1)}) custom-call(s32[5]{0:T(128)S(1)} %stack.23.pos._, bf16[512,512]{1,0:T(8,128)(2,1)S(1)} %collective-permute-done.15.refs_0_, bf16[512,512]{1,0:T(8,128)(2,1)S(1)} %collective-permute-done.11.refs_0_.refs_1_, bf16[512,512]{1,0:T(8,128)(2,1)S(1)} %collective-permute-done.4.refs_3_.refs_2_, ...), custom_call_target="tpu_custom_call" | custom-call | bytes 65536 | tf_op jit(solution)/shard_map/pallas_call | solution.py:77
  127.8 0.7 collective-permute-start.29
  128.5 4.6 %collective-permute-start.30 = (f32[256,512]{1,0:T(8,128)S(1)}, f32[256,512]{1,0:T(8,128)S(1)}, u32[]{:S(2)}, u32[]{:S(2)}) collective-permute-start(f32[256,512]{1,0:T(8,128)S(1)} %get-tuple-element.348), channel_id=1, source_target_pairs={{1,0},{3,2},{5,4},{7,6},{9,8},{11,10},{13,12},{15,14},{17,16},{19,... | collective-permute-start | bytes 1572872 | tf_op jit(solution)/shard_map/ppermute | solution.py:33
  133.1 0.7 collective-permute-start.28
  133.8 1.9 %collective-permute-start.31 = (f32[256,256]{1,0:T(8,128)S(1)}, f32[256,256]{1,0:T(8,128)S(1)}, u32[]{:S(2)}, u32[]{:S(2)}) collective-permute-start(f32[256,256]{1,0:T(8,128)S(1)} %get-tuple-element.321), channel_id=1, source_target_pairs={{1,129},{129,1},{3,131},{131,3},{5,133},{133,5},{7,135},{135,7},{9... | collective-permute-start | bytes 786440 | tf_op jit(solution)/shard_map/ppermute | solution.py:33
  135.7 5.5 %collective-permute-done.31.from_y = f32[256,256]{1,0:T(8,128)S(1)} collective-permute-done((f32[256,256]{1,0:T(8,128)S(1)}, f32[256,256]{1,0:T(8,128)S(1)}, u32[]{:S(2)}, u32[]{:S(2)}) %collective-permute-start.31) | collective-permute-done | bytes 262176 | tf_op jit(solution)/shard_map/ppermute | solution.py:33
  141.2 0.6 shard_map.69
  141.8 0.6 shard_map.70
  142.4 1.3 collective-permute-start.34
  143.7 0.7 collective-permute-start.32
  144.4 1.3 collective-permute-start.33
  145.7 1.7 %shard_map.71 = bf16[2048,256]{1,0:T(8,128)(2,1)} custom-call(s32[5]{0:T(128)S(1)} %stack.23.pos._, f32[2048,256]{1,0:T(8,128)S(1)} %get-tuple-element.353.a, f32[2048,256]{1,0:T(8,128)S(1)} %collective-permute-done.27.b), custom_call_target="tpu_custom_call" | custom-call | bytes 65536 | tf_op jit(solution)/shard_map/pallas_call | solution.py:77
  147.8 9.4 %collective-permute-done.33.cross = f32[256,256]{1,0:T(8,128)S(1)} collective-permute-done((f32[256,256]{1,0:T(8,128)S(1)}, f32[256,256]{1,0:T(8,128)S(1)}, u32[]{:S(2)}, u32[]{:S(2)}) %collective-permute-start.33) | collective-permute-done | bytes 262176 | tf_op jit(solution)/shard_map/ppermute | solution.py:33
  157.2 1.4 shard_map.72
  (38 shorter events, 2.0 us)
Async XLA Ops:
  0.6 5.8 %collective-permute-start.1 = (bf16[128,4096]{1,0:T(8,128)(2,1)}, bf16[128,4096]{1,0:T(8,128)(2,1)S(1)}, u32[]{:S(2)}, u32[]{:S(2)}) collective-permute-start(bf16[128,4096]{1,0:T(8,128)(2,1)} %refs_0_.3), channel_id=1, source_target_pairs={{0,1},{1,0},{2,3},{3,2},{4,5},{5,4},{6,7},{7,6},{8,9},{9,8},{10,11... | collective-permute-start | bytes 3145736 | tf_op jit(solution)/shard_map/ppermute | solution.py:33
  4.0 6.9 %collective-permute-start.3 = (bf16[2048,256]{1,0:T(8,128)(2,1)}, bf16[2048,256]{1,0:T(8,128)(2,1)S(1)}, u32[]{:S(2)}, u32[]{:S(2)}) collective-permute-start(bf16[2048,256]{1,0:T(8,128)(2,1)} %own.1), channel_id=1, source_target_pairs={{0,1},{1,0},{2,3},{3,2},{4,5},{5,4},{6,7},{7,6},{8,9},{9,8},{10,11... | collective-permute-start | bytes 3145736 | tf_op jit(solution)/shard_map/ppermute | solution.py:33
  4.1 4.9 %collective-permute-start = (bf16[256,256]{1,0:T(8,128)(2,1)}, bf16[256,256]{1,0:T(8,128)(2,1)S(1)}, u32[]{:S(2)}, u32[]{:S(2)}) collective-permute-start(bf16[256,256]{1,0:T(8,128)(2,1)} %own), channel_id=1, source_target_pairs={{0,128},{128,0},{1,129},{129,1},{2,130},{130,2},{3,131},{131,3},{4... | collective-permute-start | bytes 393224 | tf_op jit(solution)/shard_map/ppermute | solution.py:33
  6.5 1.2 copy-start
  7.7 1.3 copy-start.3
  7.7 3.9 %copy-start.2 = (bf16[2048,256]{1,0:T(8,128)(2,1)S(1)}, bf16[2048,256]{1,0:T(8,128)(2,1)}, u32[]{:S(2)}) copy-start(bf16[2048,256]{1,0:T(8,128)(2,1)} %own.1) | copy-start | bytes 3145732
  9.5 3.3 %collective-permute-start.2 = (bf16[512,256]{1,0:T(8,128)(2,1)S(1)}, bf16[512,256]{1,0:T(8,128)(2,1)S(1)}, u32[]{:S(2)}, u32[]{:S(2)}) collective-permute-start(bf16[512,256]{1,0:T(8,128)(2,1)S(1)} %shard_map.51.mine), channel_id=1, source_target_pairs={{0,1},{1,0},{2,3},{3,2},{4,5},{5,4},{6,7},{7,6},{8,9},{9,8},{10,11... | collective-permute-start | bytes 786440 | tf_op jit(solution)/shard_map/ppermute | solution.py:33
  10.8 17.7 %copy-start.1 = (bf16[128,4096]{1,0:T(8,128)(2,1)S(1)}, bf16[128,4096]{1,0:T(8,128)(2,1)}, u32[]{:S(2)}) copy-start(bf16[128,4096]{1,0:T(8,128)(2,1)} %refs_0_.3) | copy-start | bytes 3145732
  10.8 17.7 %collective-permute-start.5 = (bf16[512,512]{1,0:T(8,128)(2,1)S(1)}, bf16[512,512]{1,0:T(8,128)(2,1)S(1)}, u32[]{:S(2)}, u32[]{:S(2)}) collective-permute-start(bf16[512,512]{1,0:T(8,128)(2,1)S(1)} %get-tuple-element.195), channel_id=1, source_target_pairs={{0,2},{1,7},{2,4},{3,1},{4,6},{5,3},{6,0},{7,5},{8,10},{9,15},{10,... | collective-permute-start | bytes 1572872 | tf_op jit(solution)/shard_map/ppermute | solution.py:33
  13.4 15.1 %collective-permute-start.4 = (bf16[512,512]{1,0:T(8,128)(2,1)S(1)}, bf16[512,512]{1,0:T(8,128)(2,1)S(1)}, u32[]{:S(2)}, u32[]{:S(2)}) collective-permute-start(bf16[512,512]{1,0:T(8,128)(2,1)S(1)} %shard_map.53.refs_3_), channel_id=1, source_target_pairs={{0,16},{1,113},{2,18},{3,115},{4,20},{5,117},{6,22},{7,119},{8,24}... | collective-permute-start | bytes 1572872 | tf_op jit(solution)/shard_map/ppermute | solution.py:33
  19.1 9.5 %collective-permute-start.6 = (bf16[256,512]{1,0:T(8,128)(2,1)S(1)}, bf16[256,512]{1,0:T(8,128)(2,1)S(1)}, u32[]{:S(2)}, u32[]{:S(2)}) collective-permute-start(bf16[256,512]{1,0:T(8,128)(2,1)S(1)} %get-tuple-element.197), channel_id=1, source_target_pairs={{0,9},{1,8},{2,11},{3,10},{4,13},{5,12},{6,15},{7,14},{8,1},{9,0},... | collective-permute-start | bytes 786440 | tf_op jit(solution)/shard_map/ppermute | solution.py:33
  29.3 15.8 %collective-permute-start.8 = (bf16[1024,512]{1,0:T(8,128)(2,1)S(1)}, bf16[1024,512]{1,0:T(8,128)(2,1)S(1)}, u32[]{:S(2)}, u32[]{:S(2)}) collective-permute-start(bf16[1024,512]{1,0:T(8,128)(2,1)S(1)} %get-tuple-element.205), channel_id=1, source_target_pairs={{0,2},{1,7},{2,4},{3,1},{4,6},{5,3},{6,0},{7,5},{8,10},{9,15},{10,... | collective-permute-start | bytes 3145736 | tf_op jit(solution)/shard_map/ppermute | solution.py:33
  29.9 8.3 %collective-permute-start.7 = (bf16[512,512]{1,0:T(8,128)(2,1)S(1)}, bf16[512,512]{1,0:T(8,128)(2,1)S(1)}, u32[]{:S(2)}, u32[]{:S(2)}) collective-permute-start(bf16[512,512]{1,0:T(8,128)(2,1)S(1)} %collective-permute-done.4.refs_3_.refs_2_), channel_id=1, source_target_pairs={{0,16},{1,113},{2,18},{3,115},{4,20},{5,117},{6,22},{7,119},{8,24}... | collective-permute-start | bytes 1572872 | tf_op jit(solution)/shard_map/ppermute | solution.py:33
  30.7 14.4 %collective-permute-start.9 = (bf16[512,512]{1,0:T(8,128)(2,1)S(1)}, bf16[512,512]{1,0:T(8,128)(2,1)S(1)}, u32[]{:S(2)}, u32[]{:S(2)}) collective-permute-start(bf16[512,512]{1,0:T(8,128)(2,1)S(1)} %get-tuple-element.207), channel_id=1, source_target_pairs={{0,9},{1,8},{2,11},{3,10},{4,13},{5,12},{6,15},{7,14},{8,1},{9,0},... | collective-permute-start | bytes 1572872 | tf_op jit(solution)/shard_map/ppermute | solution.py:33
  30.7 3.7 %collective-permute-start.10 = (bf16[256,512]{1,0:T(8,128)(2,1)S(1)}, bf16[256,512]{1,0:T(8,128)(2,1)S(1)}, u32[]{:S(2)}, u32[]{:S(2)}) collective-permute-start(bf16[256,512]{1,0:T(8,128)(2,1)S(1)} %get-tuple-element.209), channel_id=1, source_target_pairs={{0,1},{1,0},{2,3},{3,2},{4,5},{5,4},{6,7},{7,6},{8,9},{9,8},{10,11... | collective-permute-start | bytes 786440 | tf_op jit(solution)/shard_map/ppermute | solution.py:33
  45.9 17.5 %collective-permute-start.12 = (bf16[1280,512]{1,0:T(8,128)(2,1)S(1)}, bf16[1280,512]{1,0:T(8,128)(2,1)S(1)}, u32[]{:S(2)}, u32[]{:S(2)}) collective-permute-start(bf16[1280,512]{1,0:T(8,128)(2,1)S(1)} %get-tuple-element.218), channel_id=1, source_target_pairs={{0,2},{1,7},{2,4},{3,1},{4,6},{5,3},{6,0},{7,5},{8,10},{9,15},{10,... | collective-permute-start | bytes 3932168 | tf_op jit(solution)/shard_map/ppermute | solution.py:33
  47.7 8.3 %collective-permute-start.11 = (bf16[512,512]{1,0:T(8,128)(2,1)S(1)}, bf16[512,512]{1,0:T(8,128)(2,1)S(1)}, u32[]{:S(2)}, u32[]{:S(2)}) collective-permute-start(bf16[512,512]{1,0:T(8,128)(2,1)S(1)} %collective-permute-done.7.refs_1_.refs_2_), channel_id=1, source_target_pairs={{0,16},{1,113},{2,18},{3,115},{4,20},{5,117},{6,22},{7,119},{8,24}... | collective-permute-start | bytes 1572872 | tf_op jit(solution)/shard_map/ppermute | solution.py:33
  48.4 14.9 %collective-permute-start.13 = (bf16[512,512]{1,0:T(8,128)(2,1)S(1)}, bf16[512,512]{1,0:T(8,128)(2,1)S(1)}, u32[]{:S(2)}, u32[]{:S(2)}) collective-permute-start(bf16[512,512]{1,0:T(8,128)(2,1)S(1)} %get-tuple-element.220), channel_id=1, source_target_pairs={{0,9},{1,8},{2,11},{3,10},{4,13},{5,12},{6,15},{7,14},{8,1},{9,0},... | collective-permute-start | bytes 1572872 | tf_op jit(solution)/shard_map/ppermute | solution.py:33
  48.4 4.5 %collective-permute-start.14 = (bf16[384,512]{1,0:T(8,128)(2,1)S(1)}, bf16[384,512]{1,0:T(8,128)(2,1)S(1)}, u32[]{:S(2)}, u32[]{:S(2)}) collective-permute-start(bf16[384,512]{1,0:T(8,128)(2,1)S(1)} %get-tuple-element.222), channel_id=1, source_target_pairs={{0,1},{1,0},{2,3},{3,2},{4,5},{5,4},{6,7},{7,6},{8,9},{9,8},{10,11... | collective-permute-start | bytes 1179656 | tf_op jit(solution)/shard_map/ppermute | solution.py:33
  64.1 18.7 %collective-permute-start.16 = (bf16[1280,512]{1,0:T(8,128)(2,1)S(1)}, bf16[1280,512]{1,0:T(8,128)(2,1)S(1)}, u32[]{:S(2)}, u32[]{:S(2)}) collective-permute-start(bf16[1280,512]{1,0:T(8,128)(2,1)S(1)} %get-tuple-element.231), channel_id=1, source_target_pairs={{0,2},{1,7},{2,4},{3,1},{4,6},{5,3},{6,0},{7,5},{8,10},{9,15},{10,... | collective-permute-start | bytes 3932168 | tf_op jit(solution)/shard_map/ppermute | solution.py:33
  68.2 17.1 %collective-permute-start.21 = (f32[512,512]{1,0:T(8,128)S(1)}, f32[512,512]{1,0:T(8,128)S(1)}, u32[]{:S(2)}, u32[]{:S(2)}) collective-permute-start(f32[512,512]{1,0:T(8,128)S(1)} %shard_map.57), channel_id=1, source_target_pairs={{0,112},{1,17},{2,114},{3,19},{4,116},{5,21},{6,118},{7,23},{8,120... | collective-permute-start | bytes 3145736 | tf_op jit(solution)/shard_map/ppermute | solution.py:33
  68.5 14.3 %collective-permute-start.18 = (bf16[512,512]{1,0:T(8,128)(2,1)S(1)}, bf16[512,512]{1,0:T(8,128)(2,1)S(1)}, u32[]{:S(2)}, u32[]{:S(2)}) collective-permute-start(bf16[512,512]{1,0:T(8,128)(2,1)S(1)} %get-tuple-element.235), channel_id=1, source_target_pairs={{0,9},{1,8},{2,11},{3,10},{4,13},{5,12},{6,15},{7,14},{8,1},{9,0},... | collective-permute-start | bytes 1572872 | tf_op jit(solution)/shard_map/ppermute | solution.py:33
  71.7 1.7 %collective-permute-start.17 = (bf16[384,512]{1,0:T(8,128)(2,1)S(1)}, bf16[384,512]{1,0:T(8,128)(2,1)S(1)}, u32[]{:S(2)}, u32[]{:S(2)}) collective-permute-start(bf16[384,512]{1,0:T(8,128)(2,1)S(1)} %get-tuple-element.233), channel_id=1, source_target_pairs={{0,1},{1,0},{2,3},{3,2},{4,5},{5,4},{6,7},{7,6},{8,9},{9,8},{10,11... | collective-permute-start | bytes 1179656 | tf_op jit(solution)/shard_map/ppermute | solution.py:33
  85.9 16.9 %collective-permute-start.22 = (f32[512,512]{1,0:T(8,128)S(1)}, f32[512,512]{1,0:T(8,128)S(1)}, u32[]{:S(2)}, u32[]{:S(2)}) collective-permute-start(f32[512,512]{1,0:T(8,128)S(1)} %shard_map.60), channel_id=1, source_target_pairs={{0,112},{1,17},{2,114},{3,19},{4,116},{5,21},{6,118},{7,23},{8,120... | collective-permute-start | bytes 3145736 | tf_op jit(solution)/shard_map/ppermute | solution.py:33
  88.0 12.4 %collective-permute-start.19 = (bf16[768,512]{1,0:T(8,128)(2,1)S(1)}, bf16[768,512]{1,0:T(8,128)(2,1)S(1)}, u32[]{:S(2)}, u32[]{:S(2)}) collective-permute-start(bf16[768,512]{1,0:T(8,128)(2,1)S(1)} %get-tuple-element.251), channel_id=1, source_target_pairs={{0,2},{1,7},{2,4},{3,1},{4,6},{5,3},{6,0},{7,5},{8,10},{9,15},{10,... | collective-permute-start | bytes 2359304 | tf_op jit(solution)/shard_map/ppermute | solution.py:33
  88.4 12.1 %collective-permute-start.20 = (bf16[384,512]{1,0:T(8,128)(2,1)S(1)}, bf16[384,512]{1,0:T(8,128)(2,1)S(1)}, u32[]{:S(2)}, u32[]{:S(2)}) collective-permute-start(bf16[384,512]{1,0:T(8,128)(2,1)S(1)} %get-tuple-element.252), channel_id=1, source_target_pairs={{0,1},{1,0},{2,3},{3,2},{4,5},{5,4},{6,7},{7,6},{8,9},{9,8},{10,11... | collective-permute-start | bytes 1179656 | tf_op jit(solution)/shard_map/ppermute | solution.py:33
  91.0 9.4 %collective-permute-start.23 = (bf16[256,512]{1,0:T(8,128)(2,1)S(1)}, bf16[256,512]{1,0:T(8,128)(2,1)S(1)}, u32[]{:S(2)}, u32[]{:S(2)}) collective-permute-start(bf16[256,512]{1,0:T(8,128)(2,1)S(1)} %get-tuple-element.268), channel_id=1, source_target_pairs={{0,9},{1,8},{2,11},{3,10},{4,13},{5,12},{6,15},{7,14},{8,1},{9,0},... | collective-permute-start | bytes 786440 | tf_op jit(solution)/shard_map/ppermute | solution.py:33
  103.5 19.9 %collective-permute-start.26 = (f32[512,512]{1,0:T(8,128)S(1)}, f32[512,512]{1,0:T(8,128)S(1)}, u32[]{:S(2)}, u32[]{:S(2)}) collective-permute-start(f32[512,512]{1,0:T(8,128)S(1)} %shard_map.63), channel_id=1, source_target_pairs={{0,112},{1,17},{2,114},{3,19},{4,116},{5,21},{6,118},{7,23},{8,120... | collective-permute-start | bytes 3145736 | tf_op jit(solution)/shard_map/ppermute | solution.py:33
  103.9 20.7 %collective-permute-start.15 = (bf16[512,512]{1,0:T(8,128)(2,1)S(1)}, bf16[512,512]{1,0:T(8,128)(2,1)S(1)}, u32[]{:S(2)}, u32[]{:S(2)}) collective-permute-start(bf16[512,512]{1,0:T(8,128)(2,1)S(1)} %collective-permute-done.11.refs_0_.refs_1_), channel_id=1, source_target_pairs={{0,16},{2,18},{4,20},{6,22},{8,24},{10,26},{12,28},{14,30},{16,32}... | collective-permute-start | bytes 1572872 | tf_op jit(solution)/shard_map/ppermute | solution.py:33
  104.6 10.0 %collective-permute-start.24 = (bf16[256,512]{1,0:T(8,128)(2,1)S(1)}, bf16[256,512]{1,0:T(8,128)(2,1)S(1)}, u32[]{:S(2)}, u32[]{:S(2)}) collective-permute-start(bf16[256,512]{1,0:T(8,128)(2,1)S(1)} %get-tuple-element.303), channel_id=1, source_target_pairs={{0,2},{1,7},{2,4},{3,1},{4,6},{5,3},{6,0},{7,5},{8,10},{9,15},{10,... | collective-permute-start | bytes 786440 | tf_op jit(solution)/shard_map/ppermute | solution.py:33
  107.3 7.3 %collective-permute-start.25 = (bf16[128,512]{1,0:T(8,128)(2,1)S(1)}, bf16[128,512]{1,0:T(8,128)(2,1)S(1)}, u32[]{:S(2)}, u32[]{:S(2)}) collective-permute-start(bf16[128,512]{1,0:T(8,128)(2,1)S(1)} %get-tuple-element.304), channel_id=1, source_target_pairs={{0,1},{1,0},{2,3},{3,2},{4,5},{5,4},{6,7},{7,6},{8,9},{9,8},{10,11... | collective-permute-start | bytes 393224 | tf_op jit(solution)/shard_map/ppermute | solution.py:33
  127.6 18.1 %collective-permute-start.27 = (f32[2048,256]{1,0:T(8,128)S(1)}, f32[2048,256]{1,0:T(8,128)S(1)}, u32[]{:S(2)}, u32[]{:S(2)}) collective-permute-start(f32[2048,256]{1,0:T(8,128)S(1)} %get-tuple-element.346), channel_id=1, source_target_pairs={{0,1},{1,0},{2,3},{3,2},{4,5},{5,4},{6,7},{7,6},{8,9},{9,8},{10,11... | collective-permute-start | bytes 6291464 | tf_op jit(solution)/shard_map/ppermute | solution.py:33
  127.8 13.4 %collective-permute-start.29 = (f32[512,256]{1,0:T(8,128)S(1)}, f32[512,256]{1,0:T(8,128)S(1)}, u32[]{:S(2)}, u32[]{:S(2)}) collective-permute-start(f32[512,256]{1,0:T(8,128)S(1)} %get-tuple-element.347), channel_id=1, source_target_pairs={{0,112},{2,114},{4,116},{6,118},{8,120},{10,122},{12,124},{14,126}... | collective-permute-start | bytes 1572872 | tf_op jit(solution)/shard_map/ppermute | solution.py:33
  128.5 12.7 %collective-permute-start.30 = (f32[256,512]{1,0:T(8,128)S(1)}, f32[256,512]{1,0:T(8,128)S(1)}, u32[]{:S(2)}, u32[]{:S(2)}) collective-permute-start(f32[256,512]{1,0:T(8,128)S(1)} %get-tuple-element.348), channel_id=1, source_target_pairs={{1,0},{3,2},{5,4},{7,6},{9,8},{11,10},{13,12},{15,14},{17,16},{19,... | collective-permute-start | bytes 1572872 | tf_op jit(solution)/shard_map/ppermute | solution.py:33
  133.1 8.7 %collective-permute-start.28 = (f32[512,256]{1,0:T(8,128)S(1)}, f32[512,256]{1,0:T(8,128)S(1)}, u32[]{:S(2)}, u32[]{:S(2)}) collective-permute-start(f32[512,256]{1,0:T(8,128)S(1)} %get-tuple-element.319), channel_id=1, source_target_pairs={{0,112},{2,114},{4,116},{6,118},{8,120},{10,122},{12,124},{14,126}... | collective-permute-start | bytes 1572872 | tf_op jit(solution)/shard_map/ppermute | solution.py:33
  133.8 7.4 %collective-permute-start.31 = (f32[256,256]{1,0:T(8,128)S(1)}, f32[256,256]{1,0:T(8,128)S(1)}, u32[]{:S(2)}, u32[]{:S(2)}) collective-permute-start(f32[256,256]{1,0:T(8,128)S(1)} %get-tuple-element.321), channel_id=1, source_target_pairs={{1,129},{129,1},{3,131},{131,3},{5,133},{133,5},{7,135},{135,7},{9... | collective-permute-start | bytes 786440 | tf_op jit(solution)/shard_map/ppermute | solution.py:33
  142.4 5.4 %collective-permute-start.34 = (f32[256,256]{1,0:T(8,128)S(1)}, f32[256,256]{1,0:T(8,128)S(1)}, u32[]{:S(2)}, u32[]{:S(2)}) collective-permute-start(f32[256,256]{1,0:T(8,128)S(1)} %shard_map.70), channel_id=1, source_target_pairs={{0,1},{2,3},{4,5},{6,7},{8,9},{10,11},{12,13},{14,15},{16,17},{18,... | collective-permute-start | bytes 786440 | tf_op jit(solution)/shard_map/ppermute | solution.py:33
  143.7 4.1 %collective-permute-start.32 = (f32[256,256]{1,0:T(8,128)S(1)}, f32[256,256]{1,0:T(8,128)S(1)}, u32[]{:S(2)}, u32[]{:S(2)}) collective-permute-start(f32[256,256]{1,0:T(8,128)S(1)} %get-tuple-element.355), channel_id=1, source_target_pairs={{0,128},{128,0},{2,130},{130,2},{4,132},{132,4},{6,134},{134,6},{8... | collective-permute-start | bytes 786440 | tf_op jit(solution)/shard_map/ppermute | solution.py:33
  144.4 12.8 %collective-permute-start.33 = (f32[256,256]{1,0:T(8,128)S(1)}, f32[256,256]{1,0:T(8,128)S(1)}, u32[]{:S(2)}, u32[]{:S(2)}) collective-permute-start(f32[256,256]{1,0:T(8,128)S(1)} %get-tuple-element.351), channel_id=1, source_target_pairs={{0,129},{128,1},{2,131},{130,3},{4,133},{132,5},{6,135},{134,7},{8... | collective-permute-start | bytes 786440 | tf_op jit(solution)/shard_map/ppermute | solution.py:33

commit v3 on v2

--- a/solution.py
+++ b/solution.py
@@ -19,6 +19,8 @@
 N_Z = 8
 STEPS = 4
 MIB = 1 << 20
+SHARES = (slice(0, BLK), slice(BLK, BLK + HALF), slice(BLK + HALF, 2 * BLK))
+PAD = 16
 
 
 def permute(value, axes, target):
@@ -138,6 +140,8 @@
     y_out = outs.pop(0) if (2 in parts or 1 in parts) else None
     d_out = outs.pop(0) if (2 in parts or 3 in parts) else None
     before = stage - 1
+    if y_out is not None:
+        y_out[y_out.shape[0] - PAD :] = jnp.zeros((PAD, FEAT), BF16)
     if 3 in parts:
         was = offset("x", before, 2)
         to = offset("x", stage, 3)
@@ -217,9 +221,9 @@
 
 def attn_kernel(where, again, n_near, pos, *refs):
     near, refs = refs[:n_near], refs[n_near:]
-    sums = refs[:2] if again else ()
-    arrays = refs[len(sums) : -3]
-    keep, send, w = refs[-3:]
+    sums = refs[:3] if again else ()
+    arrays = refs[len(sums) : -4]
+    *outs, w = refs[-4:]
     for i in range(len(where)):
         a, b = near[2 * i : 2 * i + 2]
         w[i * FEAT : (i + 1) * FEAT] = jnp.where(pos[3] == 0, a[...], b[...])
@@ -234,8 +238,8 @@
         for h in range(n // HALF):
             rows = pl.ds(pl.multiple_of(blocks[i + h] * HALF, HALF), HALF)
             part = res[h * HALF : (h + 1) * HALF]
-            for j, out in enumerate((keep, send)):
-                block = part[:, j * BLK : (j + 1) * BLK]
+            for j, (out, columns) in enumerate(zip(outs, SHARES)):
+                block = part[:, columns]
                 out[rows, :] = block + sums[j][rows, :] if again else block
         i += n // HALF
 
@@ -244,15 +248,9 @@
     out[...] = a[...] + b[...]
 
 
-def add_split_kernel(_, a, b, out, away, own):
-    total = a[...] + b[...]
-    out[...] = total
-    away[...] = total[:, :BLK]
-    own[...] = total[:, BLK:]
-
-
-def round_kernel(_, a, b, out):
-    out[...] = (a[...] + b[...]).astype(BF16)
+def round_kernel(_, keep, first, second, out):
+    out[:, :HALF] = (keep[:, :HALF] + first[...]).astype(BF16)
+    out[:, HALF:] = (keep[:, HALF:] + second[...]).astype(BF16)
 
 
 def early_kernel(_, s4, to_core, to_y):
@@ -260,13 +258,10 @@
     to_y[...] = s4[:BLK, :BLK]
 
 
-def late_kernel(_, away, early, same, cross):
-    same[...] = away[:BLK] + early[:, :BLK]
-    cross[...] = away[BLK:]
-
-
-def cut_kernel(_, own, near):
-    near[...] = own[BLK:]
+def late_kernel(_, r4, early, same, cross, near):
+    same[...] = r4[:BLK, :BLK] + early[:, :BLK]
+    cross[...] = r4[BLK:, :BLK]
+    near[...] = r4[BLK:, BLK:]
 
 
 def final_kernel(pos, r4, s4, early, same, cross, near, from_y, out):
@@ -274,7 +269,7 @@
 
     @pl.when(mine)
     def _():
-        out[...] = (r4[:BLK] + early[:, BLK:] + same[...]).T
+        out[...] = (r4[:BLK, BLK:] + early[:, BLK:] + same[...]).T
 
     @pl.when(jnp.logical_not(mine))
     def _():
@@ -310,7 +305,7 @@
         outs.append(shape(sum({1: 512, 2: 512, 3: 256}[p] for p in parts), FEAT))
         has_y, has_d = 2 in parts or 1 in parts, 2 in parts or 3 in parts
         if has_y:
-            outs.append(shape(sum({1: 256, 2: 256, 3: 0}[p] for p in parts), FEAT))
+            outs.append(shape(sum({1: 256, 2: 256, 3: 0}[p] for p in parts) + PAD, FEAT))
         if has_d:
             outs.append(shape(sum({1: 0, 2: 256, 3: 128}[p] for p in parts), FEAT))
         if 1 in parts:
@@ -344,7 +339,7 @@
         ]
         return run(
             functools.partial(attn_kernel, where, bool(sums), len(near)),
-            (shape(16 * HALF, BLK, F32),) * 2, 16, *near, *sums, *arrays,
+            tuple(shape(16 * HALF, n, F32) for n in (BLK, HALF, HALF)), 16, *near, *sums, *arrays,
             scratch=[pltpu.VMEM((len(steps) * FEAT, 2 * BLK), BF16)],
         )
 
@@ -355,11 +350,11 @@
     stage(1)
     w_mine = run(stack_kernel, shape(FEAT, BLK), 4, w_away, o_weight)
     w_other = send(core, w_mine)
-    turned = run(turn_kernel, shape(2 * BLK, 16 * HALF), 8, attn_out, other_attn)
     w0 = run(join_kernel, shape(FEAT, 2 * BLK), 4, w_mine, w_other)
     w1 = send(against_z, w0)
     wait(w1)
     stage(2)
+    turned = run(turn_kernel, shape(2 * BLK, 16 * HALF), 8, attn_out, other_attn)
     w2 = send(against_z, w1)
     wait(w2)
     stage(3)
@@ -380,26 +375,22 @@
     near = (w0, w1, w2, w3, w4)
     sums = attn((1, 2), near)
     g4 = weight(3)
-    half = shape(2 * BLK, BLK, F32)
-    s4, s4_away, s4_own = run(
-        add_split_kernel, (shape(2 * BLK, FEAT, F32), half, half), 4, r3, g4
-    )
-    r4_away, r4_own = along_z_last(s4_away), along_z_last(s4_own)
+    s4 = add(r3, g4)
+    r4 = along_z_last(s4)
     to_core, to_y = run(early_kernel, (shape(BLK, FEAT, F32), shape(BLK, BLK, F32)), 4, s4)
     early = permute(to_core, ("c",), lambda i: (0,) if i == 1 else None)
     from_y = permute(to_y, ("yl", "c"), lambda i, j: (i + 1, j) if j == 1 else None)
 
-    keep, out = attn((0, 3), near, sums)
-    other = send(core, out)
+    keep, *out = attn((0, 3), near, sums)
+    other = [send(core, o) for o in out]
     wait(early, from_y)
-    same, cross = run(late_kernel, (shape(BLK, BLK, F32),) * 2, 4, r4_away, early)
+    same, cross, near = run(late_kernel, (shape(BLK, BLK, F32),) * 3, 4, r4, early)
     same = permute(same, ("yl", "c"), lambda i, j: (i + 1, 0) if j == 0 else None)
     cross = permute(cross, ("yl", "c"), lambda i, j: (i + 1, 1) if j == 0 else None)
-    near = run(cut_kernel, shape(BLK, BLK, F32), 4, r4_own)
     near = permute(near, ("c",), lambda i: (1,) if i == 0 else None)
-    attn_grad = run(round_kernel, shape(16 * HALF, BLK), 8, keep, other)
+    attn_grad = run(round_kernel, shape(16 * HALF, BLK), 8, keep, *other)
     weight_grad = run(
-        final_kernel, shape(BLK, BLK, F32), 4, r4_own, s4, early, same, cross, near, from_y
+        final_kernel, shape(BLK, BLK, F32), 4, r4, s4, early, same, cross, near, from_y
     )
     return attn_grad, weight_grad
 

time: 159 us -> 151 us (0.950)
  starting transfers between devices: 52.7 us -> 48.1 us
  waiting for transfers between devices: 77.3 us -> 74.9 us
    ppermute x35, starting transfers between devices: 52.7 us -> 48.1 us  [permute(): return lax.ppermute(value, axes if len(axes) > 1 else axes[0], pairs)]
    ppermute x35, waiting for transfers between devices: 77.3 us -> 74.9 us  [permute(): return lax.ppermute(value, axes if len(axes) > 1 else axes[0], pairs)]
    pallas_call x23 -> x22, Pallas kernels: 26.3 us -> 25.7 us  [call(): pl.pallas_call(kernel, out_shape=out_shape, in_specs=[pl.BlockSpec(memory...]
  transfers between devices with their start and end apart: 35 -> 35, of which waited for: 16 -> 17; matrix products, arithmetic and copies ran while one was open for 0% -> 0% of each run, Pallas kernels for 12% -> 14%
where the time goes in v3:
time: 151 us
  waiting for transfers between devices  74.9 us (50%)
  starting transfers between devices  48.1 us (32%)
  Pallas kernels  25.7 us (17%)
    ppermute x35, waiting for transfers between devices, permute(): return lax.ppermute(value, axes if len(axes) > 1 else axes[0], pairs)  74.9 us
    ppermute x35, starting transfers between devices, permute(): return lax.ppermute(value, axes if len(axes) > 1 else axes[0], pairs)  48.1 us
    pallas_call x22, Pallas kernels, call(): pl.pallas_call(kernel, out_shape=out_shape, in_specs=[pl.BlockSpec(memory...  25.7 us
  transfers between devices with their start and end apart: 35, of which 17 were waited for; matrix products, arithmetic and copies ran while one was open for 0% of the time, Pallas kernels for 14%

profile of v3, /device:TPU:1, one launch (start us, length us, event | category | flops | bytes accessed | tf_op | source)
XLA Modules:
  0.0 150.9 jit_solution(1071119895054287329)
XLA Ops:
  0.6 3.3 %collective-permute-start.1 = (bf16[128,4096]{1,0:T(8,128)(2,1)}, bf16[128,4096]{1,0:T(8,128)(2,1)S(1)}, u32[]{:S(2)}, u32[]{:S(2)}) collective-permute-start(bf16[128,4096]{1,0:T(8,128)(2,1)} %refs_0_.3), channel_id=1, source_target_pairs={{0,1},{1,0},{2,3},{3,2},{4,5},{5,4},{6,7},{7,6},{8,9},{9,8},{10,11... | collective-permute-start | bytes 3145736 | tf_op jit(solution)/shard_map/ppermute | solution.py:35
  4.0 2.4 %collective-permute-done.1.refs_1_ = bf16[128,4096]{1,0:T(8,128)(2,1)S(1)} collective-permute-done((bf16[128,4096]{1,0:T(8,128)(2,1)}, bf16[128,4096]{1,0:T(8,128)(2,1)S(1)}, u32[]{:S(2)}, u32[]{:S(2)}) %collective-permute-start.1) | collective-permute-done | bytes 1048608 | tf_op jit(solution)/shard_map/ppermute | solution.py:35
  6.5 1.2 copy-done
  7.7 0.6 shard_map.50
  8.3 0.9 collective-permute-done.away
  9.2 0.6 shard_map.51.mine
  9.8 1.0 collective-permute-start.2
  10.8 0.7 collective-permute-start.5
  11.9 0.6 shard_map.52.refs_3_
  12.5 5.2 %collective-permute-start.3 = (bf16[512,512]{1,0:T(8,128)(2,1)S(1)}, bf16[512,512]{1,0:T(8,128)(2,1)S(1)}, u32[]{:S(2)}, u32[]{:S(2)}) collective-permute-start(bf16[512,512]{1,0:T(8,128)(2,1)S(1)} %shard_map.52.refs_3_), channel_id=1, source_target_pairs={{0,16},{1,113},{2,18},{3,115},{4,20},{5,117},{6,22},{7,119},{8,24}... | collective-permute-start | bytes 1572872 | tf_op jit(solution)/shard_map/ppermute | solution.py:35
  17.7 3.3 %collective-permute-start.6 = (bf16[272,512]{1,0:T(8,128)(2,1)S(1)}, bf16[272,512]{1,0:T(8,128)(2,1)S(1)}, u32[]{:S(2)}, u32[]{:S(2)}) collective-permute-start(bf16[272,512]{1,0:T(8,128)(2,1)S(1)} %get-tuple-element.197), channel_id=1, source_target_pairs={{0,9},{1,8},{2,11},{3,10},{4,13},{5,12},{6,15},{7,14},{8,1},{9,0},... | collective-permute-start | bytes 835592 | tf_op jit(solution)/shard_map/ppermute | solution.py:35
  21.1 7.0 %collective-permute-done.6.refs_3_.refs_1_.refs_8_ = bf16[272,512]{1,0:T(8,128)(2,1)S(1)} collective-permute-done((bf16[272,512]{1,0:T(8,128)(2,1)S(1)}, bf16[272,512]{1,0:T(8,128)(2,1)S(1)}, u32[]{:S(2)}, u32[]{:S(2)}) %collective-permute-start.6) | collective-permute-done | bytes 278560 | tf_op jit(solution)/shard_map/ppermute | solution.py:35
  28.1 0.7 shard_map.53
  28.8 1.2 collective-permute-start.8
  30.0 2.3 %collective-permute-start.9 = (bf16[528,512]{1,0:T(8,128)(2,1)S(1)}, bf16[528,512]{1,0:T(8,128)(2,1)S(1)}, u32[]{:S(2)}, u32[]{:S(2)}) collective-permute-start(bf16[528,512]{1,0:T(8,128)(2,1)S(1)} %get-tuple-element.209), channel_id=1, source_target_pairs={{0,9},{1,8},{2,11},{3,10},{4,13},{5,12},{6,15},{7,14},{8,1},{9,0},... | collective-permute-start | bytes 1622024 | tf_op jit(solution)/shard_map/ppermute | solution.py:35
  32.3 1.2 shard_map.54.turned
  33.6 0.8 collective-permute-start.7
  34.8 1.2 collective-permute-done.10.refs_4_.refs_7_.refs_13_
  36.0 6.0 %collective-permute-done.7.refs_1_.refs_2_ = bf16[512,512]{1,0:T(8,128)(2,1)S(1)} collective-permute-done((bf16[512,512]{1,0:T(8,128)(2,1)S(1)}, bf16[512,512]{1,0:T(8,128)(2,1)S(1)}, u32[]{:S(2)}, u32[]{:S(2)}) %collective-permute-start.7) | collective-permute-done | bytes 524320 | tf_op jit(solution)/shard_map/ppermute | solution.py:35
  42.0 3.6 %collective-permute-done.9.refs_3_.refs_5_.refs_1_.refs_11_ = bf16[528,512]{1,0:T(8,128)(2,1)S(1)} collective-permute-done((bf16[528,512]{1,0:T(8,128)(2,1)S(1)}, bf16[528,512]{1,0:T(8,128)(2,1)S(1)}, u32[]{:S(2)}, u32[]{:S(2)}) %collective-permute-start.9) | collective-permute-done | bytes 540704 | tf_op jit(solution)/shard_map/ppermute | solution.py:35
  45.6 0.7 shard_map.55
  46.3 2.1 %collective-permute-start.12 = (bf16[1280,512]{1,0:T(8,128)(2,1)S(1)}, bf16[1280,512]{1,0:T(8,128)(2,1)S(1)}, u32[]{:S(2)}, u32[]{:S(2)}) collective-permute-start(bf16[1280,512]{1,0:T(8,128)(2,1)S(1)} %get-tuple-element.220), channel_id=1, source_target_pairs={{0,2},{1,7},{2,4},{3,1},{4,6},{5,3},{6,0},{7,5},{8,10},{9,15},{10,... | collective-permute-start | bytes 3932168 | tf_op jit(solution)/shard_map/ppermute | solution.py:35
  48.4 2.0 %collective-permute-start.13 = (bf16[528,512]{1,0:T(8,128)(2,1)S(1)}, bf16[528,512]{1,0:T(8,128)(2,1)S(1)}, u32[]{:S(2)}, u32[]{:S(2)}) collective-permute-start(bf16[528,512]{1,0:T(8,128)(2,1)S(1)} %get-tuple-element.222), channel_id=1, source_target_pairs={{0,9},{1,8},{2,11},{3,10},{4,13},{5,12},{6,15},{7,14},{8,1},{9,0},... | collective-permute-start | bytes 1622024 | tf_op jit(solution)/shard_map/ppermute | solution.py:35
  50.4 0.7 collective-permute-start.11
  51.1 1.7 %collective-permute-done.14.refs_4_.refs_8_.refs_7_.refs_10_.refs_14_ = bf16[384,512]{1,0:T(8,128)(2,1)S(1)} collective-permute-done((bf16[384,512]{1,0:T(8,128)(2,1)S(1)}, bf16[384,512]{1,0:T(8,128)(2,1)S(1)}, u32[]{:S(2)}, u32[]{:S(2)}) %collective-permute-start.14) | collective-permute-done | bytes 393248 | tf_op jit(solution)/shard_map/ppermute | solution.py:35
  52.9 5.9 %collective-permute-done.11.refs_0_.refs_1_ = bf16[512,512]{1,0:T(8,128)(2,1)S(1)} collective-permute-done((bf16[512,512]{1,0:T(8,128)(2,1)S(1)}, bf16[512,512]{1,0:T(8,128)(2,1)S(1)}, u32[]{:S(2)}, u32[]{:S(2)}) %collective-permute-start.11) | collective-permute-done | bytes 524320 | tf_op jit(solution)/shard_map/ppermute | solution.py:35
  58.7 4.2 %collective-permute-done.13.refs_3_.refs_5_.refs_1_.refs_8_ = bf16[528,512]{1,0:T(8,128)(2,1)S(1)} collective-permute-done((bf16[528,512]{1,0:T(8,128)(2,1)S(1)}, bf16[528,512]{1,0:T(8,128)(2,1)S(1)}, u32[]{:S(2)}, u32[]{:S(2)}) %collective-permute-start.13) | collective-permute-done | bytes 540704 | tf_op jit(solution)/shard_map/ppermute | solution.py:35
  63.1 0.7 shard_map.56
  63.9 3.2 %collective-permute-start.16 = (bf16[1280,512]{1,0:T(8,128)(2,1)S(1)}, bf16[1280,512]{1,0:T(8,128)(2,1)S(1)}, u32[]{:S(2)}, u32[]{:S(2)}) collective-permute-start(bf16[1280,512]{1,0:T(8,128)(2,1)S(1)} %get-tuple-element.233), channel_id=1, source_target_pairs={{0,2},{1,7},{2,4},{3,1},{4,6},{5,3},{6,0},{7,5},{8,10},{9,15},{10,... | collective-permute-start | bytes 3932168 | tf_op jit(solution)/shard_map/ppermute | solution.py:35
  67.1 1.8 %shard_map.57 = f32[512,512]{1,0:T(8,128)S(1)} custom-call(s32[5]{0:T(128)S(1)} %stack.23.pos._, bf16[512,2048]{1,0:T(8,128)(2,1)S(1)} %shard_map.54.turned, bf16[256,512]{1,0:T(8,128)(2,1)S(1)} %get-tuple-element.330.refs_0_.refs_7_, bf16[272,512]{1,0:T(8,128)(2,1)S(1)} %collective-permute-done.6.refs_3_.refs_1_.refs_8_, ...), custom_call_target="tpu_custom_call" | custom-call | bytes 65536 | tf_op jit(solution)/shard_map/pallas_call | solution.py:79
  69.0 2.9 %collective-permute-start.18 = (bf16[528,512]{1,0:T(8,128)(2,1)S(1)}, bf16[528,512]{1,0:T(8,128)(2,1)S(1)}, u32[]{:S(2)}, u32[]{:S(2)}) collective-permute-start(bf16[528,512]{1,0:T(8,128)(2,1)S(1)} %get-tuple-element.237), channel_id=1, source_target_pairs={{0,9},{1,8},{2,11},{3,10},{4,13},{5,12},{6,15},{7,14},{8,1},{9,0},... | collective-permute-start | bytes 1622024 | tf_op jit(solution)/shard_map/ppermute | solution.py:35
  71.9 1.7 %collective-permute-done.17.refs_2_.refs_8_.refs_7_.refs_11_ = bf16[384,512]{1,0:T(8,128)(2,1)S(1)} collective-permute-done((bf16[384,512]{1,0:T(8,128)(2,1)S(1)}, bf16[384,512]{1,0:T(8,128)(2,1)S(1)}, u32[]{:S(2)}, u32[]{:S(2)}) %collective-permute-start.17) | collective-permute-done | bytes 393248 | tf_op jit(solution)/shard_map/ppermute | solution.py:35
  73.6 11.0 %collective-permute-done.18.refs_1_.refs_5_.refs_13_.refs_16_ = bf16[528,512]{1,0:T(8,128)(2,1)S(1)} collective-permute-done((bf16[528,512]{1,0:T(8,128)(2,1)S(1)}, bf16[528,512]{1,0:T(8,128)(2,1)S(1)}, u32[]{:S(2)}, u32[]{:S(2)}) %collective-permute-start.18) | collective-permute-done | bytes 540704 | tf_op jit(solution)/shard_map/ppermute | solution.py:35
  84.6 0.6 shard_map.58
  85.3 1.8 %shard_map.59.b = f32[512,512]{1,0:T(8,128)S(1)} custom-call(s32[5]{0:T(128)S(1)} %stack.23.pos._, bf16[512,2048]{1,0:T(8,128)(2,1)S(1)} %shard_map.54.turned, bf16[256,512]{1,0:T(8,128)(2,1)S(1)} %get-tuple-element.291.refs_0_.refs_4_, bf16[528,512]{1,0:T(8,128)(2,1)S(1)} %collective-permute-done.9.refs_3_.refs_5_.refs_1_.refs_11_, ...), custom_call_target="tpu_custom_call" | custom-call | bytes 65536 | tf_op jit(solution)/shard_map/pallas_call | solution.py:79
  87.1 0.6 shard_map.60
  87.7 1.1 collective-permute-start.22
  88.8 2.7 %collective-permute-start.19 = (bf16[768,512]{1,0:T(8,128)(2,1)S(1)}, bf16[768,512]{1,0:T(8,128)(2,1)S(1)}, u32[]{:S(2)}, u32[]{:S(2)}) collective-permute-start(bf16[768,512]{1,0:T(8,128)(2,1)S(1)} %get-tuple-element.253), channel_id=1, source_target_pairs={{0,2},{1,7},{2,4},{3,1},{4,6},{5,3},{6,0},{7,5},{8,10},{9,15},{10,... | collective-permute-start | bytes 2359304 | tf_op jit(solution)/shard_map/ppermute | solution.py:35
  91.5 1.2 collective-permute-start.23
  92.7 9.2 %collective-permute-done.23.refs_1_.refs_5_.refs_19_ = bf16[272,512]{1,0:T(8,128)(2,1)S(1)} collective-permute-done((bf16[272,512]{1,0:T(8,128)(2,1)S(1)}, bf16[272,512]{1,0:T(8,128)(2,1)S(1)}, u32[]{:S(2)}, u32[]{:S(2)}) %collective-permute-start.23) | collective-permute-done | bytes 278560 | tf_op jit(solution)/shard_map/ppermute | solution.py:35
  101.9 0.6 shard_map.61
  102.5 1.8 %shard_map.62.b = f32[512,512]{1,0:T(8,128)S(1)} custom-call(s32[5]{0:T(128)S(1)} %stack.23.pos._, bf16[512,2048]{1,0:T(8,128)(2,1)S(1)} %shard_map.54.turned, bf16[256,512]{1,0:T(8,128)(2,1)S(1)} %get-tuple-element.299.refs_0_.refs_12_, bf16[528,512]{1,0:T(8,128)(2,1)S(1)} %collective-permute-done.13.refs_3_.refs_5_.refs_1_.refs_8_, ...), custom_call_target="tpu_custom_call" | custom-call | bytes 65536 | tf_op jit(solution)/shard_map/pallas_call | solution.py:79
  104.3 0.6 shard_map.63
  105.1 0.7 collective-permute-start.15
  105.8 1.7 %collective-permute-start.24 = (bf16[256,512]{1,0:T(8,128)(2,1)S(1)}, bf16[256,512]{1,0:T(8,128)(2,1)S(1)}, u32[]{:S(2)}, u32[]{:S(2)}) collective-permute-start(bf16[256,512]{1,0:T(8,128)(2,1)S(1)} %get-tuple-element.306), channel_id=1, source_target_pairs={{0,2},{1,7},{2,4},{3,1},{4,6},{5,3},{6,0},{7,5},{8,10},{9,15},{10,... | collective-permute-start | bytes 786440 | tf_op jit(solution)/shard_map/ppermute | solution.py:35
  107.5 2.3 %collective-permute-start.25 = (bf16[128,512]{1,0:T(8,128)(2,1)S(1)}, bf16[128,512]{1,0:T(8,128)(2,1)S(1)}, u32[]{:S(2)}, u32[]{:S(2)}) collective-permute-start(bf16[128,512]{1,0:T(8,128)(2,1)S(1)} %get-tuple-element.307), channel_id=1, source_target_pairs={{0,1},{1,0},{2,3},{3,2},{4,5},{5,4},{6,7},{7,6},{8,9},{9,8},{10,11... | collective-permute-start | bytes 393224 | tf_op jit(solution)/shard_map/ppermute | solution.py:35
  109.8 2.9 %shard_map.64 = (f32[2048,256]{1,0:T(8,128)S(1)}, f32[2048,128]{1,0:T(8,128)S(1)}, f32[2048,128]{1,0:T(8,128)S(1)}) custom-call(s32[5]{0:T(128)S(1)} %stack.23.pos._, bf16[512,512]{1,0:T(8,128)(2,1)S(1)} %collective-permute-done.11.refs_0_.refs_1_, bf16[512,512]{1,0:T(8,128)(2,1)S(1)} %collective-permute-done.7.refs_1_.refs_2_, ...), custom_call_target="tpu_custom_call" | custom-call | bytes 65536 | tf_op jit(solution)/shard_map/pallas_call | solution.py:79
  112.7 1.8 %shard_map.65.b = f32[512,512]{1,0:T(8,128)S(1)} custom-call(s32[5]{0:T(128)S(1)} %stack.23.pos._, bf16[512,2048]{1,0:T(8,128)(2,1)S(1)} %shard_map.54.turned, bf16[256,512]{1,0:T(8,128)(2,1)S(1)} %get-tuple-element.338.refs_0_.refs_15_, bf16[528,512]{1,0:T(8,128)(2,1)S(1)} %collective-permute-done.18.refs_1_.refs_5_.refs_13_.refs_16_, ...), custom_call_target="tpu_custom_call" | custom-call | bytes 65536 | tf_op jit(solution)/shard_map/pallas_call | solution.py:79
  114.5 10.9 %collective-permute-done.26.a = f32[512,512]{1,0:T(8,128)S(1)} collective-permute-done((f32[512,512]{1,0:T(8,128)S(1)}, f32[512,512]{1,0:T(8,128)S(1)}, u32[]{:S(2)}, u32[]{:S(2)}) %collective-permute-start.26) | collective-permute-done | bytes 1048608 | tf_op jit(solution)/shard_map/ppermute | solution.py:35
  125.5 0.6 shard_map.66.s4
  126.1 0.9 collective-permute-start.29
  127.1 0.6 shard_map.67
  127.7 3.0 %shard_map.68 = (f32[2048,256]{1,0:T(8,128)S(1)}, f32[2048,128]{1,0:T(8,128)S(1)}, f32[2048,128]{1,0:T(8,128)S(1)}) custom-call(s32[5]{0:T(128)S(1)} %stack.23.pos._, bf16[512,512]{1,0:T(8,128)(2,1)S(1)} %collective-permute-done.15.refs_0_, bf16[512,512]{1,0:T(8,128)(2,1)S(1)} %collective-permute-done.11.refs_0_.refs_1_, ...), custom_call_target="tpu_custom_call" | custom-call | bytes 65536 | tf_op jit(solution)/shard_map/pallas_call | solution.py:79
  130.8 0.5 collective-permute-start.27
  131.3 2.0 %collective-permute-start.30 = (f32[256,512]{1,0:T(8,128)S(1)}, f32[256,512]{1,0:T(8,128)S(1)}, u32[]{:S(2)}, u32[]{:S(2)}) collective-permute-start(f32[256,512]{1,0:T(8,128)S(1)} %get-tuple-element.351), channel_id=1, source_target_pairs={{1,0},{3,2},{5,4},{7,6},{9,8},{11,10},{13,12},{15,14},{17,16},{19,... | collective-permute-start | bytes 1572872 | tf_op jit(solution)/shard_map/ppermute | solution.py:35
  133.3 2.0 %collective-permute-start.31 = (f32[256,256]{1,0:T(8,128)S(1)}, f32[256,256]{1,0:T(8,128)S(1)}, u32[]{:S(2)}, u32[]{:S(2)}) collective-permute-start(f32[256,256]{1,0:T(8,128)S(1)} %get-tuple-element.322), channel_id=1, source_target_pairs={{1,129},{129,1},{3,131},{131,3},{5,133},{133,5},{7,135},{135,7},{9... | collective-permute-start | bytes 786440 | tf_op jit(solution)/shard_map/ppermute | solution.py:35
  135.4 5.1 %collective-permute-done.31.from_y = f32[256,256]{1,0:T(8,128)S(1)} collective-permute-done((f32[256,256]{1,0:T(8,128)S(1)}, f32[256,256]{1,0:T(8,128)S(1)}, u32[]{:S(2)}, u32[]{:S(2)}) %collective-permute-start.31) | collective-permute-done | bytes 262176 | tf_op jit(solution)/shard_map/ppermute | solution.py:35
  140.5 0.6 shard_map.69
  141.1 0.7 collective-permute-start.32
  141.8 1.3 collective-permute-start.33
  143.1 1.3 collective-permute-start.34
  144.4 1.7 %shard_map.70 = bf16[2048,256]{1,0:T(8,128)(2,1)} custom-call(s32[5]{0:T(128)S(1)} %stack.23.pos._, f32[2048,256]{1,0:T(8,128)S(1)} %get-tuple-element.355.keep, f32[2048,128]{1,0:T(8,128)S(1)} %collective-permute-done.27.first, f32[2048,128]{1,0:T(8,128)S(1)} %collective-permute-done.28.second), custom_call_target="tpu_custom_call" | custom-call | bytes 65536 | tf_op jit(solution)/shard_map/pallas_call | solution.py:79
  146.1 3.4 %collective-permute-done.33.cross = f32[256,256]{1,0:T(8,128)S(1)} collective-permute-done((f32[256,256]{1,0:T(8,128)S(1)}, f32[256,256]{1,0:T(8,128)S(1)}, u32[]{:S(2)}, u32[]{:S(2)}) %collective-permute-start.33) | collective-permute-done | bytes 262176 | tf_op jit(solution)/shard_map/ppermute | solution.py:35
  149.5 1.4 shard_map.71
  (37 shorter events, 1.6 us)
Async XLA Ops:
  0.6 5.8 %collective-permute-start.1 = (bf16[128,4096]{1,0:T(8,128)(2,1)}, bf16[128,4096]{1,0:T(8,128)(2,1)S(1)}, u32[]{:S(2)}, u32[]{:S(2)}) collective-permute-start(bf16[128,4096]{1,0:T(8,128)(2,1)} %refs_0_.3), channel_id=1, source_target_pairs={{0,1},{1,0},{2,3},{3,2},{4,5},{5,4},{6,7},{7,6},{8,9},{9,8},{10,11... | collective-permute-start | bytes 3145736 | tf_op jit(solution)/shard_map/ppermute | solution.py:35
  4.0 5.3 %collective-permute-start = (bf16[256,256]{1,0:T(8,128)(2,1)}, bf16[256,256]{1,0:T(8,128)(2,1)S(1)}, u32[]{:S(2)}, u32[]{:S(2)}) collective-permute-start(bf16[256,256]{1,0:T(8,128)(2,1)} %own), channel_id=1, source_target_pairs={{0,128},{128,0},{1,129},{129,1},{2,130},{130,2},{3,131},{131,3},{4... | collective-permute-start | bytes 393224 | tf_op jit(solution)/shard_map/ppermute | solution.py:35
  6.5 1.2 copy-start
  7.7 1.6 %copy-start.3 = (bf16[256,256]{1,0:T(8,128)(2,1)S(1)}, bf16[256,256]{1,0:T(8,128)(2,1)}, u32[]{:S(2)}) copy-start(bf16[256,256]{1,0:T(8,128)(2,1)} %own) | copy-start | bytes 393220
  8.3 9.4 %copy-start.2 = (bf16[2048,256]{1,0:T(8,128)(2,1)S(1)}, bf16[2048,256]{1,0:T(8,128)(2,1)}, u32[]{:S(2)}) copy-start(bf16[2048,256]{1,0:T(8,128)(2,1)} %own.1) | copy-start | bytes 3145732
  9.8 2.1 %collective-permute-start.2 = (bf16[512,256]{1,0:T(8,128)(2,1)S(1)}, bf16[512,256]{1,0:T(8,128)(2,1)S(1)}, u32[]{:S(2)}, u32[]{:S(2)}) collective-permute-start(bf16[512,256]{1,0:T(8,128)(2,1)S(1)} %shard_map.51.mine), channel_id=1, source_target_pairs={{0,1},{1,0},{2,3},{3,2},{4,5},{5,4},{6,7},{7,6},{8,9},{9,8},{10,11... | collective-permute-start | bytes 786440 | tf_op jit(solution)/shard_map/ppermute | solution.py:35
  10.8 17.3 %collective-permute-start.5 = (bf16[512,512]{1,0:T(8,128)(2,1)S(1)}, bf16[512,512]{1,0:T(8,128)(2,1)S(1)}, u32[]{:S(2)}, u32[]{:S(2)}) collective-permute-start(bf16[512,512]{1,0:T(8,128)(2,1)S(1)} %get-tuple-element.195), channel_id=1, source_target_pairs={{0,2},{1,7},{2,4},{3,1},{4,6},{5,3},{6,0},{7,5},{8,10},{9,15},{10,... | collective-permute-start | bytes 1572872 | tf_op jit(solution)/shard_map/ppermute | solution.py:35
  12.5 15.6 %collective-permute-start.3 = (bf16[512,512]{1,0:T(8,128)(2,1)S(1)}, bf16[512,512]{1,0:T(8,128)(2,1)S(1)}, u32[]{:S(2)}, u32[]{:S(2)}) collective-permute-start(bf16[512,512]{1,0:T(8,128)(2,1)S(1)} %shard_map.52.refs_3_), channel_id=1, source_target_pairs={{0,16},{1,113},{2,18},{3,115},{4,20},{5,117},{6,22},{7,119},{8,24}... | collective-permute-start | bytes 1572872 | tf_op jit(solution)/shard_map/ppermute | solution.py:35
  17.7 14.6 %collective-permute-start.4 = (bf16[2048,256]{1,0:T(8,128)(2,1)S(1)}, bf16[2048,256]{1,0:T(8,128)(2,1)S(1)}, u32[]{:S(2)}, u32[]{:S(2)}) collective-permute-start(bf16[2048,256]{1,0:T(8,128)(2,1)S(1)} %copy-done.2), channel_id=1, source_target_pairs={{0,1},{1,0},{2,3},{3,2},{4,5},{5,4},{6,7},{7,6},{8,9},{9,8},{10,11... | collective-permute-start | bytes 3145736 | tf_op jit(solution)/shard_map/ppermute | solution.py:35
  17.7 10.3 %collective-permute-start.6 = (bf16[272,512]{1,0:T(8,128)(2,1)S(1)}, bf16[272,512]{1,0:T(8,128)(2,1)S(1)}, u32[]{:S(2)}, u32[]{:S(2)}) collective-permute-start(bf16[272,512]{1,0:T(8,128)(2,1)S(1)} %get-tuple-element.197), channel_id=1, source_target_pairs={{0,9},{1,8},{2,11},{3,10},{4,13},{5,12},{6,15},{7,14},{8,1},{9,0},... | collective-permute-start | bytes 835592 | tf_op jit(solution)/shard_map/ppermute | solution.py:35
  28.8 16.8 %collective-permute-start.8 = (bf16[1024,512]{1,0:T(8,128)(2,1)S(1)}, bf16[1024,512]{1,0:T(8,128)(2,1)S(1)}, u32[]{:S(2)}, u32[]{:S(2)}) collective-permute-start(bf16[1024,512]{1,0:T(8,128)(2,1)S(1)} %get-tuple-element.207), channel_id=1, source_target_pairs={{0,2},{1,7},{2,4},{3,1},{4,6},{5,3},{6,0},{7,5},{8,10},{9,15},{10,... | collective-permute-start | bytes 3145736 | tf_op jit(solution)/shard_map/ppermute | solution.py:35
  30.0 15.5 %copy-start.1 = (bf16[128,4096]{1,0:T(8,128)(2,1)S(1)}, bf16[128,4096]{1,0:T(8,128)(2,1)}, u32[]{:S(2)}) copy-start(bf16[128,4096]{1,0:T(8,128)(2,1)} %refs_0_.3) | copy-start | bytes 3145732
  30.0 15.5 %collective-permute-start.9 = (bf16[528,512]{1,0:T(8,128)(2,1)S(1)}, bf16[528,512]{1,0:T(8,128)(2,1)S(1)}, u32[]{:S(2)}, u32[]{:S(2)}) collective-permute-start(bf16[528,512]{1,0:T(8,128)(2,1)S(1)} %get-tuple-element.209), channel_id=1, source_target_pairs={{0,9},{1,8},{2,11},{3,10},{4,13},{5,12},{6,15},{7,14},{8,1},{9,0},... | collective-permute-start | bytes 1622024 | tf_op jit(solution)/shard_map/ppermute | solution.py:35
  33.6 8.4 %collective-permute-start.7 = (bf16[512,512]{1,0:T(8,128)(2,1)S(1)}, bf16[512,512]{1,0:T(8,128)(2,1)S(1)}, u32[]{:S(2)}, u32[]{:S(2)}) collective-permute-start(bf16[512,512]{1,0:T(8,128)(2,1)S(1)} %collective-permute-done.3.refs_3_.refs_2_), channel_id=1, source_target_pairs={{0,16},{1,113},{2,18},{3,115},{4,20},{5,117},{6,22},{7,119},{8,24}... | collective-permute-start | bytes 1572872 | tf_op jit(solution)/shard_map/ppermute | solution.py:35
  34.4 1.6 %collective-permute-start.10 = (bf16[256,512]{1,0:T(8,128)(2,1)S(1)}, bf16[256,512]{1,0:T(8,128)(2,1)S(1)}, u32[]{:S(2)}, u32[]{:S(2)}) collective-permute-start(bf16[256,512]{1,0:T(8,128)(2,1)S(1)} %get-tuple-element.211), channel_id=1, source_target_pairs={{0,1},{1,0},{2,3},{3,2},{4,5},{5,4},{6,7},{7,6},{8,9},{9,8},{10,11... | collective-permute-start | bytes 786440 | tf_op jit(solution)/shard_map/ppermute | solution.py:35
  46.3 16.8 %collective-permute-start.12 = (bf16[1280,512]{1,0:T(8,128)(2,1)S(1)}, bf16[1280,512]{1,0:T(8,128)(2,1)S(1)}, u32[]{:S(2)}, u32[]{:S(2)}) collective-permute-start(bf16[1280,512]{1,0:T(8,128)(2,1)S(1)} %get-tuple-element.220), channel_id=1, source_target_pairs={{0,2},{1,7},{2,4},{3,1},{4,6},{5,3},{6,0},{7,5},{8,10},{9,15},{10,... | collective-permute-start | bytes 3932168 | tf_op jit(solution)/shard_map/ppermute | solution.py:35
  48.4 14.5 %collective-permute-start.13 = (bf16[528,512]{1,0:T(8,128)(2,1)S(1)}, bf16[528,512]{1,0:T(8,128)(2,1)S(1)}, u32[]{:S(2)}, u32[]{:S(2)}) collective-permute-start(bf16[528,512]{1,0:T(8,128)(2,1)S(1)} %get-tuple-element.222), channel_id=1, source_target_pairs={{0,9},{1,8},{2,11},{3,10},{4,13},{5,12},{6,15},{7,14},{8,1},{9,0},... | collective-permute-start | bytes 1622024 | tf_op jit(solution)/shard_map/ppermute | solution.py:35
  50.4 8.3 %collective-permute-start.11 = (bf16[512,512]{1,0:T(8,128)(2,1)S(1)}, bf16[512,512]{1,0:T(8,128)(2,1)S(1)}, u32[]{:S(2)}, u32[]{:S(2)}) collective-permute-start(bf16[512,512]{1,0:T(8,128)(2,1)S(1)} %collective-permute-done.7.refs_1_.refs_2_), channel_id=1, source_target_pairs={{0,16},{1,113},{2,18},{3,115},{4,20},{5,117},{6,22},{7,119},{8,24}... | collective-permute-start | bytes 1572872 | tf_op jit(solution)/shard_map/ppermute | solution.py:35
  51.1 1.7 %collective-permute-start.14 = (bf16[384,512]{1,0:T(8,128)(2,1)S(1)}, bf16[384,512]{1,0:T(8,128)(2,1)S(1)}, u32[]{:S(2)}, u32[]{:S(2)}) collective-permute-start(bf16[384,512]{1,0:T(8,128)(2,1)S(1)} %get-tuple-element.224), channel_id=1, source_target_pairs={{0,1},{1,0},{2,3},{3,2},{4,5},{5,4},{6,7},{7,6},{8,9},{9,8},{10,11... | collective-permute-start | bytes 1179656 | tf_op jit(solution)/shard_map/ppermute | solution.py:35
  63.9 20.8 %collective-permute-start.16 = (bf16[1280,512]{1,0:T(8,128)(2,1)S(1)}, bf16[1280,512]{1,0:T(8,128)(2,1)S(1)}, u32[]{:S(2)}, u32[]{:S(2)}) collective-permute-start(bf16[1280,512]{1,0:T(8,128)(2,1)S(1)} %get-tuple-element.233), channel_id=1, source_target_pairs={{0,2},{1,7},{2,4},{3,1},{4,6},{5,3},{6,0},{7,5},{8,10},{9,15},{10,... | collective-permute-start | bytes 3932168 | tf_op jit(solution)/shard_map/ppermute | solution.py:35
  68.9 18.2 %collective-permute-start.21 = (f32[512,512]{1,0:T(8,128)S(1)}, f32[512,512]{1,0:T(8,128)S(1)}, u32[]{:S(2)}, u32[]{:S(2)}) collective-permute-start(f32[512,512]{1,0:T(8,128)S(1)} %shard_map.57), channel_id=1, source_target_pairs={{0,112},{1,17},{2,114},{3,19},{4,116},{5,21},{6,118},{7,23},{8,120... | collective-permute-start | bytes 3145736 | tf_op jit(solution)/shard_map/ppermute | solution.py:35
  69.0 15.7 %collective-permute-start.18 = (bf16[528,512]{1,0:T(8,128)(2,1)S(1)}, bf16[528,512]{1,0:T(8,128)(2,1)S(1)}, u32[]{:S(2)}, u32[]{:S(2)}) collective-permute-start(bf16[528,512]{1,0:T(8,128)(2,1)S(1)} %get-tuple-element.237), channel_id=1, source_target_pairs={{0,9},{1,8},{2,11},{3,10},{4,13},{5,12},{6,15},{7,14},{8,1},{9,0},... | collective-permute-start | bytes 1622024 | tf_op jit(solution)/shard_map/ppermute | solution.py:35
  71.9 1.7 %collective-permute-start.17 = (bf16[384,512]{1,0:T(8,128)(2,1)S(1)}, bf16[384,512]{1,0:T(8,128)(2,1)S(1)}, u32[]{:S(2)}, u32[]{:S(2)}) collective-permute-start(bf16[384,512]{1,0:T(8,128)(2,1)S(1)} %get-tuple-element.235), channel_id=1, source_target_pairs={{0,1},{1,0},{2,3},{3,2},{4,5},{5,4},{6,7},{7,6},{8,9},{9,8},{10,11... | collective-permute-start | bytes 1179656 | tf_op jit(solution)/shard_map/ppermute | solution.py:35
  87.7 16.5 %collective-permute-start.22 = (f32[512,512]{1,0:T(8,128)S(1)}, f32[512,512]{1,0:T(8,128)S(1)}, u32[]{:S(2)}, u32[]{:S(2)}) collective-permute-start(f32[512,512]{1,0:T(8,128)S(1)} %shard_map.60), channel_id=1, source_target_pairs={{0,112},{1,17},{2,114},{3,19},{4,116},{5,21},{6,118},{7,23},{8,120... | collective-permute-start | bytes 3145736 | tf_op jit(solution)/shard_map/ppermute | solution.py:35
  88.8 13.1 %collective-permute-start.19 = (bf16[768,512]{1,0:T(8,128)(2,1)S(1)}, bf16[768,512]{1,0:T(8,128)(2,1)S(1)}, u32[]{:S(2)}, u32[]{:S(2)}) collective-permute-start(bf16[768,512]{1,0:T(8,128)(2,1)S(1)} %get-tuple-element.253), channel_id=1, source_target_pairs={{0,2},{1,7},{2,4},{3,1},{4,6},{5,3},{6,0},{7,5},{8,10},{9,15},{10,... | collective-permute-start | bytes 2359304 | tf_op jit(solution)/shard_map/ppermute | solution.py:35
  91.5 10.4 %collective-permute-start.20 = (bf16[384,512]{1,0:T(8,128)(2,1)S(1)}, bf16[384,512]{1,0:T(8,128)(2,1)S(1)}, u32[]{:S(2)}, u32[]{:S(2)}) collective-permute-start(bf16[384,512]{1,0:T(8,128)(2,1)S(1)} %get-tuple-element.254), channel_id=1, source_target_pairs={{0,1},{1,0},{2,3},{3,2},{4,5},{5,4},{6,7},{7,6},{8,9},{9,8},{10,11... | collective-permute-start | bytes 1179656 | tf_op jit(solution)/shard_map/ppermute | solution.py:35
  91.5 10.4 %collective-permute-start.23 = (bf16[272,512]{1,0:T(8,128)(2,1)S(1)}, bf16[272,512]{1,0:T(8,128)(2,1)S(1)}, u32[]{:S(2)}, u32[]{:S(2)}) collective-permute-start(bf16[272,512]{1,0:T(8,128)(2,1)S(1)} %get-tuple-element.270), channel_id=1, source_target_pairs={{0,9},{1,8},{2,11},{3,10},{4,13},{5,12},{6,15},{7,14},{8,1},{9,0},... | collective-permute-start | bytes 835592 | tf_op jit(solution)/shard_map/ppermute | solution.py:35
  104.9 20.6 %collective-permute-start.26 = (f32[512,512]{1,0:T(8,128)S(1)}, f32[512,512]{1,0:T(8,128)S(1)}, u32[]{:S(2)}, u32[]{:S(2)}) collective-permute-start(f32[512,512]{1,0:T(8,128)S(1)} %shard_map.63), channel_id=1, source_target_pairs={{0,112},{1,17},{2,114},{3,19},{4,116},{5,21},{6,118},{7,23},{8,120... | collective-permute-start | bytes 3145736 | tf_op jit(solution)/shard_map/ppermute | solution.py:35
  105.1 22.6 %collective-permute-start.15 = (bf16[512,512]{1,0:T(8,128)(2,1)S(1)}, bf16[512,512]{1,0:T(8,128)(2,1)S(1)}, u32[]{:S(2)}, u32[]{:S(2)}) collective-permute-start(bf16[512,512]{1,0:T(8,128)(2,1)S(1)} %collective-permute-done.11.refs_0_.refs_1_), channel_id=1, source_target_pairs={{0,16},{2,18},{4,20},{6,22},{8,24},{10,26},{12,28},{14,30},{16,32}... | collective-permute-start | bytes 1572872 | tf_op jit(solution)/shard_map/ppermute | solution.py:35
  105.8 7.0 %collective-permute-start.24 = (bf16[256,512]{1,0:T(8,128)(2,1)S(1)}, bf16[256,512]{1,0:T(8,128)(2,1)S(1)}, u32[]{:S(2)}, u32[]{:S(2)}) collective-permute-start(bf16[256,512]{1,0:T(8,128)(2,1)S(1)} %get-tuple-element.306), channel_id=1, source_target_pairs={{0,2},{1,7},{2,4},{3,1},{4,6},{5,3},{6,0},{7,5},{8,10},{9,15},{10,... | collective-permute-start | bytes 786440 | tf_op jit(solution)/shard_map/ppermute | solution.py:35
  107.5 5.2 %collective-permute-start.25 = (bf16[128,512]{1,0:T(8,128)(2,1)S(1)}, bf16[128,512]{1,0:T(8,128)(2,1)S(1)}, u32[]{:S(2)}, u32[]{:S(2)}) collective-permute-start(bf16[128,512]{1,0:T(8,128)(2,1)S(1)} %get-tuple-element.307), channel_id=1, source_target_pairs={{0,1},{1,0},{2,3},{3,2},{4,5},{5,4},{6,7},{7,6},{8,9},{9,8},{10,11... | collective-permute-start | bytes 393224 | tf_op jit(solution)/shard_map/ppermute | solution.py:35
  126.1 14.3 %collective-permute-start.29 = (f32[512,512]{1,0:T(8,128)S(1)}, f32[512,512]{1,0:T(8,128)S(1)}, u32[]{:S(2)}, u32[]{:S(2)}) collective-permute-start(f32[512,512]{1,0:T(8,128)S(1)} %shard_map.66.s4), channel_id=1, source_target_pairs={{0,112},{2,114},{4,116},{6,118},{8,120},{10,122},{12,124},{14,126}... | collective-permute-start | bytes 3145736 | tf_op jit(solution)/shard_map/ppermute | solution.py:35
  130.7 13.7 %collective-permute-start.28 = (f32[2048,128]{1,0:T(8,128)S(1)}, f32[2048,128]{1,0:T(8,128)S(1)}, u32[]{:S(2)}, u32[]{:S(2)}) collective-permute-start(f32[2048,128]{1,0:T(8,128)S(1)} %get-tuple-element.350), channel_id=1, source_target_pairs={{0,1},{1,0},{2,3},{3,2},{4,5},{5,4},{6,7},{7,6},{8,9},{9,8},{10,11... | collective-permute-start | bytes 3145736 | tf_op jit(solution)/shard_map/ppermute | solution.py:35
  130.8 13.6 %collective-permute-start.27 = (f32[2048,128]{1,0:T(8,128)S(1)}, f32[2048,128]{1,0:T(8,128)S(1)}, u32[]{:S(2)}, u32[]{:S(2)}) collective-permute-start(f32[2048,128]{1,0:T(8,128)S(1)} %get-tuple-element.349), channel_id=1, source_target_pairs={{0,1},{1,0},{2,3},{3,2},{4,5},{5,4},{6,7},{7,6},{8,9},{9,8},{10,11... | collective-permute-start | bytes 3145736 | tf_op jit(solution)/shard_map/ppermute | solution.py:35
  131.3 9.2 %collective-permute-start.30 = (f32[256,512]{1,0:T(8,128)S(1)}, f32[256,512]{1,0:T(8,128)S(1)}, u32[]{:S(2)}, u32[]{:S(2)}) collective-permute-start(f32[256,512]{1,0:T(8,128)S(1)} %get-tuple-element.351), channel_id=1, source_target_pairs={{1,0},{3,2},{5,4},{7,6},{9,8},{11,10},{13,12},{15,14},{17,16},{19,... | collective-permute-start | bytes 1572872 | tf_op jit(solution)/shard_map/ppermute | solution.py:35
  133.3 7.1 %collective-permute-start.31 = (f32[256,256]{1,0:T(8,128)S(1)}, f32[256,256]{1,0:T(8,128)S(1)}, u32[]{:S(2)}, u32[]{:S(2)}) collective-permute-start(f32[256,256]{1,0:T(8,128)S(1)} %get-tuple-element.322), channel_id=1, source_target_pairs={{1,129},{129,1},{3,131},{131,3},{5,133},{133,5},{7,135},{135,7},{9... | collective-permute-start | bytes 786440 | tf_op jit(solution)/shard_map/ppermute | solution.py:35
  141.1 5.0 %collective-permute-start.32 = (f32[256,256]{1,0:T(8,128)S(1)}, f32[256,256]{1,0:T(8,128)S(1)}, u32[]{:S(2)}, u32[]{:S(2)}) collective-permute-start(f32[256,256]{1,0:T(8,128)S(1)} %get-tuple-element.358), channel_id=1, source_target_pairs={{0,128},{128,0},{2,130},{130,2},{4,132},{132,4},{6,134},{134,6},{8... | collective-permute-start | bytes 786440 | tf_op jit(solution)/shard_map/ppermute | solution.py:35
  141.8 7.7 %collective-permute-start.33 = (f32[256,256]{1,0:T(8,128)S(1)}, f32[256,256]{1,0:T(8,128)S(1)}, u32[]{:S(2)}, u32[]{:S(2)}) collective-permute-start(f32[256,256]{1,0:T(8,128)S(1)} %get-tuple-element.359), channel_id=1, source_target_pairs={{0,129},{128,1},{2,131},{130,3},{4,133},{132,5},{6,135},{134,7},{8... | collective-permute-start | bytes 786440 | tf_op jit(solution)/shard_map/ppermute | solution.py:35
  143.1 6.4 %collective-permute-start.34 = (f32[256,256]{1,0:T(8,128)S(1)}, f32[256,256]{1,0:T(8,128)S(1)}, u32[]{:S(2)}, u32[]{:S(2)}) collective-permute-start(f32[256,256]{1,0:T(8,128)S(1)} %get-tuple-element.354), channel_id=1, source_target_pairs={{0,1},{2,3},{4,5},{6,7},{8,9},{10,11},{12,13},{14,15},{16,17},{18,... | collective-permute-start | bytes 786440 | tf_op jit(solution)/shard_map/ppermute | solution.py:35

commit v4 on v3

--- a/solution.py
+++ b/solution.py
@@ -368,10 +368,10 @@
     g2 = weight(1)
     s2 = add(r1, g2)
     r2 = send(along_z, s2)
-    stage(6)
     g3 = weight(2)
     s3 = add(r2, g3)
     r3 = send(along_z, s3)
+    stage(6)
     near = (w0, w1, w2, w3, w4)
     sums = attn((1, 2), near)
     g4 = weight(3)

time: 151 us -> 157 us (1.040)
  starting transfers between devices: 48.1 us -> 54.6 us
    ppermute x35, starting transfers between devices: 48.1 us -> 54.6 us  [permute(): return lax.ppermute(value, axes if len(axes) > 1 else axes[0], pairs)]
  transfers between devices with their start and end apart: 35 -> 35, of which waited for: 17 -> 21; matrix products, arithmetic and copies ran while one was open for 0% -> 0% of each run, Pallas kernels for 14% -> 13%
where the time goes in v4:
time: 157 us; the launch traced here: 156 us
  waiting for transfers between devices  73.8 us (47%)
  starting transfers between devices  54.6 us (35%)
  Pallas kernels  25.7 us (16%)
    ppermute x35, waiting for transfers between devices, permute(): return lax.ppermute(value, axes if len(axes) > 1 else axes[0], pairs)  73.8 us
    ppermute x35, starting transfers between devices, permute(): return lax.ppermute(value, axes if len(axes) > 1 else axes[0], pairs)  54.6 us
    pallas_call x22, Pallas kernels, call(): pl.pallas_call(kernel, out_shape=out_shape, in_specs=[pl.BlockSpec(memory...  25.7 us
  transfers between devices with their start and end apart: 35, of which 21 were waited for; matrix products, arithmetic and copies ran while one was open for 0% of the time, Pallas kernels for 13%

profile of v4, /device:TPU:1, one launch (start us, length us, event | category | flops | bytes accessed | tf_op | source)
XLA Modules:
  0.0 156.3 jit_solution(13668207569120077259)
XLA Ops:
  0.6 3.3 %collective-permute-start.1 = (bf16[128,4096]{1,0:T(8,128)(2,1)}, bf16[128,4096]{1,0:T(8,128)(2,1)S(1)}, u32[]{:S(2)}, u32[]{:S(2)}) collective-permute-start(bf16[128,4096]{1,0:T(8,128)(2,1)} %refs_0_.3), channel_id=1, source_target_pairs={{0,1},{1,0},{2,3},{3,2},{4,5},{5,4},{6,7},{7,6},{8,9},{9,8},{10,11... | collective-permute-start | bytes 3145736 | tf_op jit(solution)/shard_map/ppermute | solution.py:35
  4.0 2.4 %collective-permute-done.1.refs_1_ = bf16[128,4096]{1,0:T(8,128)(2,1)S(1)} collective-permute-done((bf16[128,4096]{1,0:T(8,128)(2,1)}, bf16[128,4096]{1,0:T(8,128)(2,1)S(1)}, u32[]{:S(2)}, u32[]{:S(2)}) %collective-permute-start.1) | collective-permute-done | bytes 1048608 | tf_op jit(solution)/shard_map/ppermute | solution.py:35
  6.5 1.2 copy-done
  7.7 0.6 shard_map.50
  8.3 0.9 collective-permute-done.away
  9.8 1.0 collective-permute-start.2
  10.8 0.7 collective-permute-start.5
  11.9 0.6 shard_map.52.refs_3_
  12.5 5.2 %collective-permute-start.3 = (bf16[512,512]{1,0:T(8,128)(2,1)S(1)}, bf16[512,512]{1,0:T(8,128)(2,1)S(1)}, u32[]{:S(2)}, u32[]{:S(2)}) collective-permute-start(bf16[512,512]{1,0:T(8,128)(2,1)S(1)} %shard_map.52.refs_3_), channel_id=1, source_target_pairs={{0,16},{1,113},{2,18},{3,115},{4,20},{5,117},{6,22},{7,119},{8,24}... | collective-permute-start | bytes 1572872 | tf_op jit(solution)/shard_map/ppermute | solution.py:35
  17.7 3.3 %collective-permute-start.6 = (bf16[272,512]{1,0:T(8,128)(2,1)S(1)}, bf16[272,512]{1,0:T(8,128)(2,1)S(1)}, u32[]{:S(2)}, u32[]{:S(2)}) collective-permute-start(bf16[272,512]{1,0:T(8,128)(2,1)S(1)} %get-tuple-element.197), channel_id=1, source_target_pairs={{0,9},{1,8},{2,11},{3,10},{4,13},{5,12},{6,15},{7,14},{8,1},{9,0},... | collective-permute-start | bytes 835592 | tf_op jit(solution)/shard_map/ppermute | solution.py:35
  21.1 7.0 %collective-permute-done.6.refs_3_.refs_1_.refs_8_ = bf16[272,512]{1,0:T(8,128)(2,1)S(1)} collective-permute-done((bf16[272,512]{1,0:T(8,128)(2,1)S(1)}, bf16[272,512]{1,0:T(8,128)(2,1)S(1)}, u32[]{:S(2)}, u32[]{:S(2)}) %collective-permute-start.6) | collective-permute-done | bytes 278560 | tf_op jit(solution)/shard_map/ppermute | solution.py:35
  28.1 0.7 shard_map.53
  28.8 1.2 collective-permute-start.8
  30.0 2.3 %collective-permute-start.9 = (bf16[528,512]{1,0:T(8,128)(2,1)S(1)}, bf16[528,512]{1,0:T(8,128)(2,1)S(1)}, u32[]{:S(2)}, u32[]{:S(2)}) collective-permute-start(bf16[528,512]{1,0:T(8,128)(2,1)S(1)} %get-tuple-element.209), channel_id=1, source_target_pairs={{0,9},{1,8},{2,11},{3,10},{4,13},{5,12},{6,15},{7,14},{8,1},{9,0},... | collective-permute-start | bytes 1622024 | tf_op jit(solution)/shard_map/ppermute | solution.py:35
  32.3 1.2 shard_map.54.turned
  33.6 0.8 collective-permute-start.7
  34.8 1.2 collective-permute-done.10.refs_4_.refs_7_.refs_13_
  36.0 6.0 %collective-permute-done.7.refs_1_.refs_2_ = bf16[512,512]{1,0:T(8,128)(2,1)S(1)} collective-permute-done((bf16[512,512]{1,0:T(8,128)(2,1)S(1)}, bf16[512,512]{1,0:T(8,128)(2,1)S(1)}, u32[]{:S(2)}, u32[]{:S(2)}) %collective-permute-start.7) | collective-permute-done | bytes 524320 | tf_op jit(solution)/shard_map/ppermute | solution.py:35
  42.0 3.6 %collective-permute-done.9.refs_3_.refs_5_.refs_1_.refs_11_ = bf16[528,512]{1,0:T(8,128)(2,1)S(1)} collective-permute-done((bf16[528,512]{1,0:T(8,128)(2,1)S(1)}, bf16[528,512]{1,0:T(8,128)(2,1)S(1)}, u32[]{:S(2)}, u32[]{:S(2)}) %collective-permute-start.9) | collective-permute-done | bytes 540704 | tf_op jit(solution)/shard_map/ppermute | solution.py:35
  45.6 0.7 shard_map.55
  46.3 2.1 %collective-permute-start.12 = (bf16[1280,512]{1,0:T(8,128)(2,1)S(1)}, bf16[1280,512]{1,0:T(8,128)(2,1)S(1)}, u32[]{:S(2)}, u32[]{:S(2)}) collective-permute-start(bf16[1280,512]{1,0:T(8,128)(2,1)S(1)} %get-tuple-element.220), channel_id=1, source_target_pairs={{0,2},{1,7},{2,4},{3,1},{4,6},{5,3},{6,0},{7,5},{8,10},{9,15},{10,... | collective-permute-start | bytes 3932168 | tf_op jit(solution)/shard_map/ppermute | solution.py:35
  48.4 2.0 %collective-permute-start.13 = (bf16[528,512]{1,0:T(8,128)(2,1)S(1)}, bf16[528,512]{1,0:T(8,128)(2,1)S(1)}, u32[]{:S(2)}, u32[]{:S(2)}) collective-permute-start(bf16[528,512]{1,0:T(8,128)(2,1)S(1)} %get-tuple-element.222), channel_id=1, source_target_pairs={{0,9},{1,8},{2,11},{3,10},{4,13},{5,12},{6,15},{7,14},{8,1},{9,0},... | collective-permute-start | bytes 1622024 | tf_op jit(solution)/shard_map/ppermute | solution.py:35
  50.4 0.7 collective-permute-start.11
  51.1 1.7 %collective-permute-done.14.refs_4_.refs_8_.refs_7_.refs_10_.refs_14_ = bf16[384,512]{1,0:T(8,128)(2,1)S(1)} collective-permute-done((bf16[384,512]{1,0:T(8,128)(2,1)S(1)}, bf16[384,512]{1,0:T(8,128)(2,1)S(1)}, u32[]{:S(2)}, u32[]{:S(2)}) %collective-permute-start.14) | collective-permute-done | bytes 393248 | tf_op jit(solution)/shard_map/ppermute | solution.py:35
  52.9 5.9 %collective-permute-done.11.refs_0_.refs_1_ = bf16[512,512]{1,0:T(8,128)(2,1)S(1)} collective-permute-done((bf16[512,512]{1,0:T(8,128)(2,1)S(1)}, bf16[512,512]{1,0:T(8,128)(2,1)S(1)}, u32[]{:S(2)}, u32[]{:S(2)}) %collective-permute-start.11) | collective-permute-done | bytes 524320 | tf_op jit(solution)/shard_map/ppermute | solution.py:35
  58.7 4.2 %collective-permute-done.13.refs_3_.refs_5_.refs_1_.refs_8_ = bf16[528,512]{1,0:T(8,128)(2,1)S(1)} collective-permute-done((bf16[528,512]{1,0:T(8,128)(2,1)S(1)}, bf16[528,512]{1,0:T(8,128)(2,1)S(1)}, u32[]{:S(2)}, u32[]{:S(2)}) %collective-permute-start.13) | collective-permute-done | bytes 540704 | tf_op jit(solution)/shard_map/ppermute | solution.py:35
  63.1 0.7 shard_map.56
  63.9 3.2 %collective-permute-start.16 = (bf16[1280,512]{1,0:T(8,128)(2,1)S(1)}, bf16[1280,512]{1,0:T(8,128)(2,1)S(1)}, u32[]{:S(2)}, u32[]{:S(2)}) collective-permute-start(bf16[1280,512]{1,0:T(8,128)(2,1)S(1)} %get-tuple-element.233), channel_id=1, source_target_pairs={{0,2},{1,7},{2,4},{3,1},{4,6},{5,3},{6,0},{7,5},{8,10},{9,15},{10,... | collective-permute-start | bytes 3932168 | tf_op jit(solution)/shard_map/ppermute | solution.py:35
  67.1 1.8 %shard_map.57 = f32[512,512]{1,0:T(8,128)S(1)} custom-call(s32[5]{0:T(128)S(1)} %stack.23.pos._, bf16[512,2048]{1,0:T(8,128)(2,1)S(1)} %shard_map.54.turned, bf16[256,512]{1,0:T(8,128)(2,1)S(1)} %get-tuple-element.330.refs_0_.refs_7_, bf16[272,512]{1,0:T(8,128)(2,1)S(1)} %collective-permute-done.6.refs_3_.refs_1_.refs_8_, ...), custom_call_target="tpu_custom_call" | custom-call | bytes 65536 | tf_op jit(solution)/shard_map/pallas_call | solution.py:79
  69.0 2.9 %collective-permute-start.18 = (bf16[528,512]{1,0:T(8,128)(2,1)S(1)}, bf16[528,512]{1,0:T(8,128)(2,1)S(1)}, u32[]{:S(2)}, u32[]{:S(2)}) collective-permute-start(bf16[528,512]{1,0:T(8,128)(2,1)S(1)} %get-tuple-element.237), channel_id=1, source_target_pairs={{0,9},{1,8},{2,11},{3,10},{4,13},{5,12},{6,15},{7,14},{8,1},{9,0},... | collective-permute-start | bytes 1622024 | tf_op jit(solution)/shard_map/ppermute | solution.py:35
  71.9 1.7 %collective-permute-done.17.refs_2_.refs_8_.refs_7_.refs_11_ = bf16[384,512]{1,0:T(8,128)(2,1)S(1)} collective-permute-done((bf16[384,512]{1,0:T(8,128)(2,1)S(1)}, bf16[384,512]{1,0:T(8,128)(2,1)S(1)}, u32[]{:S(2)}, u32[]{:S(2)}) %collective-permute-start.17) | collective-permute-done | bytes 393248 | tf_op jit(solution)/shard_map/ppermute | solution.py:35
  73.6 11.0 %collective-permute-done.18.refs_1_.refs_5_.refs_13_.refs_16_ = bf16[528,512]{1,0:T(8,128)(2,1)S(1)} collective-permute-done((bf16[528,512]{1,0:T(8,128)(2,1)S(1)}, bf16[528,512]{1,0:T(8,128)(2,1)S(1)}, u32[]{:S(2)}, u32[]{:S(2)}) %collective-permute-start.18) | collective-permute-done | bytes 540704 | tf_op jit(solution)/shard_map/ppermute | solution.py:35
  84.6 0.6 shard_map.58
  85.3 1.8 %shard_map.59.b = f32[512,512]{1,0:T(8,128)S(1)} custom-call(s32[5]{0:T(128)S(1)} %stack.23.pos._, bf16[512,2048]{1,0:T(8,128)(2,1)S(1)} %shard_map.54.turned, bf16[256,512]{1,0:T(8,128)(2,1)S(1)} %get-tuple-element.291.refs_0_.refs_4_, bf16[528,512]{1,0:T(8,128)(2,1)S(1)} %collective-permute-done.9.refs_3_.refs_5_.refs_1_.refs_11_, ...), custom_call_target="tpu_custom_call" | custom-call | bytes 65536 | tf_op jit(solution)/shard_map/pallas_call | solution.py:79
  87.1 0.6 shard_map.60
  87.7 1.1 collective-permute-start.23
  88.8 2.7 %collective-permute-start.19 = (bf16[768,512]{1,0:T(8,128)(2,1)S(1)}, bf16[768,512]{1,0:T(8,128)(2,1)S(1)}, u32[]{:S(2)}, u32[]{:S(2)}) collective-permute-start(bf16[768,512]{1,0:T(8,128)(2,1)S(1)} %get-tuple-element.253), channel_id=1, source_target_pairs={{0,2},{1,7},{2,4},{3,1},{4,6},{5,3},{6,0},{7,5},{8,10},{9,15},{10,... | collective-permute-start | bytes 2359304 | tf_op jit(solution)/shard_map/ppermute | solution.py:35
  91.5 1.7 %collective-permute-done.20.refs_8_.refs_2_.refs_15_.refs_7_.refs_21_ = bf16[384,512]{1,0:T(8,128)(2,1)S(1)} collective-permute-done((bf16[384,512]{1,0:T(8,128)(2,1)S(1)}, bf16[384,512]{1,0:T(8,128)(2,1)S(1)}, u32[]{:S(2)}, u32[]{:S(2)}) %collective-permute-start.20) | collective-permute-done | bytes 393248 | tf_op jit(solution)/shard_map/ppermute | solution.py:35
  93.2 7.2 %collective-permute-done.19.refs_6_.refs_0_.refs_14_.refs_3_.refs_4_.refs_18_ = bf16[768,512]{1,0:T(8,128)(2,1)S(1)} collective-permute-done((bf16[768,512]{1,0:T(8,128)(2,1)S(1)}, bf16[768,512]{1,0:T(8,128)(2,1)S(1)}, u32[]{:S(2)}, u32[]{:S(2)}) %collective-permute-start.19) | collective-permute-done | bytes 786464 | tf_op jit(solution)/shard_map/ppermute | solution.py:35
  100.4 1.8 %shard_map.61.b = f32[512,512]{1,0:T(8,128)S(1)} custom-call(s32[5]{0:T(128)S(1)} %stack.23.pos._, bf16[512,2048]{1,0:T(8,128)(2,1)S(1)} %shard_map.54.turned, bf16[256,512]{1,0:T(8,128)(2,1)S(1)} %get-tuple-element.299.refs_0_.refs_12_, bf16[528,512]{1,0:T(8,128)(2,1)S(1)} %collective-permute-done.13.refs_3_.refs_5_.refs_1_.refs_8_, ...), custom_call_target="tpu_custom_call" | custom-call | bytes 65536 | tf_op jit(solution)/shard_map/pallas_call | solution.py:79
  102.7 0.6 shard_map.62
  103.5 5.2 %collective-permute-start.21 = (bf16[272,512]{1,0:T(8,128)(2,1)S(1)}, bf16[272,512]{1,0:T(8,128)(2,1)S(1)}, u32[]{:S(2)}, u32[]{:S(2)}) collective-permute-start(bf16[272,512]{1,0:T(8,128)(2,1)S(1)} %get-tuple-element.256), channel_id=1, source_target_pairs={{0,9},{1,8},{2,11},{3,10},{4,13},{5,12},{6,15},{7,14},{8,1},{9,0},... | collective-permute-start | bytes 835592 | tf_op jit(solution)/shard_map/ppermute | solution.py:35
  108.6 0.7 collective-permute-start.15
  109.3 6.8 %collective-permute-done.21.refs_1_.refs_5_.refs_19_ = bf16[272,512]{1,0:T(8,128)(2,1)S(1)} collective-permute-done((bf16[272,512]{1,0:T(8,128)(2,1)S(1)}, bf16[272,512]{1,0:T(8,128)(2,1)S(1)}, u32[]{:S(2)}, u32[]{:S(2)}) %collective-permute-start.21) | collective-permute-done | bytes 278560 | tf_op jit(solution)/shard_map/ppermute | solution.py:35
  116.7 0.6 collective-permute-start.24
  117.3 0.7 collective-permute-start.25
  118.0 2.9 %shard_map.64 = (f32[2048,256]{1,0:T(8,128)S(1)}, f32[2048,128]{1,0:T(8,128)S(1)}, f32[2048,128]{1,0:T(8,128)S(1)}) custom-call(s32[5]{0:T(128)S(1)} %stack.23.pos._, bf16[512,512]{1,0:T(8,128)(2,1)S(1)} %collective-permute-done.11.refs_0_.refs_1_, bf16[512,512]{1,0:T(8,128)(2,1)S(1)} %collective-permute-done.7.refs_1_.refs_2_, ...), custom_call_target="tpu_custom_call" | custom-call | bytes 65536 | tf_op jit(solution)/shard_map/pallas_call | solution.py:79
  120.9 1.4 collective-permute-done.24.refs_6_.refs_20_
  122.3 1.8 %shard_map.65.b = f32[512,512]{1,0:T(8,128)S(1)} custom-call(s32[5]{0:T(128)S(1)} %stack.23.pos._, bf16[512,2048]{1,0:T(8,128)(2,1)S(1)} %shard_map.54.turned, bf16[256,512]{1,0:T(8,128)(2,1)S(1)} %get-tuple-element.338.refs_0_.refs_15_, bf16[528,512]{1,0:T(8,128)(2,1)S(1)} %collective-permute-done.18.refs_1_.refs_5_.refs_13_.refs_16_, ...), custom_call_target="tpu_custom_call" | custom-call | bytes 65536 | tf_op jit(solution)/shard_map/pallas_call | solution.py:79
  124.2 0.6 shard_map.66.s4
  124.8 0.9 collective-permute-start.29
  125.8 0.6 shard_map.67
  126.4 3.0 %shard_map.68 = (f32[2048,256]{1,0:T(8,128)S(1)}, f32[2048,128]{1,0:T(8,128)S(1)}, f32[2048,128]{1,0:T(8,128)S(1)}) custom-call(s32[5]{0:T(128)S(1)} %stack.23.pos._, bf16[512,512]{1,0:T(8,128)(2,1)S(1)} %collective-permute-done.15.refs_0_, bf16[512,512]{1,0:T(8,128)(2,1)S(1)} %collective-permute-done.11.refs_0_.refs_1_, ...), custom_call_target="tpu_custom_call" | custom-call | bytes 65536 | tf_op jit(solution)/shard_map/pallas_call | solution.py:79
  129.4 4.4 %collective-permute-start.28 = (f32[2048,128]{1,0:T(8,128)S(1)}, f32[2048,128]{1,0:T(8,128)S(1)}, u32[]{:S(2)}, u32[]{:S(2)}) collective-permute-start(f32[2048,128]{1,0:T(8,128)S(1)} %get-tuple-element.350), channel_id=1, source_target_pairs={{0,1},{1,0},{2,3},{3,2},{4,5},{5,4},{6,7},{7,6},{8,9},{9,8},{10,11... | collective-permute-start | bytes 3145736 | tf_op jit(solution)/shard_map/ppermute | solution.py:35
  133.9 2.3 %collective-permute-start.30 = (f32[256,512]{1,0:T(8,128)S(1)}, f32[256,512]{1,0:T(8,128)S(1)}, u32[]{:S(2)}, u32[]{:S(2)}) collective-permute-start(f32[256,512]{1,0:T(8,128)S(1)} %get-tuple-element.351), channel_id=1, source_target_pairs={{1,0},{3,2},{5,4},{7,6},{9,8},{11,10},{13,12},{15,14},{17,16},{19,... | collective-permute-start | bytes 1572872 | tf_op jit(solution)/shard_map/ppermute | solution.py:35
  136.3 3.1 %collective-permute-start.31 = (f32[256,256]{1,0:T(8,128)S(1)}, f32[256,256]{1,0:T(8,128)S(1)}, u32[]{:S(2)}, u32[]{:S(2)}) collective-permute-start(f32[256,256]{1,0:T(8,128)S(1)} %get-tuple-element.322), channel_id=1, source_target_pairs={{1,129},{129,1},{3,131},{131,3},{5,133},{133,5},{7,135},{135,7},{9... | collective-permute-start | bytes 786440 | tf_op jit(solution)/shard_map/ppermute | solution.py:35
  139.4 4.2 %collective-permute-done.31.from_y = f32[256,256]{1,0:T(8,128)S(1)} collective-permute-done((f32[256,256]{1,0:T(8,128)S(1)}, f32[256,256]{1,0:T(8,128)S(1)}, u32[]{:S(2)}, u32[]{:S(2)}) %collective-permute-start.31) | collective-permute-done | bytes 262176 | tf_op jit(solution)/shard_map/ppermute | solution.py:35
  143.5 0.6 shard_map.69
  144.2 0.7 collective-permute-start.32
  144.8 1.3 collective-permute-start.33
  146.1 1.3 collective-permute-start.34
  147.5 1.7 %shard_map.70 = bf16[2048,256]{1,0:T(8,128)(2,1)} custom-call(s32[5]{0:T(128)S(1)} %stack.23.pos._, f32[2048,256]{1,0:T(8,128)S(1)} %get-tuple-element.355.keep, f32[2048,128]{1,0:T(8,128)S(1)} %collective-permute-done.27.first, f32[2048,128]{1,0:T(8,128)S(1)} %collective-permute-done.28.second), custom_call_target="tpu_custom_call" | custom-call | bytes 65536 | tf_op jit(solution)/shard_map/pallas_call | solution.py:79
  149.2 5.7 %collective-permute-done.33.cross = f32[256,256]{1,0:T(8,128)S(1)} collective-permute-done((f32[256,256]{1,0:T(8,128)S(1)}, f32[256,256]{1,0:T(8,128)S(1)}, u32[]{:S(2)}, u32[]{:S(2)}) %collective-permute-start.33) | collective-permute-done | bytes 262176 | tf_op jit(solution)/shard_map/ppermute | solution.py:35
  154.9 1.4 shard_map.71
  (37 shorter events, 3.2 us)
Async XLA Ops:
  0.6 5.8 %collective-permute-start.1 = (bf16[128,4096]{1,0:T(8,128)(2,1)}, bf16[128,4096]{1,0:T(8,128)(2,1)S(1)}, u32[]{:S(2)}, u32[]{:S(2)}) collective-permute-start(bf16[128,4096]{1,0:T(8,128)(2,1)} %refs_0_.3), channel_id=1, source_target_pairs={{0,1},{1,0},{2,3},{3,2},{4,5},{5,4},{6,7},{7,6},{8,9},{9,8},{10,11... | collective-permute-start | bytes 3145736 | tf_op jit(solution)/shard_map/ppermute | solution.py:35
  4.0 5.3 %collective-permute-start = (bf16[256,256]{1,0:T(8,128)(2,1)}, bf16[256,256]{1,0:T(8,128)(2,1)S(1)}, u32[]{:S(2)}, u32[]{:S(2)}) collective-permute-start(bf16[256,256]{1,0:T(8,128)(2,1)} %own), channel_id=1, source_target_pairs={{0,128},{128,0},{1,129},{129,1},{2,130},{130,2},{3,131},{131,3},{4... | collective-permute-start | bytes 393224 | tf_op jit(solution)/shard_map/ppermute | solution.py:35
  6.5 1.2 copy-start
  7.7 1.6 copy-start.3
  8.3 9.4 %copy-start.2 = (bf16[2048,256]{1,0:T(8,128)(2,1)S(1)}, bf16[2048,256]{1,0:T(8,128)(2,1)}, u32[]{:S(2)}) copy-start(bf16[2048,256]{1,0:T(8,128)(2,1)} %own.1) | copy-start | bytes 3145732
  9.8 2.1 %collective-permute-start.2 = (bf16[512,256]{1,0:T(8,128)(2,1)S(1)}, bf16[512,256]{1,0:T(8,128)(2,1)S(1)}, u32[]{:S(2)}, u32[]{:S(2)}) collective-permute-start(bf16[512,256]{1,0:T(8,128)(2,1)S(1)} %shard_map.51.mine), channel_id=1, source_target_pairs={{0,1},{1,0},{2,3},{3,2},{4,5},{5,4},{6,7},{7,6},{8,9},{9,8},{10,11... | collective-permute-start | bytes 786440 | tf_op jit(solution)/shard_map/ppermute | solution.py:35
  10.8 17.3 %collective-permute-start.5 = (bf16[512,512]{1,0:T(8,128)(2,1)S(1)}, bf16[512,512]{1,0:T(8,128)(2,1)S(1)}, u32[]{:S(2)}, u32[]{:S(2)}) collective-permute-start(bf16[512,512]{1,0:T(8,128)(2,1)S(1)} %get-tuple-element.195), channel_id=1, source_target_pairs={{0,2},{1,7},{2,4},{3,1},{4,6},{5,3},{6,0},{7,5},{8,10},{9,15},{10,... | collective-permute-start | bytes 1572872 | tf_op jit(solution)/shard_map/ppermute | solution.py:35
  12.5 15.6 %collective-permute-start.3 = (bf16[512,512]{1,0:T(8,128)(2,1)S(1)}, bf16[512,512]{1,0:T(8,128)(2,1)S(1)}, u32[]{:S(2)}, u32[]{:S(2)}) collective-permute-start(bf16[512,512]{1,0:T(8,128)(2,1)S(1)} %shard_map.52.refs_3_), channel_id=1, source_target_pairs={{0,16},{1,113},{2,18},{3,115},{4,20},{5,117},{6,22},{7,119},{8,24}... | collective-permute-start | bytes 1572872 | tf_op jit(solution)/shard_map/ppermute | solution.py:35
  17.7 14.6 %collective-permute-start.4 = (bf16[2048,256]{1,0:T(8,128)(2,1)S(1)}, bf16[2048,256]{1,0:T(8,128)(2,1)S(1)}, u32[]{:S(2)}, u32[]{:S(2)}) collective-permute-start(bf16[2048,256]{1,0:T(8,128)(2,1)S(1)} %copy-done.2), channel_id=1, source_target_pairs={{0,1},{1,0},{2,3},{3,2},{4,5},{5,4},{6,7},{7,6},{8,9},{9,8},{10,11... | collective-permute-start | bytes 3145736 | tf_op jit(solution)/shard_map/ppermute | solution.py:35
  17.7 10.3 %collective-permute-start.6 = (bf16[272,512]{1,0:T(8,128)(2,1)S(1)}, bf16[272,512]{1,0:T(8,128)(2,1)S(1)}, u32[]{:S(2)}, u32[]{:S(2)}) collective-permute-start(bf16[272,512]{1,0:T(8,128)(2,1)S(1)} %get-tuple-element.197), channel_id=1, source_target_pairs={{0,9},{1,8},{2,11},{3,10},{4,13},{5,12},{6,15},{7,14},{8,1},{9,0},... | collective-permute-start | bytes 835592 | tf_op jit(solution)/shard_map/ppermute | solution.py:35
  28.8 16.8 %collective-permute-start.8 = (bf16[1024,512]{1,0:T(8,128)(2,1)S(1)}, bf16[1024,512]{1,0:T(8,128)(2,1)S(1)}, u32[]{:S(2)}, u32[]{:S(2)}) collective-permute-start(bf16[1024,512]{1,0:T(8,128)(2,1)S(1)} %get-tuple-element.207), channel_id=1, source_target_pairs={{0,2},{1,7},{2,4},{3,1},{4,6},{5,3},{6,0},{7,5},{8,10},{9,15},{10,... | collective-permute-start | bytes 3145736 | tf_op jit(solution)/shard_map/ppermute | solution.py:35
  30.0 15.5 %copy-start.1 = (bf16[128,4096]{1,0:T(8,128)(2,1)S(1)}, bf16[128,4096]{1,0:T(8,128)(2,1)}, u32[]{:S(2)}) copy-start(bf16[128,4096]{1,0:T(8,128)(2,1)} %refs_0_.3) | copy-start | bytes 3145732
  30.0 15.5 %collective-permute-start.9 = (bf16[528,512]{1,0:T(8,128)(2,1)S(1)}, bf16[528,512]{1,0:T(8,128)(2,1)S(1)}, u32[]{:S(2)}, u32[]{:S(2)}) collective-permute-start(bf16[528,512]{1,0:T(8,128)(2,1)S(1)} %get-tuple-element.209), channel_id=1, source_target_pairs={{0,9},{1,8},{2,11},{3,10},{4,13},{5,12},{6,15},{7,14},{8,1},{9,0},... | collective-permute-start | bytes 1622024 | tf_op jit(solution)/shard_map/ppermute | solution.py:35
  33.6 8.4 %collective-permute-start.7 = (bf16[512,512]{1,0:T(8,128)(2,1)S(1)}, bf16[512,512]{1,0:T(8,128)(2,1)S(1)}, u32[]{:S(2)}, u32[]{:S(2)}) collective-permute-start(bf16[512,512]{1,0:T(8,128)(2,1)S(1)} %collective-permute-done.3.refs_3_.refs_2_), channel_id=1, source_target_pairs={{0,16},{1,113},{2,18},{3,115},{4,20},{5,117},{6,22},{7,119},{8,24}... | collective-permute-start | bytes 1572872 | tf_op jit(solution)/shard_map/ppermute | solution.py:35
  34.4 1.6 %collective-permute-start.10 = (bf16[256,512]{1,0:T(8,128)(2,1)S(1)}, bf16[256,512]{1,0:T(8,128)(2,1)S(1)}, u32[]{:S(2)}, u32[]{:S(2)}) collective-permute-start(bf16[256,512]{1,0:T(8,128)(2,1)S(1)} %get-tuple-element.211), channel_id=1, source_target_pairs={{0,1},{1,0},{2,3},{3,2},{4,5},{5,4},{6,7},{7,6},{8,9},{9,8},{10,11... | collective-permute-start | bytes 786440 | tf_op jit(solution)/shard_map/ppermute | solution.py:35
  46.3 16.8 %collective-permute-start.12 = (bf16[1280,512]{1,0:T(8,128)(2,1)S(1)}, bf16[1280,512]{1,0:T(8,128)(2,1)S(1)}, u32[]{:S(2)}, u32[]{:S(2)}) collective-permute-start(bf16[1280,512]{1,0:T(8,128)(2,1)S(1)} %get-tuple-element.220), channel_id=1, source_target_pairs={{0,2},{1,7},{2,4},{3,1},{4,6},{5,3},{6,0},{7,5},{8,10},{9,15},{10,... | collective-permute-start | bytes 3932168 | tf_op jit(solution)/shard_map/ppermute | solution.py:35
  48.4 14.5 %collective-permute-start.13 = (bf16[528,512]{1,0:T(8,128)(2,1)S(1)}, bf16[528,512]{1,0:T(8,128)(2,1)S(1)}, u32[]{:S(2)}, u32[]{:S(2)}) collective-permute-start(bf16[528,512]{1,0:T(8,128)(2,1)S(1)} %get-tuple-element.222), channel_id=1, source_target_pairs={{0,9},{1,8},{2,11},{3,10},{4,13},{5,12},{6,15},{7,14},{8,1},{9,0},... | collective-permute-start | bytes 1622024 | tf_op jit(solution)/shard_map/ppermute | solution.py:35
  50.4 8.3 %collective-permute-start.11 = (bf16[512,512]{1,0:T(8,128)(2,1)S(1)}, bf16[512,512]{1,0:T(8,128)(2,1)S(1)}, u32[]{:S(2)}, u32[]{:S(2)}) collective-permute-start(bf16[512,512]{1,0:T(8,128)(2,1)S(1)} %collective-permute-done.7.refs_1_.refs_2_), channel_id=1, source_target_pairs={{0,16},{1,113},{2,18},{3,115},{4,20},{5,117},{6,22},{7,119},{8,24}... | collective-permute-start | bytes 1572872 | tf_op jit(solution)/shard_map/ppermute | solution.py:35
  51.1 1.7 %collective-permute-start.14 = (bf16[384,512]{1,0:T(8,128)(2,1)S(1)}, bf16[384,512]{1,0:T(8,128)(2,1)S(1)}, u32[]{:S(2)}, u32[]{:S(2)}) collective-permute-start(bf16[384,512]{1,0:T(8,128)(2,1)S(1)} %get-tuple-element.224), channel_id=1, source_target_pairs={{0,1},{1,0},{2,3},{3,2},{4,5},{5,4},{6,7},{7,6},{8,9},{9,8},{10,11... | collective-permute-start | bytes 1179656 | tf_op jit(solution)/shard_map/ppermute | solution.py:35
  63.9 20.8 %collective-permute-start.16 = (bf16[1280,512]{1,0:T(8,128)(2,1)S(1)}, bf16[1280,512]{1,0:T(8,128)(2,1)S(1)}, u32[]{:S(2)}, u32[]{:S(2)}) collective-permute-start(bf16[1280,512]{1,0:T(8,128)(2,1)S(1)} %get-tuple-element.233), channel_id=1, source_target_pairs={{0,2},{1,7},{2,4},{3,1},{4,6},{5,3},{6,0},{7,5},{8,10},{9,15},{10,... | collective-permute-start | bytes 3932168 | tf_op jit(solution)/shard_map/ppermute | solution.py:35
  68.9 18.2 %collective-permute-start.22 = (f32[512,512]{1,0:T(8,128)S(1)}, f32[512,512]{1,0:T(8,128)S(1)}, u32[]{:S(2)}, u32[]{:S(2)}) collective-permute-start(f32[512,512]{1,0:T(8,128)S(1)} %shard_map.57), channel_id=1, source_target_pairs={{0,112},{1,17},{2,114},{3,19},{4,116},{5,21},{6,118},{7,23},{8,120... | collective-permute-start | bytes 3145736 | tf_op jit(solution)/shard_map/ppermute | solution.py:35
  69.0 15.7 %collective-permute-start.18 = (bf16[528,512]{1,0:T(8,128)(2,1)S(1)}, bf16[528,512]{1,0:T(8,128)(2,1)S(1)}, u32[]{:S(2)}, u32[]{:S(2)}) collective-permute-start(bf16[528,512]{1,0:T(8,128)(2,1)S(1)} %get-tuple-element.237), channel_id=1, source_target_pairs={{0,9},{1,8},{2,11},{3,10},{4,13},{5,12},{6,15},{7,14},{8,1},{9,0},... | collective-permute-start | bytes 1622024 | tf_op jit(solution)/shard_map/ppermute | solution.py:35
  71.9 1.7 %collective-permute-start.17 = (bf16[384,512]{1,0:T(8,128)(2,1)S(1)}, bf16[384,512]{1,0:T(8,128)(2,1)S(1)}, u32[]{:S(2)}, u32[]{:S(2)}) collective-permute-start(bf16[384,512]{1,0:T(8,128)(2,1)S(1)} %get-tuple-element.235), channel_id=1, source_target_pairs={{0,1},{1,0},{2,3},{3,2},{4,5},{5,4},{6,7},{7,6},{8,9},{9,8},{10,11... | collective-permute-start | bytes 1179656 | tf_op jit(solution)/shard_map/ppermute | solution.py:35
  87.7 14.9 %collective-permute-start.23 = (f32[512,512]{1,0:T(8,128)S(1)}, f32[512,512]{1,0:T(8,128)S(1)}, u32[]{:S(2)}, u32[]{:S(2)}) collective-permute-start(f32[512,512]{1,0:T(8,128)S(1)} %shard_map.60), channel_id=1, source_target_pairs={{0,112},{1,17},{2,114},{3,19},{4,116},{5,21},{6,118},{7,23},{8,120... | collective-permute-start | bytes 3145736 | tf_op jit(solution)/shard_map/ppermute | solution.py:35
  88.8 11.6 %collective-permute-start.19 = (bf16[768,512]{1,0:T(8,128)(2,1)S(1)}, bf16[768,512]{1,0:T(8,128)(2,1)S(1)}, u32[]{:S(2)}, u32[]{:S(2)}) collective-permute-start(bf16[768,512]{1,0:T(8,128)(2,1)S(1)} %get-tuple-element.253), channel_id=1, source_target_pairs={{0,2},{1,7},{2,4},{3,1},{4,6},{5,3},{6,0},{7,5},{8,10},{9,15},{10,... | collective-permute-start | bytes 2359304 | tf_op jit(solution)/shard_map/ppermute | solution.py:35
  91.5 1.7 %collective-permute-start.20 = (bf16[384,512]{1,0:T(8,128)(2,1)S(1)}, bf16[384,512]{1,0:T(8,128)(2,1)S(1)}, u32[]{:S(2)}, u32[]{:S(2)}) collective-permute-start(bf16[384,512]{1,0:T(8,128)(2,1)S(1)} %get-tuple-element.254), channel_id=1, source_target_pairs={{0,1},{1,0},{2,3},{3,2},{4,5},{5,4},{6,7},{7,6},{8,9},{9,8},{10,11... | collective-permute-start | bytes 1179656 | tf_op jit(solution)/shard_map/ppermute | solution.py:35
  103.3 20.9 %collective-permute-start.26 = (f32[512,512]{1,0:T(8,128)S(1)}, f32[512,512]{1,0:T(8,128)S(1)}, u32[]{:S(2)}, u32[]{:S(2)}) collective-permute-start(f32[512,512]{1,0:T(8,128)S(1)} %shard_map.62), channel_id=1, source_target_pairs={{0,112},{1,17},{2,114},{3,19},{4,116},{5,21},{6,118},{7,23},{8,120... | collective-permute-start | bytes 3145736 | tf_op jit(solution)/shard_map/ppermute | solution.py:35
  103.5 12.7 %collective-permute-start.21 = (bf16[272,512]{1,0:T(8,128)(2,1)S(1)}, bf16[272,512]{1,0:T(8,128)(2,1)S(1)}, u32[]{:S(2)}, u32[]{:S(2)}) collective-permute-start(bf16[272,512]{1,0:T(8,128)(2,1)S(1)} %get-tuple-element.256), channel_id=1, source_target_pairs={{0,9},{1,8},{2,11},{3,10},{4,13},{5,12},{6,15},{7,14},{8,1},{9,0},... | collective-permute-start | bytes 835592 | tf_op jit(solution)/shard_map/ppermute | solution.py:35
  108.6 17.8 %collective-permute-start.15 = (bf16[512,512]{1,0:T(8,128)(2,1)S(1)}, bf16[512,512]{1,0:T(8,128)(2,1)S(1)}, u32[]{:S(2)}, u32[]{:S(2)}) collective-permute-start(bf16[512,512]{1,0:T(8,128)(2,1)S(1)} %collective-permute-done.11.refs_0_.refs_1_), channel_id=1, source_target_pairs={{0,16},{2,18},{4,20},{6,22},{8,24},{10,26},{12,28},{14,30},{16,32}... | collective-permute-start | bytes 1572872 | tf_op jit(solution)/shard_map/ppermute | solution.py:35
  116.7 5.6 %collective-permute-start.24 = (bf16[256,512]{1,0:T(8,128)(2,1)S(1)}, bf16[256,512]{1,0:T(8,128)(2,1)S(1)}, u32[]{:S(2)}, u32[]{:S(2)}) collective-permute-start(bf16[256,512]{1,0:T(8,128)(2,1)S(1)} %get-tuple-element.306), channel_id=1, source_target_pairs={{0,2},{1,7},{2,4},{3,1},{4,6},{5,3},{6,0},{7,5},{8,10},{9,15},{10,... | collective-permute-start | bytes 786440 | tf_op jit(solution)/shard_map/ppermute | solution.py:35
  117.3 3.6 %collective-permute-start.25 = (bf16[128,512]{1,0:T(8,128)(2,1)S(1)}, bf16[128,512]{1,0:T(8,128)(2,1)S(1)}, u32[]{:S(2)}, u32[]{:S(2)}) collective-permute-start(bf16[128,512]{1,0:T(8,128)(2,1)S(1)} %get-tuple-element.307), channel_id=1, source_target_pairs={{0,1},{1,0},{2,3},{3,2},{4,5},{5,4},{6,7},{7,6},{8,9},{9,8},{10,11... | collective-permute-start | bytes 393224 | tf_op jit(solution)/shard_map/ppermute | solution.py:35
  124.8 18.7 %collective-permute-start.29 = (f32[512,512]{1,0:T(8,128)S(1)}, f32[512,512]{1,0:T(8,128)S(1)}, u32[]{:S(2)}, u32[]{:S(2)}) collective-permute-start(f32[512,512]{1,0:T(8,128)S(1)} %shard_map.66.s4), channel_id=1, source_target_pairs={{0,112},{2,114},{4,116},{6,118},{8,120},{10,122},{12,124},{14,126}... | collective-permute-start | bytes 3145736 | tf_op jit(solution)/shard_map/ppermute | solution.py:35
  129.4 18.0 %collective-permute-start.28 = (f32[2048,128]{1,0:T(8,128)S(1)}, f32[2048,128]{1,0:T(8,128)S(1)}, u32[]{:S(2)}, u32[]{:S(2)}) collective-permute-start(f32[2048,128]{1,0:T(8,128)S(1)} %get-tuple-element.350), channel_id=1, source_target_pairs={{0,1},{1,0},{2,3},{3,2},{4,5},{5,4},{6,7},{7,6},{8,9},{9,8},{10,11... | collective-permute-start | bytes 3145736 | tf_op jit(solution)/shard_map/ppermute | solution.py:35
  133.8 13.6 %collective-permute-start.27 = (f32[2048,128]{1,0:T(8,128)S(1)}, f32[2048,128]{1,0:T(8,128)S(1)}, u32[]{:S(2)}, u32[]{:S(2)}) collective-permute-start(f32[2048,128]{1,0:T(8,128)S(1)} %get-tuple-element.349), channel_id=1, source_target_pairs={{0,1},{1,0},{2,3},{3,2},{4,5},{5,4},{6,7},{7,6},{8,9},{9,8},{10,11... | collective-permute-start | bytes 3145736 | tf_op jit(solution)/shard_map/ppermute | solution.py:35
  133.9 9.6 %collective-permute-start.30 = (f32[256,512]{1,0:T(8,128)S(1)}, f32[256,512]{1,0:T(8,128)S(1)}, u32[]{:S(2)}, u32[]{:S(2)}) collective-permute-start(f32[256,512]{1,0:T(8,128)S(1)} %get-tuple-element.351), channel_id=1, source_target_pairs={{1,0},{3,2},{5,4},{7,6},{9,8},{11,10},{13,12},{15,14},{17,16},{19,... | collective-permute-start | bytes 1572872 | tf_op jit(solution)/shard_map/ppermute | solution.py:35
  136.3 7.3 %collective-permute-start.31 = (f32[256,256]{1,0:T(8,128)S(1)}, f32[256,256]{1,0:T(8,128)S(1)}, u32[]{:S(2)}, u32[]{:S(2)}) collective-permute-start(f32[256,256]{1,0:T(8,128)S(1)} %get-tuple-element.322), channel_id=1, source_target_pairs={{1,129},{129,1},{3,131},{131,3},{5,133},{133,5},{7,135},{135,7},{9... | collective-permute-start | bytes 786440 | tf_op jit(solution)/shard_map/ppermute | solution.py:35
  144.2 5.0 %collective-permute-start.32 = (f32[256,256]{1,0:T(8,128)S(1)}, f32[256,256]{1,0:T(8,128)S(1)}, u32[]{:S(2)}, u32[]{:S(2)}) collective-permute-start(f32[256,256]{1,0:T(8,128)S(1)} %get-tuple-element.358), channel_id=1, source_target_pairs={{0,128},{128,0},{2,130},{130,2},{4,132},{132,4},{6,134},{134,6},{8... | collective-permute-start | bytes 786440 | tf_op jit(solution)/shard_map/ppermute | solution.py:35
  144.8 10.1 %collective-permute-start.33 = (f32[256,256]{1,0:T(8,128)S(1)}, f32[256,256]{1,0:T(8,128)S(1)}, u32[]{:S(2)}, u32[]{:S(2)}) collective-permute-start(f32[256,256]{1,0:T(8,128)S(1)} %get-tuple-element.359), channel_id=1, source_target_pairs={{0,129},{128,1},{2,131},{130,3},{4,133},{132,5},{6,135},{134,7},{8... | collective-permute-start | bytes 786440 | tf_op jit(solution)/shard_map/ppermute | solution.py:35
  146.1 8.8 %collective-permute-start.34 = (f32[256,256]{1,0:T(8,128)S(1)}, f32[256,256]{1,0:T(8,128)S(1)}, u32[]{:S(2)}, u32[]{:S(2)}) collective-permute-start(f32[256,256]{1,0:T(8,128)S(1)} %get-tuple-element.354), channel_id=1, source_target_pairs={{0,1},{2,3},{4,5},{6,7},{8,9},{10,11},{12,13},{14,15},{16,17},{18,... | collective-permute-start | bytes 786440 | tf_op jit(solution)/shard_map/ppermute | solution.py:35
